TPU v7x, 32 devices: a whole 2x2x4 slice. The times are simulated.
32 devices in a mesh: seq: 4 (over x, core), ray: 8 (over z, y).
Axes of the slice: x: 2, y: 2, z: 4, core: 2. Of those that a mesh axis runs over, the one named last changes fastest.
Arguments:
- rays: bfloat16 [12288, 768], P(('seq', 'ray')), may hold values from -6 to 6
- latents: bfloat16 [12288, 768], P(('seq', 'ray')), may hold values from -6 to 6
- lengths: int32 [4, 3], P('seq'), may hold values from 1 to 1536, 3072 in all within a row
- scenes: int32 [12288], P(('seq', 'ray')), may hold values from 0 to 2
- ln_gain: bfloat16 [768], replicated, may hold values from 0.25 to 1.75
- ln_bias: bfloat16 [768], replicated, may hold values from -3 to 3
- w_query: bfloat16 [768, 768], replicated, may hold values from -0.21875 to 0.21875
- b_query: bfloat16 [768], replicated, may hold values from -3 to 3
- w_key: bfloat16 [768, 768], replicated, may hold values from -0.21875 to 0.21875
- w_value: bfloat16 [768, 768], replicated, may hold values from -0.21875 to 0.21875
- b_value: bfloat16 [768], replicated, may hold values from -0.3125 to 0.3125
- w_out: bfloat16 [768, 768], replicated, may hold values from -2 to 2
- b_out: bfloat16 [768], replicated, may hold values from -3 to 3
- w_up: bfloat16 [768, 1536], replicated, may hold values from -0.21875 to 0.21875
- b_up: bfloat16 [1536], replicated, may hold values from -3 to 3
- w_down: bfloat16 [1536, 768], replicated, may hold values from -0.15625 to 0.15625
- b_down: bfloat16 [768], replicated, may hold values from -3 to 3
- cotangent: bfloat16 [12288, 768], P(('seq', 'ray')), may hold values from -6 to 6
Outputs:
- output: bfloat16 [12288, 768], P(('seq', 'ray'))
- grad_rays: float32 [12288, 768], P(('seq', 'ray'))
- grad_latents: float32 [12288, 768], P(('seq', 'ray'))
- grad_ln_gain: float32 [768], replicated
- grad_ln_bias: float32 [768], replicated
- grad_w_query: float32 [768, 768], replicated
- grad_b_query: float32 [768], replicated
- grad_w_key: float32 [768, 768], replicated
- grad_w_value: float32 [768, 768], replicated
- grad_b_value: float32 [768], replicated
- grad_w_out: float32 [768, 768], replicated
- grad_b_out: float32 [768], replicated
- grad_w_up: float32 [768, 1536], replicated
- grad_b_up: float32 [1536], replicated
- grad_w_down: float32 [1536, 768], replicated
- grad_b_down: float32 [768], replicated
Inputs may be any that keep to these rules, and one draw needn't show every extreme that they name: Each row holds the latent lengths of the 3 scenes of one sequence, summing to 3072; the largest of a row is exactly 1536.
All inputs are finite; a program needn't handle non-finite values.
Results may differ from a plain program's by a relative error of at most 0.018.
The roundings to bfloat16 on the way count: a program that leaves them out, or rounds other values in their place, can miss the bound.
Values may be sent and summed in bfloat16 or wider, within the bound.
A program may use at most 192 MiB of HBM per device.

v0:
```python
import jax
import jax.numpy as jnp
from jax import lax
from jax.sharding import PartitionSpec as P

HEADS = 12
HEAD = 64


masked_score = -1e30


def matmul(first_arg, second_arg, first_dim, second_dim):
    return lax.dot_general(
        first_arg,
        second_arg,
        (((first_dim,), (second_dim,)), ((), ())),
        preferred_element_type=jnp.float32,
    )


def split_heads(matrix):
    return matrix.reshape(matrix.shape[0], HEADS, HEAD).transpose(1, 0, 2)


def join_heads(stacked):
    return stacked.transpose(1, 0, 2).reshape(stacked.shape[1], HEADS * HEAD)


def gelu_exact(pre_act):
    return jax.nn.gelu(pre_act, approximate=False)


def local(
    rays,
    latents,
    lengths,
    scenes,
    ln_gain,
    ln_bias,
    w_query,
    b_query,
    w_key,
    w_value,
    b_value,
    w_out,
    b_out,
    w_up,
    b_up,
    w_down,
    b_down,
    cotangent,
):
    scale = HEAD ** (-0.5)
    gathered = lax.all_gather(latents, "ray", axis=0, tiled=True)
    key_total = gathered.shape[0]
    scene_ends = jnp.cumsum(lengths[0])
    positions = jnp.arange(key_total, dtype=jnp.int32)
    segment = jnp.sum((positions[:, None] >= scene_ends[None, :]).astype(jnp.int32), axis=1)
    allowed = scenes[:, None] == segment[None, :]
    inputs = rays.astype(jnp.float32)
    row_mean = jnp.mean(inputs, axis=1, keepdims=True)
    centred = inputs - row_mean
    inverse = lax.rsqrt(jnp.mean(centred * centred, axis=1, keepdims=True) + 1e-05)
    normed = centred * inverse
    gain_full = ln_gain.astype(jnp.float32)
    shifted = (normed * gain_full + ln_bias.astype(jnp.float32)).astype(jnp.bfloat16)
    queries = (matmul(shifted, w_query, 1, 0) + b_query.astype(jnp.float32)).astype(jnp.bfloat16)
    keys = matmul(gathered, w_key, 1, 0).astype(jnp.bfloat16)
    values = (matmul(gathered, w_value, 1, 0) + b_value.astype(jnp.float32)).astype(jnp.bfloat16)
    query_heads = split_heads(queries)
    key_heads = split_heads(keys)
    value_heads = split_heads(values)

    def head_scores(query_one, key_one):
        raw_score = matmul(query_one, key_one, 1, 1)
        return jnp.where(allowed, raw_score * scale, masked_score)

    def forward_head(carry, pieces):
        query_one, key_one, value_one = pieces
        scores = head_scores(query_one, key_one)
        row_max = jnp.max(scores, axis=1, keepdims=True)
        expo_rows = jnp.exp(scores - row_max)
        row_total = jnp.sum(expo_rows, axis=1, keepdims=True)
        weights = (expo_rows / row_total).astype(jnp.bfloat16)
        mixed = matmul(weights, value_one, 1, 0)
        return (carry, (mixed, (row_max + jnp.log(row_total))[:, 0]))

    start_carry = jnp.zeros((), jnp.float32)
    unused, (mixed_heads, log_totals) = lax.scan(
        forward_head, start_carry, (query_heads, key_heads, value_heads)
    )
    attended = join_heads(mixed_heads).astype(jnp.bfloat16)
    hidden = inputs + matmul(attended, w_out, 1, 0) + b_out.astype(jnp.float32)
    hidden_low = hidden.astype(jnp.bfloat16)
    pre_act = matmul(hidden_low, w_up, 1, 0) + b_up.astype(jnp.float32)
    active = gelu_exact(pre_act).astype(jnp.bfloat16)
    result = hidden + matmul(active, w_down, 1, 0) + b_down.astype(jnp.float32)
    grad_top = cotangent.astype(jnp.float32)
    grad_w_down = matmul(active, cotangent, 0, 0)
    grad_b_down = jnp.sum(grad_top, axis=0)
    grad_active = matmul(cotangent, w_down, 1, 1)
    unused_value, gelu_back = jax.vjp(gelu_exact, pre_act)
    grad_pre = gelu_back(grad_active)[0].astype(jnp.bfloat16)
    grad_w_up = matmul(hidden_low, grad_pre, 0, 0)
    grad_b_up = jnp.sum(grad_pre.astype(jnp.float32), axis=0)
    grad_hidden = grad_top + matmul(grad_pre, w_up, 1, 1)
    grad_branch = grad_hidden.astype(jnp.bfloat16)
    grad_w_out = matmul(attended, grad_branch, 0, 0)
    grad_b_out = jnp.sum(grad_branch.astype(jnp.float32), axis=0)
    grad_attended = matmul(grad_branch, w_out, 1, 1).astype(jnp.bfloat16)

    def backward_head(carry, pieces):
        query_one, key_one, value_one, log_one, grad_one = pieces
        weights = jnp.exp(head_scores(query_one, key_one) - log_one[:, None])
        grad_weights = matmul(grad_one, value_one, 1, 1)
        row_dot = jnp.sum(weights * grad_weights, axis=1, keepdims=True)
        grad_scores = (weights * (grad_weights - row_dot)).astype(jnp.bfloat16)
        grad_query = matmul(grad_scores, key_one, 1, 0) * scale
        grad_key = matmul(grad_scores, query_one, 0, 0) * scale
        grad_value = matmul(weights.astype(jnp.bfloat16), grad_one, 0, 0)
        return (carry, (grad_query, grad_key, grad_value))

    unused_carry, (query_grads, key_grads, value_grads) = lax.scan(
        backward_head,
        start_carry,
        (query_heads, key_heads, value_heads, log_totals, split_heads(grad_attended)),
    )
    grad_queries = join_heads(query_grads).astype(jnp.bfloat16)
    grad_keys = join_heads(key_grads).astype(jnp.bfloat16)
    grad_values = join_heads(value_grads).astype(jnp.bfloat16)
    grad_w_query = matmul(shifted, grad_queries, 0, 0)
    grad_b_query = jnp.sum(grad_queries.astype(jnp.float32), axis=0)
    grad_shifted = matmul(grad_queries, w_query, 1, 1)
    grad_gain = jnp.sum(grad_shifted * normed, axis=0)
    grad_bias = jnp.sum(grad_shifted, axis=0)
    grad_normed = grad_shifted * gain_full
    grad_rays = grad_hidden + inverse * (
        grad_normed
        - jnp.mean(grad_normed, axis=1, keepdims=True)
        - normed * jnp.mean(grad_normed * normed, axis=1, keepdims=True)
    )
    grad_w_key = matmul(gathered, grad_keys, 0, 0)
    grad_w_value = matmul(gathered, grad_values, 0, 0)
    grad_b_value = jnp.sum(grad_values.astype(jnp.float32), axis=0)
    grad_latents = lax.psum_scatter(
        (matmul(grad_keys, w_key, 1, 1) + matmul(grad_values, w_value, 1, 1)).astype(jnp.bfloat16),
        "ray",
        scatter_dimension=0,
        tiled=True,
    ).astype(jnp.float32)
    summed = lax.psum(
        (
            grad_gain,
            grad_bias,
            grad_w_query,
            grad_b_query,
            grad_w_key,
            grad_w_value,
            grad_b_value,
            grad_w_out,
            grad_b_out,
            grad_w_up,
            grad_b_up,
            grad_w_down,
            grad_b_down,
        ),
        ("seq", "ray"),
    )
    return (
        result.astype(jnp.bfloat16),
        grad_rays,
        grad_latents,
        summed[0],
        summed[1],
        summed[2],
        summed[3],
        summed[4],
        summed[5],
        summed[6],
        summed[7],
        summed[8],
        summed[9],
        summed[10],
        summed[11],
        summed[12],
    )


def solution(mesh):
    in_specs = (
        P(("seq", "ray"), None),
        P(("seq", "ray"), None),
        P("seq", None),
        P(("seq", "ray")),
        P(),
        P(),
        P(),
        P(),
        P(),
        P(),
        P(),
        P(),
        P(),
        P(),
        P(),
        P(),
        P(),
        P(("seq", "ray"), None),
    )
    out_specs = (
        P(("seq", "ray"), None),
        P(("seq", "ray"), None),
        P(("seq", "ray"), None),
        P(),
        P(),
        P(),
        P(),
        P(),
        P(),
        P(),
        P(),
        P(),
        P(),
        P(),
        P(),
        P(),
    )
    return jax.shard_map(local, mesh=mesh, in_specs=in_specs, out_specs=out_specs, check_vma=False)
```

profile of v0, /device:TPU:0, one launch (start us, length us, event | category | flops | bytes accessed | tf_op | source)
XLA Modules:
  0.0 845.0 jit_solution(11128912317700024839)
XLA Ops:
  18.7 74.1 %all-gather.2.cloned.1.call-done = bf16[3072,768]{1,0:T(8,128)(2,1)} async-done(((bf16[384,768]{1,0:T(8,128)(2,1)}), bf16[3072,768]{1,0:T(8,128)(2,1)}) %all-gather.2.cloned.1.call-update) | async-done | bytes 4718608 | tf_op jit(solution)/shard_map/all_gather | solution.py:55
  92.8 8.8 %convolution_convert_fusion = bf16[3072,768]{0,1:T(8,128)(2,1)} fusion(bf16[3072,768]{1,0:T(8,128)(2,1)} %all-gather.2.cloned.1.call-done, bf16[768,768]{1,0:T(8,128)(2,1)} %param.30), kind=kOutput, calls=%fused_computation.55 | convolution fusion | flops 3626237952 | bytes 10616832 | tf_op jit(solution)/shard_map/dot_general | solution.py:14
  101.6 9.5 %copy.50 = bf16[3072,12,64]{2,0,1:T(8,128)(2,1)} copy(bf16[3072,12,64]{0,2,1:T(8,128)(2,1)} %bitcast.150) | data formatting | bytes 9437184 | tf_op jit(solution)/shard_map/reshape | solution.py:23
  111.1 8.8 %add_convert_fusion.1 = bf16[3072,768]{0,1:T(8,128)(2,1)} fusion(bf16[3072,768]{1,0:T(8,128)(2,1)} %all-gather.2.cloned.1.call-done, bf16[768,768]{1,0:T(8,128)(2,1)} %param.31, f32[768]{0:T(1024)S(1)} %convert_element_type.139), kind=kOutput, calls=%fused_computation.54 | convolution fusion | flops 3628597248 | bytes 10619904 | tf_op jit(solution)/shard_map/dot_general | solution.py:14
  119.9 9.6 %copy.51 = bf16[3072,12,64]{2,0,1:T(8,128)(2,1)} copy(bf16[3072,12,64]{0,2,1:T(8,128)(2,1)} %bitcast.149) | data formatting | bytes 9437184 | tf_op jit(solution)/shard_map/reshape | solution.py:23
  129.5 78.5 %while.28 = (s32[]{:T(128)}, bf16[12,384,64]{1,2,0:T(8,128)(2,1)S(1)}, f32[12,384]{1,0:T(8,128)}, bf16[12,384,64]{2,1,0:T(8,128)(2,1)}, bf16[12,3072,64]{2,1,0:T...) while((s32[]{:T(128)}, ...), condition=%wide.region_7.8_spmd.clone, body=%wide.region_4.7_spmd.clone.sunk | while | flops 312606336 | bytes 15961201 | solution.py:90
  132.4 2.3 fusion.132
  139.0 2.3 fusion.132
  145.5 2.3 fusion.132
  152.0 2.3 fusion.132
  158.6 2.3 fusion.132
  165.1 2.3 fusion.132
  171.6 2.3 fusion.132
  178.1 2.3 fusion.132
  184.7 2.3 fusion.132
  191.2 2.3 fusion.132
  197.7 2.3 fusion.132
  204.2 2.3 fusion.132
  211.8 7.9 convert_reduce_fusion.1
  224.7 3.6 fusion.67
  232.8 164.3 %while.29 = (s32[]{:T(128)}, bf16[12,384,64]{1,2,0:T(8,128)(2,1)}, bf16[12,3072,64]{1,2,0:T(8,128)(2,1)}, bf16[12,3072,64]{1,2,0:T(8,128)(2,1)}, bf16[12,384,64]...) while((s32[]{:T(128)}, bf16[12,384,64]{1,2,0:T(8,128)(2,1)}, ...), condition=%wide.region_10.11_spmd.clone, body=%wide.region_8.10_spmd.clone.sunk | while | flops 766992000 | bytes 39742080 | solution.py:124
  235.5 2.8 multiply_reduce_fusion.3
  239.5 2.6 fusion.143
  249.2 2.8 multiply_reduce_fusion.3
  253.2 2.6 fusion.143
  255.8 2.2 fusion.144
  262.8 2.8 multiply_reduce_fusion.3
  266.9 2.6 fusion.143
  276.5 2.8 multiply_reduce_fusion.3
  280.5 2.6 fusion.143
  283.1 2.2 fusion.144
  290.2 2.8 multiply_reduce_fusion.3
  294.2 2.6 fusion.143
  303.9 2.8 multiply_reduce_fusion.3
  307.9 2.6 fusion.143
  317.5 2.8 multiply_reduce_fusion.3
  321.6 2.6 fusion.143
  331.2 2.8 multiply_reduce_fusion.3
  335.3 2.6 fusion.143
  344.9 2.8 multiply_reduce_fusion.3
  348.9 2.6 fusion.143
  358.5 2.8 multiply_reduce_fusion.3
  362.6 2.6 fusion.143
  372.2 2.8 multiply_reduce_fusion.3
  376.3 2.6 fusion.143
  385.9 2.8 multiply_reduce_fusion.3
  389.9 2.6 fusion.143
  397.1 3.8 fusion.73
  400.9 3.8 fusion.79
  404.8 7.9 convolution_bitcast_fusion.2
  412.7 5.2 convolution_bitcast_fusion.1
  418.0 6.6 fusion.78
  424.6 8.4 add_convert_fusion
  437.9 3.2 convert_reduce_fusion
  441.8 3.4 fusion.65
  447.2 41.2 %all-reduce = (f32[768]{0:T(1024)}, f32[768]{0:T(1024)}, f32[768]{0:T(1024)}, f32[768]{0:T(1024)}, f32[768]{0:T(1024)}, /*index=5*/f32[1536]{0:T(1024)}, f32[768]{0:T(1024)}) all-reduce(f32[768]{0:T(1024)} %get-tuple-element.245, f32[768]{0:T(1024)} %get-tuple-element.248, ...), channel_id=1, replica_groups=mesh['seq'=4,'ray'=8] {'seq','ray'}, use_global_device_ids=true, to_apply=%region_15.16 | all-reduce | flops 6144 | bytes 49152 | tf_op jit(solution)/shard_map/psum | solution.py:152
  488.4 3.6 fusion.57
  492.0 232.6 %all-reduce.4.cloned.1.call-done = (f32[768,768]{1,0:T(8,128)}, f32[768,768]{0,1:T(8,128)}, f32[768,768]{0,1:T(8,128)}, f32[768,768]{1,0:T(8,128)}, f32[768,1536]{1,0:T(8,128)}, /*index=5*/f32[1536,768]{1,0:T(8,128)}) async-done(((f32[768,768]{1,0:T(8,128)}, f32[768,768]{0,1:T(8,128)}, f32[768,768]{0,1:T(8,128)}, f32[768,768]{1,0:T(8,128)}, f32[768,1536]{1,0:T(8,128)}, /*index=5*/f32[1536,768]{1,0:T(8,128)}), ...) | async-done | bytes 18874384 | tf_op jit(solution)/shard_map/psum | solution.py:152
  724.6 3.0 copy.56
  727.6 3.0 copy.57
  730.7 94.0 %reduce-scatter.2.cloned.1.call-done = bf16[384,768]{1,0:T(8,128)(2,1)} async-done(((bf16[3072,768]{1,0:T(8,128)(2,1)}), bf16[384,768]{1,0:T(8,128)(2,1)}) %reduce-scatter.2.cloned.1.call-update) | async-done | bytes 589840 | tf_op jit(solution)/shard_map/reduce_scatter | solution.py:146
  824.7 2.3 convert_element_type.164
  827.0 3.3 copy.93
  830.3 3.4 copy.94
  (234 shorter events, 181.4 us)
Async XLA Ops:
  7.2 204.3 %copy-start = (bf16[1536,768]{1,0:T(8,128)(2,1)S(1)}, bf16[1536,768]{1,0:T(8,128)(2,1)}, u32[]{:S(2)}) copy-start(bf16[1536,768]{1,0:T(8,128)(2,1)} %param.37) | copy-start | bytes 7077892
  7.2 85.6 %all-gather.2.cloned.1.call-start = ((), (), s32[]{:S(2)}) async-start(), calls=%async_computation.1 | async-start | bytes 5308416 | tf_op jit(solution)/shard_map/all_gather | solution.py:55
  7.9 716.7 %all-reduce.4.cloned.1.call-start = ((), (), s32[]{:S(2)}) async-start(), calls=%async_computation.3 | async-start | bytes 37748736 | tf_op jit(solution)/shard_map/psum | solution.py:152
  9.4 3.3 copy-start.17
  10.1 2.6 copy-start.10
  11.3 1.4 copy-start.12
  12.7 0.6 copy-start.14
  15.5 1.8 copy-start.20
  15.5 1.7 copy-start.26
  15.5 1.9 copy-start.21
  15.5 2.5 copy-start.19
  129.5 78.6 %copy-start.1 = (bf16[384,768]{1,0:T(8,128)(2,1)S(1)}, bf16[384,768]{1,0:T(8,128)(2,1)}, u32[]{:S(2)}) copy-start(bf16[384,768]{1,0:T(8,128)(2,1)} %param.22) | copy-start | bytes 1769476
  208.1 3.4 copy-start.6
  208.1 2.2 copy-start.18
  208.1 2.3 copy-start.24
  210.4 14.3 %copy-start.8 = (f32[384,768]{1,0:T(8,128)}, f32[384,768]{1,0:T(8,128)S(1)}, u32[]{:S(2)}) copy-start(f32[384,768]{1,0:T(8,128)S(1)} %fusion.55) | copy-start | bytes 3538948
  210.4 1.5 copy-start.4
  219.7 1.3 copy-start.9
  221.0 1.5 copy-start.7
  232.8 164.3 %copy-start.11 = (f32[768]{0:T(1024)S(1)}, f32[768]{0:T(1024)}, u32[]{:S(2)}) copy-start(f32[768]{0:T(1024)} %copy-done.10) | copy-start | bytes 9220
  397.0 3.9 copy-start.3
  397.1 3.9 copy-start.5
  397.1 7.7 copy-start.23
  400.9 11.7 %slice-start = ((s8[4718592]{0:T(1024)(128)(4,1)}), s8[4194304]{0:T(1024)(128)(4,1)S(1)}, s32[]{:S(2)}) async-start(s8[4718592]{0:T(1024)(128)(4,1)} %bitcast.152), calls=%async_computation.4 | async-start | bytes 8388608
  400.9 11.7 %slice-start.6 = ((s8[4718592]{0:T(1024)(128)(4,1)}), s8[4194304]{0:T(1024)(128)(4,1)S(1)}, s32[]{:S(2)}) async-start(s8[4718592]{0:T(1024)(128)(4,1)} %bitcast.164), calls=%async_computation.10 | async-start | bytes 8388608
  404.8 7.9 slice-start.1
  404.8 7.9 slice-start.7
  417.9 406.7 %reduce-scatter.2.cloned.1.call-start = ((), (), s32[]{:S(2)}) async-start(), calls=%async_computation.2 | async-start | bytes 5308416 | tf_op jit(solution)/shard_map/reduce_scatter | solution.py:146
  418.0 6.6 copy-start.25
  433.0 0.7 copy-start.22
  437.9 3.8 copy-start.13
  441.7 3.4 copy-start.2
  441.8 3.4 copy-start.15
  445.2 2.0 copy-start.16
  824.7 9.0 %slice-start.4 = ((s8[4718592]{0:T(1024)(128)(4,1)}), s8[4194304]{0:T(1024)(128)(4,1)S(1)}, s32[]{:S(2)}) async-start(s8[4718592]{0:T(1024)(128)(4,1)} %bitcast.157), calls=%async_computation.8 | async-start | bytes 8388608
  827.0 6.7 slice-start.5
  830.3 5.6 slice-start.2
  833.6 2.2 slice-start.3
Sparse Core Ops, SparseCore 0:
  10.2 82.5 all-gather.1
  418.1 306.4 all-reduce.3
  729.3 95.3 reduce-scatter.1
where the time goes:
time: 859 us; the launch traced here: 845 us
  waiting for transfers between devices  401 us (47%)
  matrix products  275 us (32%)
  local copies, waits for them, and re-layouts  69 us (8%)
  other arithmetic  42.7 us (5%)
  blocking collectives  41.2 us (5%)
  between operations  14.6 us (2%)
    dot_general x102, matrix products, matmul(): lax.dot_general(first_arg, second_arg, (((first_dim,), (second_dim,)), ((...  275 us
    psum x1, waiting for transfers between devices, local(): lax.psum((grad_gain, grad_bias, grad_w_query, grad_b_query, grad_w_key, g...  233 us
    reduce_scatter x1, waiting for transfers between devices, local(): lax.psum_scatter((matmul(grad_keys, w_key, 1, 1) + matmul(grad_values, w_...  94 us
    all_gather x1, waiting for transfers between devices, local(): gathered = lax.all_gather(latents, 'ray', axis=0, tiled=True)  74.1 us
    psum x1, blocking collectives, local(): lax.psum((grad_gain, grad_bias, grad_w_query, grad_b_query, grad_w_key, g...  41.2 us
    unnamed x77, local copies, waits for them, and re-layouts  20.4 us
    reshape x2, local copies, waits for them, and re-layouts, split_heads(): return matrix.reshape(matrix.shape[0], HEADS, HEAD).transpose(1, 0, 2)  19.1 us
  transfers between devices with their start and end apart: 3, of which 3 were waited for; matrix products, arithmetic and copies ran while one was open for 6% of the time, Pallas kernels for 0%

commit v1 on v0

v1 whole, which is shorter than its diff:
```python
import functools

import jax
import jax.numpy as jnp
from jax import lax
from jax.experimental import pallas as pl
from jax.experimental.pallas import tpu as pltpu
from jax.sharding import PartitionSpec as P

HEADS = 12
HEAD = 64
TILE = 64
WIDE = 256
PACK = WIDE // HEAD
CHUNK = 256

masked_score = -1e30
f32 = jnp.float32
bf16 = jnp.bfloat16


def matmul(first_arg, second_arg, first_dim, second_dim):
    return lax.dot_general(
        first_arg,
        second_arg,
        (((first_dim,), (second_dim,)), ((), ())),
        preferred_element_type=jnp.float32,
    )


def gelu_exact(pre_act):
    return jax.nn.gelu(pre_act, approximate=False)


def own_block():
    row = lax.broadcasted_iota(jnp.int32, (WIDE, WIDE), 0) // TILE
    column = lax.broadcasted_iota(jnp.int32, (WIDE, WIDE), 1) // HEAD
    return row == column


def spread_heads(tile):
    return jnp.where(own_block(), jnp.concatenate([tile] * PACK, axis=0), jnp.zeros((), tile.dtype))


def fold_heads(square):
    kept = jnp.where(own_block(), square, 0.0)
    return sum(kept[TILE * h : TILE * (h + 1), :] for h in range(PACK))


def fold_rows(block, combine):
    return combine(block.reshape(block.shape[0] // 8, 8, WIDE), axis=0)


def in_scene(chunk, start, end):
    rows = lax.broadcasted_iota(jnp.int32, (CHUNK, WIDE), 0) + chunk * CHUNK
    return (rows >= start) & (rows < end)


def chunk_at(chunk):
    return pl.ds(pl.multiple_of(chunk * CHUNK, CHUNK), CHUNK)


def attend_kernel(tiles, meta, q_ref, k_ref, vt_ref, att_ref, lse_ref, s_ref):
    att_ref[...] = jnp.zeros_like(att_ref)
    lse_ref[...] = jnp.zeros_like(lse_ref)

    def one_tile(t, carry):
        start, end = meta[1 + t], meta[1 + tiles + t]
        first, last = start // CHUNK, (end + CHUNK - 1) // CHUNK
        ray_rows = pl.ds(pl.multiple_of(t * TILE, TILE), TILE)
        spread = spread_heads(q_ref[ray_rows, :])

        def score(j, top):
            s = matmul(k_ref[chunk_at(j), :], spread, 1, 1)
            s = jnp.where(in_scene(j, start, end), s, masked_score)
            s_ref[chunk_at(j), :] = s
            return jnp.maximum(top, fold_rows(s, jnp.max))

        top = lax.fori_loop(first, last, score, jnp.full((8, WIDE), masked_score, f32))
        top = jnp.max(top, axis=0, keepdims=True)

        def expo(j, total):
            e = jnp.exp(s_ref[chunk_at(j), :] - top)
            s_ref[chunk_at(j), :] = e
            return total + fold_rows(e, jnp.sum)

        total = lax.fori_loop(first, last, expo, jnp.zeros((8, WIDE), f32))
        total = jnp.sum(total, axis=0, keepdims=True)
        rest = 1.0 / total

        def mix(j, mixed):
            w = (s_ref[chunk_at(j), :] * rest).astype(bf16)
            return mixed + matmul(vt_ref[:, chunk_at(j)], w, 1, 0)

        mixed = lax.fori_loop(first, last, mix, jnp.zeros((WIDE, WIDE), f32))
        att_ref[ray_rows, :] = fold_heads(mixed.T)
        lse_ref[0, pl.ds(t, 1), :] = top + jnp.log(total)
        return carry

    lax.fori_loop(0, meta[0], one_tile, 0)


def attend_back_kernel(tiles, meta, q_ref, k_ref, kt_ref, v_ref, g_ref, att_ref, lse_ref, gq_ref, gk_ref, gv_ref, gk_sum, gv_sum, gqt_sum):
    gq_ref[...] = jnp.zeros_like(gq_ref)
    gk_sum[...] = jnp.zeros_like(gk_sum)
    gv_sum[...] = jnp.zeros_like(gv_sum)

    def one_tile(t, carry):
        start, end = meta[1 + t], meta[1 + tiles + t]
        first, last = start // CHUNK, (end + CHUNK - 1) // CHUNK
        ray_rows = pl.ds(pl.multiple_of(t * TILE, TILE), TILE)
        q_spread = spread_heads(q_ref[ray_rows, :])
        g_tile = g_ref[ray_rows, :]
        g_spread = spread_heads(g_tile)
        product = spread_heads(g_tile.astype(f32) * att_ref[ray_rows, :])
        dots = lax.dot_general(
            jnp.ones((8, WIDE), f32),
            product,
            (((1,), (1,)), ((), ())),
            precision=lax.Precision.HIGHEST,
            preferred_element_type=f32,
        )[0:1, :]
        lse = lse_ref[0, pl.ds(t, 1), :]
        gqt_sum[...] = jnp.zeros_like(gqt_sum)

        def step(j, carry):
            at = chunk_at(j)
            s = matmul(k_ref[at, :], q_spread, 1, 1)
            p = jnp.where(in_scene(j, start, end), jnp.exp(s - lse), 0.0)
            gv_sum[at, :] += matmul(p.astype(bf16), g_spread, 1, 0)
            gp = matmul(v_ref[at, :], g_spread, 1, 1)
            gs = (p * (gp - dots)).astype(bf16)
            gk_sum[at, :] += matmul(gs, q_spread, 1, 0)
            gqt_sum[...] += matmul(kt_ref[:, at], gs, 1, 0)
            return carry

        lax.fori_loop(first, last, step, 0)
        gq_ref[ray_rows, :] = (fold_heads(gqt_sum[...].T) * HEAD ** (-0.5)).astype(bf16)
        return carry

    lax.fori_loop(0, meta[0], one_tile, 0)
    gk_ref[...] = gk_sum[...].astype(bf16)
    gv_ref[...] = gv_sum[...].astype(bf16)


def scene_plan(lengths, scenes, rays):
    tiles = rays // TILE + lengths.shape[0] - 1
    kinds = jnp.arange(lengths.shape[0], dtype=jnp.int32)
    one_hot = scenes[:, None] == kinds[None, :]
    before = jnp.tril(jnp.ones((rays, rays), bf16), -1)
    rank = matmul(before, one_hot.astype(bf16), 1, 0).astype(jnp.int32)
    counts = jnp.sum(one_hot.astype(jnp.int32), axis=0)
    scene_tiles = (counts + TILE - 1) // TILE
    tile_ends = jnp.cumsum(scene_tiles)
    first_slot = (tile_ends - scene_tiles) * TILE
    slot = jnp.sum(jnp.where(one_hot, rank + first_slot[None, :], 0), axis=1)
    order = (jnp.arange(tiles * TILE, dtype=jnp.int32)[:, None] == slot[None, :]).astype(bf16)
    ends = jnp.cumsum(lengths)
    tile_scene = jnp.sum(jnp.arange(tiles, dtype=jnp.int32)[:, None] >= tile_ends[None, :], axis=1)
    pick = tile_scene[:, None] == kinds[None, :]
    tile_start = jnp.sum(jnp.where(pick, (ends - lengths)[None, :], 0), axis=1)
    tile_end = jnp.sum(jnp.where(pick, ends[None, :], 0), axis=1)
    meta = jnp.concatenate([tile_ends[-1:], tile_start, tile_end]).astype(jnp.int32)
    return tiles, order, meta


def local(
    rays,
    latents,
    lengths,
    scenes,
    ln_gain,
    ln_bias,
    w_query,
    b_query,
    w_key,
    w_value,
    b_value,
    w_out,
    b_out,
    w_up,
    b_up,
    w_down,
    b_down,
    cotangent,
):
    scale = HEAD ** (-0.5)
    width = rays.shape[1]
    groups = width // WIDE
    gathered = lax.all_gather(latents, "ray", axis=0, tiled=True)
    key_total = gathered.shape[0]
    tiles, order, meta = scene_plan(lengths[0], scenes, rays.shape[0])
    slots = tiles * TILE
    inputs = rays.astype(f32)
    row_mean = jnp.mean(inputs, axis=1, keepdims=True)
    centred = inputs - row_mean
    inverse = lax.rsqrt(jnp.mean(centred * centred, axis=1, keepdims=True) + 1e-05)
    normed = centred * inverse
    gain_full = ln_gain.astype(f32)
    shifted = (normed * gain_full + ln_bias.astype(f32)).astype(bf16)
    queries = (matmul(shifted, w_query, 1, 0) + b_query.astype(f32)).astype(bf16)
    q_sorted = (matmul(order, queries, 1, 0) * scale).astype(bf16)
    keys = matmul(gathered, w_key, 1, 0).astype(bf16)
    keys_t = matmul(w_key, gathered, 0, 1).astype(bf16)
    values = (matmul(gathered, w_value, 1, 0) + b_value.astype(f32)).astype(bf16)
    values_t = (matmul(w_value, gathered, 0, 1) + b_value.astype(f32)[:, None]).astype(bf16)

    smem = pl.BlockSpec(memory_space=pltpu.SMEM)
    slot_spec = pl.BlockSpec((slots, WIDE), lambda g: (0, g))
    key_spec = pl.BlockSpec((key_total, WIDE), lambda g: (0, g))
    turned_spec = pl.BlockSpec((WIDE, key_total), lambda g: (g, 0))
    lse_spec = pl.BlockSpec((1, tiles, WIDE), lambda g: (g, 0, 0))
    params = pltpu.CompilerParams(vmem_limit_bytes=48 << 20)
    att_sorted, lse = pl.pallas_call(
        functools.partial(attend_kernel, tiles),
        grid=(groups,),
        out_shape=(
            jax.ShapeDtypeStruct((slots, width), f32),
            jax.ShapeDtypeStruct((groups, tiles, WIDE), f32),
        ),
        in_specs=[smem, slot_spec, key_spec, turned_spec],
        out_specs=(slot_spec, lse_spec),
        scratch_shapes=[pltpu.VMEM((key_total, WIDE), f32)],
        compiler_params=params,
        name="attend",
    )(meta, q_sorted, keys, values_t)
    attended = matmul(order, att_sorted.astype(bf16), 0, 0).astype(bf16)

    hidden = inputs + matmul(attended, w_out, 1, 0) + b_out.astype(f32)
    hidden_low = hidden.astype(bf16)
    pre_act = matmul(hidden_low, w_up, 1, 0) + b_up.astype(f32)
    active = gelu_exact(pre_act).astype(bf16)
    result = hidden + matmul(active, w_down, 1, 0) + b_down.astype(f32)
    grad_top = cotangent.astype(f32)
    grad_w_down = matmul(active, cotangent, 0, 0)
    grad_b_down = jnp.sum(grad_top, axis=0)
    grad_active = matmul(cotangent, w_down, 1, 1)
    unused_value, gelu_back = jax.vjp(gelu_exact, pre_act)
    grad_pre = gelu_back(grad_active)[0].astype(bf16)
    grad_w_up = matmul(hidden_low, grad_pre, 0, 0)
    grad_b_up = jnp.sum(grad_pre.astype(f32), axis=0)
    grad_hidden = grad_top + matmul(grad_pre, w_up, 1, 1)
    grad_branch = grad_hidden.astype(bf16)
    grad_w_out = matmul(attended, grad_branch, 0, 0)
    grad_b_out = jnp.sum(grad_branch.astype(f32), axis=0)
    grad_attended = matmul(grad_branch, w_out, 1, 1).astype(bf16)
    early = lax.psum(
        tuple(g.astype(bf16) for g in (grad_w_out, grad_w_up, grad_w_down)), ("seq", "ray")
    )
    g_sorted = matmul(order, grad_attended, 1, 0).astype(bf16)

    gq_sorted, grad_keys, grad_values = pl.pallas_call(
        functools.partial(attend_back_kernel, tiles),
        grid=(groups,),
        out_shape=(
            jax.ShapeDtypeStruct((slots, width), bf16),
            jax.ShapeDtypeStruct((key_total, width), bf16),
            jax.ShapeDtypeStruct((key_total, width), bf16),
        ),
        in_specs=[smem, slot_spec, key_spec, turned_spec, key_spec, slot_spec, slot_spec, lse_spec],
        out_specs=(slot_spec, key_spec, key_spec),
        scratch_shapes=[
            pltpu.VMEM((key_total, WIDE), f32),
            pltpu.VMEM((key_total, WIDE), f32),
            pltpu.VMEM((WIDE, WIDE), f32),
        ],
        compiler_params=params,
        name="attend_back",
    )(meta, q_sorted, keys, keys_t, values, g_sorted, att_sorted, lse)
    grad_queries = matmul(order, gq_sorted, 0, 0).astype(bf16)

    grad_w_query = matmul(shifted, grad_queries, 0, 0)
    grad_b_query = jnp.sum(grad_queries.astype(f32), axis=0)
    grad_shifted = matmul(grad_queries, w_query, 1, 1)
    grad_gain = jnp.sum(grad_shifted * normed, axis=0)
    grad_bias = jnp.sum(grad_shifted, axis=0)
    grad_normed = grad_shifted * gain_full
    grad_rays = grad_hidden + inverse * (
        grad_normed
        - jnp.mean(grad_normed, axis=1, keepdims=True)
        - normed * jnp.mean(grad_normed * normed, axis=1, keepdims=True)
    )
    grad_w_key = matmul(gathered, grad_keys, 0, 0)
    grad_w_value = matmul(gathered, grad_values, 0, 0)
    grad_b_value = jnp.sum(grad_values.astype(f32), axis=0)
    grad_latents = lax.psum_scatter(
        (matmul(grad_keys, w_key, 1, 1) + matmul(grad_values, w_value, 1, 1)).astype(bf16),
        "ray",
        scatter_dimension=0,
        tiled=True,
    ).astype(f32)
    late = lax.psum(
        tuple(g.astype(bf16) for g in (grad_w_query, grad_w_key, grad_w_value)), ("seq", "ray")
    )
    rows = lax.psum(
        (grad_gain, grad_bias, grad_b_query, grad_b_value, grad_b_out, grad_b_up, grad_b_down),
        ("seq", "ray"),
    )
    return (
        result.astype(bf16),
        grad_rays,
        grad_latents,
        rows[0],
        rows[1],
        late[0].astype(f32),
        rows[2],
        late[1].astype(f32),
        late[2].astype(f32),
        rows[3],
        early[0].astype(f32),
        rows[4],
        early[1].astype(f32),
        rows[5],
        early[2].astype(f32),
        rows[6],
    )


def solution(mesh):
    whole = P(("seq", "ray"), None)
    in_specs = (whole, whole, P("seq", None), P(("seq", "ray"))) + (P(),) * 13 + (whole,)
    out_specs = (whole,) * 3 + (P(),) * 13
    return jax.shard_map(local, mesh=mesh, in_specs=in_specs, out_specs=out_specs, check_vma=False)
```

time: 859 us -> 619 us (0.72); the launches traced: 845 us -> 615 us
  matrix products: 275 us -> 92.7 us
  waiting for transfers between devices: 401 us -> 283 us
  Pallas kernels: 0 us -> 116 us
  local copies, waits for them, and re-layouts: 69 us -> 10.3 us
  blocking collectives: 41.2 us -> 73.4 us
  other arithmetic: 42.7 us -> 26.2 us
    dot_general x102 -> x23, matrix products: 275 us -> 92.7 us  [matmul(): lax.dot_general(first_arg, second_arg, (((first_dim,), (second_dim,)), ((...]
    pallas_call x0 -> x2, Pallas kernels: none -> 116 us  [the longest x1 68.6 us: local(): pl.pallas_call(functools.partial(attend_back_kernel, tiles), grid=(groups...]
    psum x1, waiting for transfers between devices: 233 us -> 127 us  [local(): lax.psum(tuple((g.astype(bf16) for g in (grad_w_query, grad_w_key, grad_w...]
    psum x1, blocking collectives: 41.2 us -> 73.4 us  [local(): lax.psum((grad_gain, grad_bias, grad_b_query, grad_b_value, grad_b_out, g...]
    reshape x2 -> x0, local copies, waits for them, and re-layouts: 19.1 us -> none  [split_heads(): return matrix.reshape(matrix.shape[0], HEADS, HEAD).transpose(1, 0, 2)]
    dynamic_update_slice x12 -> x0, local copies, waits for them, and re-layouts: 15.9 us -> none  [local(): lax.scan(forward_head, start_carry, (query_heads, key_heads, value_heads))]
    reduce_sum x16 -> x5, other arithmetic: 15.9 us -> 3.82 us  [the longest x1 2.14 us: local(): grad_b_out = jnp.sum(grad_branch.astype(f32), axis=0)]
    unnamed x77 -> x94, local copies, waits for them, and re-layouts: 20.4 us -> 9.68 us
  transfers between devices with their start and end apart: 3 -> 3, of which waited for: 3 -> 3; matrix products, arithmetic and copies ran while one was open for 6% -> 9% of each run, Pallas kernels for 0% -> 0%
where the time goes in v1:
time: 619 us; the launch traced here: 615 us
  waiting for transfers between devices  283 us (46%)
  Pallas kernels  116 us (19%)
  matrix products  92.7 us (15%)
  blocking collectives  73.4 us (12%)
  other arithmetic  26.2 us (4%)
  between operations  14.5 us (2%)
  local copies, waits for them, and re-layouts  10.3 us (2%)
    psum x1, waiting for transfers between devices, local(): lax.psum(tuple((g.astype(bf16) for g in (grad_w_query, grad_w_key, grad_w...  127 us
    dot_general x23, matrix products, matmul(): lax.dot_general(first_arg, second_arg, (((first_dim,), (second_dim,)), ((...  92.7 us
    reduce_scatter x1, waiting for transfers between devices, local(): lax.psum_scatter((matmul(grad_keys, w_key, 1, 1) + matmul(grad_values, w_...  84.2 us
    psum x1, blocking collectives, local(): lax.psum((grad_gain, grad_bias, grad_b_query, grad_b_value, grad_b_out, g...  73.4 us
    all_gather x1, waiting for transfers between devices, local(): gathered = lax.all_gather(latents, 'ray', axis=0, tiled=True)  70.2 us
    pallas_call x1, Pallas kernels, local(): pl.pallas_call(functools.partial(attend_back_kernel, tiles), grid=(groups...  68.6 us
    pallas_call x1, Pallas kernels, local(): pl.pallas_call(functools.partial(attend_kernel, tiles), grid=(groups,), o...  47.2 us
  transfers between devices with their start and end apart: 3, of which 3 were waited for; matrix products, arithmetic and copies ran while one was open for 9% of the time, Pallas kernels for 0%

profile of v1, /device:TPU:0, one launch (start us, length us, event | category | flops | bytes accessed | tf_op | source)
XLA Modules:
  0.0 615.5 jit_solution(8135169803667331858)
XLA Ops:
  7.2 0.7 all-gather.2.cloned.1.call-update
  8.0 0.8 reduce-window.9
  8.8 0.8 convert_reduce_fusion.6
  9.6 0.2 reduce-window.6
  9.8 0.6 slice.6
  10.4 0.7 convert_element_type.157
  11.1 0.7 convert_element_type.155
  11.8 0.7 convert_element_type.154
  12.4 0.7 convert_element_type.161
  13.1 0.7 convert_element_type.165
  13.8 0.7 convert_element_type.167
  14.5 0.1 convert_reduce_fusion.7
  14.6 0.7 fusion.43
  15.2 0.1 select_reduce_fusion.1
  15.3 0.7 pad_add_fusion.meta
  16.1 1.1 fusion.28
  17.1 1.2 convert_reduce_fusion.2
  18.4 1.4 fusion.25
  19.8 2.9 multiply_convert_fusion.1.q_ref
  22.6 70.2 %all-gather.2.cloned.1.call-done = bf16[3072,768]{1,0:T(8,128)(2,1)} async-done(((bf16[384,768]{1,0:T(8,128)(2,1)}), bf16[3072,768]{1,0:T(8,128)(2,1)}) %all-gather.2.cloned.1.call-update) | async-done | bytes 4718608 | tf_op jit(solution)/shard_map/all_gather | solution.py:190
  92.8 8.9 %convolution_convert_fusion.1.k_ref = bf16[3072,768]{1,0:T(8,128)(2,1)} fusion(bf16[3072,768]{1,0:T(8,128)(2,1)} %all-gather.2.cloned.1.call-done, bf16[768,768]{1,0:T(8,128)(2,1)} %param.26), kind=kOutput, calls=%fused_computation.5 | convolution fusion | flops 3626237952 | bytes 10616832 | tf_op jit(solution)/shard_map/dot_general | solution.py:23
  101.7 6.0 add_convert_fusion.2.vt_ref
  107.7 47.2 %attend.1 = (f32[512,768]{1,0:T(8,128)S(1)}, f32[3,8,256]{2,1,0:T(8,128)S(1)}) custom-call(s32[17]{0:T(128)S(1)} %pad_add_fusion.meta, bf16[512,768]{1,0:T(8,128)(2,1)S(1)} %multiply_convert_fusion.1.q_ref, bf16[3072,768]{1,0:T(8,128)(2,1)} %convolution_convert_fusion.1.k_ref, bf16[768,3072]{1,0:T(8,128)(2,1)} %add_convert_fusion.2.vt_ref), custom_call_target="tpu_custom_call" | custom-call | tf_op jit(solution)/shard_map/attend/pallas_call | solution.py:214
  154.9 0.5 convolution_convert_fusion.11
  155.4 0.6 fusion.12
  156.1 1.2 copy-done.29
  157.3 1.1 convolution_add_fusion
  158.4 0.4 copy-done.18
  158.8 8.1 %convert_reduce_fusion.1 = (f32[1536]{0:T(1024)}, bf16[384,1536]{1,0:T(8,128)(2,1)S(1)}, f32[384,1536]{1,0:T(8,128)}) fusion(f32[384,1536]{1,0:T(8,128)S(1)} %convolution_add_fusion, bf16[384,768]{1,0:T(8,128)(2,1)S(1)} %copy-done.18, bf16[1536,768]{1,0:T(8,128)(2,1)S(1)} %copy-done), kind=kOutput, calls=%fused_computation.11 | convolution fusion | flops 949615104 | bytes 8853504 | tf_op jit(solution)/shard_map/dot_general | solution.py:23
  166.9 1.0 copy-done.37
  167.9 2.1 convert_add_fusion.1
  170.1 3.7 convolution_convert_fusion.8.g_ref
  173.8 3.4 convolution_convert_fusion.4
  177.2 2.8 convolution_convert_fusion.3
  180.1 0.5 multiply_convert_fusion
  180.6 0.7 copy-done.31
  181.3 8.7 %convolution_convert_fusion.kt_ref = bf16[768,3072]{1,0:T(8,128)(2,1)} fusion(bf16[768,768]{1,0:T(8,128)(2,1)S(1)} %copy-done.31, bf16[3072,768]{1,0:T(8,128)(2,1)} %all-gather.2.cloned.1.call-done), kind=kOutput, calls=%fused_computation.4 | convolution fusion | flops 3626237952 | bytes 10616832 | tf_op jit(solution)/shard_map/dot_general | solution.py:23
  190.1 5.8 add_convert_fusion.1.v_ref
  195.9 68.6 %attend_back.1 = (bf16[512,768]{1,0:T(8,128)(2,1)S(1)}, bf16[3072,768]{1,0:T(8,128)(2,1)}, bf16[3072,768]{1,0:T(8,128)(2,1)}) custom-call(s32[17]{0:T(128)S(1)} %pad_add_fusion.meta, bf16[512,768]{1,0:T(8,128)(2,1)S(1)} %multiply_convert_fusion.1.q_ref, bf16[3072,768]{1,0:T(8,128)(2,1)} %convolution_convert_fusion.1.k_ref, ...), custom_call_target="tpu_custom_call" | custom-call | tf_op jit(solution)/shard_map/attend_back/pallas_call | solution.py:252
  264.5 1.1 convert_reduce_fusion.5
  265.6 2.0 convolution_convert_fusion.7
  267.6 2.8 convolution_convert_fusion.2
  270.4 5.0 fusion.13
  275.4 5.0 fusion.14
  280.5 6.5 %fusion.53 = f32[3072,768]{1,0:T(8,128)S(1)} fusion(bf16[3072,768]{1,0:T(8,128)(2,1)} %get-tuple-element.24, bf16[768,768]{1,0:T(8,128)(2,1)} %param.26), kind=kOutput, calls=%fused_computation.114 | convolution fusion | flops 3623878656 | bytes 15335424 | tf_op jit(solution)/shard_map/dot_general | solution.py:23
  287.1 8.3 %add_convert_fusion = bf16[3072,768]{1,0:T(8,128)(2,1)} fusion(f32[3072,768]{1,0:T(8,128)S(1)} %fusion.53, bf16[3072,768]{1,0:T(8,128)(2,1)} %get-tuple-element.25, bf16[768,768]{1,0:T(8,128)(2,1)S(1)} %copy-done.34), kind=kOutput, calls=%fused_computation.1 | convolution fusion | flops 3628597248 | bytes 20054016 | tf_op jit(solution)/shard_map/dot_general | solution.py:23
  295.4 0.7 copy-done.26
  296.0 0.6 convert_element_type.169
  296.6 0.1 convert_reduce_fusion.3
  296.7 3.1 fusion.24
  299.9 2.1 convert_reduce_fusion.4
  302.0 0.7 convert_reduce_fusion
  302.7 73.4 %all-reduce = (f32[768]{0:T(1024)}, f32[768]{0:T(1024)}, f32[768]{0:T(1024)}, f32[768]{0:T(1024)}, f32[768]{0:T(1024)}, /*index=5*/f32[1536]{0:T(1024)}, f32[768]{0:T(1024)}) all-reduce(f32[768]{0:T(1024)} %get-tuple-element.58, f32[768]{0:T(1024)} %get-tuple-element.61, ...), channel_id=1, replica_groups=mesh['seq'=4,'ray'=8] {'seq','ray'}, use_global_device_ids=true, to_apply=%region_13.14 | all-reduce | flops 6144 | bytes 49152 | tf_op jit(solution)/shard_map/psum | solution.py:295
  376.1 3.2 fusion.16
  379.3 127.4 %all-reduce.4.cloned.1.call-done = (bf16[768,768]{0,1:T(8,128)(2,1)}, bf16[768,768]{0,1:T(8,128)(2,1)}, bf16[768,768]{1,0:T(8,128)(2,1)}, bf16[768,768]{1,0:T(8,...) async-done(((bf16[768,768]{0,1:T(8,128)(2,1)}, bf16[768,768]{0,1:T(8,128)(2,1)}, bf16[768,768]{1,0:T(8,128)(2,1)}, bf16[768,768]{1,0:T(8,128)(2,1)}, ...) | async-done | bytes 9437200 | tf_op jit(solution)/shard_map/psum | solution.py:292
  506.7 2.9 convert_element_type.182
  509.6 1.8 copy.36
  511.4 2.8 copy.37
  514.2 1.6 convert_element_type.192
  515.8 0.9 copy-done.9
  516.7 2.8 convert_element_type.195
  519.6 2.5 convert_element_type.198
  522.1 84.2 %reduce-scatter.2.cloned.1.call-done = bf16[384,768]{1,0:T(8,128)(2,1)} async-done(((bf16[3072,768]{1,0:T(8,128)(2,1)}), bf16[384,768]{1,0:T(8,128)(2,1)}) %reduce-scatter.2.cloned.1.call-update) | async-done | bytes 589840 | tf_op jit(solution)/shard_map/reduce_scatter | solution.py:286
  606.3 2.2 convert_element_type.180
  (100 shorter events, 0.4 us)
Async XLA Ops:
  7.2 151.2 %copy-start = (bf16[1536,768]{1,0:T(8,128)(2,1)S(1)}, bf16[1536,768]{1,0:T(8,128)(2,1)}, u32[]{:S(2)}) copy-start(bf16[1536,768]{1,0:T(8,128)(2,1)} %param.33) | copy-start | bytes 7077892
  7.2 85.6 %all-gather.2.cloned.1.call-start = ((), (), s32[]{:S(2)}) async-start(), calls=%async_computation.1 | async-start | bytes 5308416 | tf_op jit(solution)/shard_map/all_gather | solution.py:190
  7.9 498.8 %all-reduce.4.cloned.1.call-start = ((), (), s32[]{:S(2)}) async-start(), calls=%async_computation.3 | async-start | bytes 18874368 | tf_op jit(solution)/shard_map/psum | solution.py:292
  11.7 10.9 %copy-start.21 = (f32[768]{0:T(1024)}, f32[768]{0:T(1024)S(1)}, u32[]{:S(2)}) copy-start(f32[768]{0:T(1024)S(1)} %convert_element_type.155) | copy-start | bytes 9220
  17.1 152.9 %copy-start.24 = (s32[384]{0:T(512)}, s32[384]{0:T(512)S(1)}, u32[]{:S(2)}) copy-start(s32[384]{0:T(512)S(1)} %fusion.28) | copy-start | bytes 4612
  19.7 277.0 %copy-start.20 = (f32[384]{0:T(512)}, f32[384]{0:T(512)S(1)}, u32[]{:S(2)}) copy-start(f32[384]{0:T(512)S(1)} %add_rsqrt_fusion) | copy-start | bytes 4612
  92.8 8.9 %copy-start.27 = (bf16[3072,768]{1,0:T(8,128)(2,1)S(1)}, bf16[3072,768]{1,0:T(8,128)(2,1)}, u32[]{:S(2)}) copy-start(bf16[3072,768]{1,0:T(8,128)(2,1)} %all-gather.2.cloned.1.call-done) | copy-start | bytes 14155780
  92.8 8.9 %copy-start.32 = (bf16[768,768]{1,0:T(8,128)(2,1)S(1)}, bf16[768,768]{1,0:T(8,128)(2,1)}, u32[]{:S(2)}) copy-start(bf16[768,768]{1,0:T(8,128)(2,1)} %param.27) | copy-start | bytes 3538948
  107.7 47.7 %copy-start.4 = (bf16[384,768]{1,0:T(8,128)(2,1)S(1)}, bf16[384,768]{1,0:T(8,128)(2,1)}, u32[]{:S(2)}) copy-start(bf16[384,768]{1,0:T(8,128)(2,1)} %param.18) | copy-start | bytes 1769476
  107.7 47.7 %copy-start.30 = (bf16[768,768]{1,0:T(8,128)(2,1)S(1)}, bf16[768,768]{1,0:T(8,128)(2,1)}, u32[]{:S(2)}) copy-start(bf16[768,768]{1,0:T(8,128)(2,1)} %param.29) | copy-start | bytes 3538948
  154.9 1.2 copy-start.1
  155.4 3.0 copy-start.10
  155.4 1.9 copy-start.29
  157.3 1.1 copy-start.35
  157.3 1.5 copy-start.18
  158.8 8.1 %copy-start.11 = (f32[384,1536]{1,0:T(8,128)}, f32[384,1536]{1,0:T(8,128)S(1)}, u32[]{:S(2)}) copy-start(f32[384,1536]{1,0:T(8,128)S(1)} %convolution_add_fusion) | copy-start | bytes 7077892
  166.9 1.0 copy-start.37
  173.8 3.4 copy-start.36
  173.8 3.4 copy-start.38
  177.2 2.8 copy-start.12
  177.2 2.8 copy-start.13
  180.1 1.3 copy-start.31
  180.1 10.0 %slice-start.4 = ((s8[4718592]{0:T(1024)(128)(4,1)}), s8[4194304]{0:T(1024)(128)(4,1)S(1)}, s32[]{:S(2)}) async-start(s8[4718592]{0:T(1024)(128)(4,1)} %bitcast.63), calls=%async_computation.8 | async-start | bytes 8388608
  181.3 86.3 %copy-start.16 = (bf16[384,1536]{1,0:T(8,128)(2,1)}, bf16[384,1536]{1,0:T(8,128)(2,1)S(1)}, u32[]{:S(2)}) copy-start(bf16[384,1536]{1,0:T(8,128)(2,1)S(1)} %multiply_convert_fusion) | copy-start | bytes 3538948
  181.3 8.7 %slice-start.5 = ((s8[4718592]{0:T(1024)(128)(4,1)}), s8[524288]{0:T(1024)(128)(4,1)S(1)}, s32[]{:S(2)}) async-start(s8[4718592]{0:T(1024)(128)(4,1)} %bitcast.63), calls=%async_computation.9 | async-start | bytes 1048576
  181.3 8.7 %copy-start.33 = (bf16[768,768]{1,0:T(8,128)(2,1)S(1)}, bf16[768,768]{1,0:T(8,128)(2,1)}, u32[]{:S(2)}) copy-start(bf16[768,768]{1,0:T(8,128)(2,1)} %param.27) | copy-start | bytes 3538948
  190.1 5.8 copy-start.2
  190.1 5.8 copy-start.3
  195.9 68.6 %copy-start.25 = (s32[384]{0:T(512)S(1)}, s32[384]{0:T(512)}, u32[]{:S(2)}) copy-start(s32[384]{0:T(512)} %copy-done.24) | copy-start | bytes 4612
  195.9 69.7 %copy-start.5 = (bf16[384,768]{1,0:T(8,128)(2,1)S(1)}, bf16[384,768]{1,0:T(8,128)(2,1)}, u32[]{:S(2)}) copy-start(bf16[384,768]{1,0:T(8,128)(2,1)} %param.18) | copy-start | bytes 1769476
  195.9 69.7 %copy-start.22 = (f32[768]{0:T(1024)S(1)}, f32[768]{0:T(1024)}, u32[]{:S(2)}) copy-start(f32[768]{0:T(1024)} %copy-done.21) | copy-start | bytes 9220
  264.5 3.1 copy-start.19
  265.6 4.8 copy-start.39
  265.6 4.8 copy-start.28
  267.6 7.8 %slice-start = ((s8[4718592]{0:T(1024)(128)(4,1)}), s8[4194304]{0:T(1024)(128)(4,1)S(1)}, s32[]{:S(2)}) async-start(s8[4718592]{0:T(1024)(128)(4,1)} %bitcast.58), calls=%async_computation.4 | async-start | bytes 8388608
  270.4 5.0 slice-start.1
  280.5 325.9 %reduce-scatter.2.cloned.1.call-start = ((), (), s32[]{:S(2)}) async-start(), calls=%async_computation.2 | async-start | bytes 5308416 | tf_op jit(solution)/shard_map/reduce_scatter | solution.py:286
  280.5 6.5 %copy-start.34 = (bf16[768,768]{1,0:T(8,128)(2,1)S(1)}, bf16[768,768]{1,0:T(8,128)(2,1)}, u32[]{:S(2)}) copy-start(bf16[768,768]{1,0:T(8,128)(2,1)} %param.27) | copy-start | bytes 3538948
  295.3 0.7 copy-start.26
  295.3 1.4 copy-start.6
  296.6 3.3 copy-start.7
  296.6 5.4 slice-start.2
  296.7 5.3 slice-start.3
  302.0 74.1 %copy-start.17 = (bf16[384,1536]{1,0:T(8,128)(2,1)S(1)}, bf16[384,1536]{1,0:T(8,128)(2,1)}, u32[]{:S(2)}) copy-start(bf16[384,1536]{1,0:T(8,128)(2,1)} %copy-done.16) | copy-start | bytes 3538948
  302.0 74.1 %copy-start.23 = (f32[768]{0:T(1024)S(1)}, f32[768]{0:T(1024)}, u32[]{:S(2)}) copy-start(f32[768]{0:T(1024)} %convert_element_type.169) | copy-start | bytes 9220
  506.7 2.9 copy-start.15
  511.4 2.8 copy-start.14
  514.2 2.5 copy-start.9
  516.7 2.8 copy-start.8
Sparse Core Ops, SparseCore 0:
  10.2 82.5 all-gather.1
  280.6 226.0 all-reduce.3
  510.8 95.5 reduce-scatter.1

commit v2 on v1

--- a/solution.py
+++ b/solution.py
@@ -162,6 +162,553 @@
     tile_end = jnp.sum(jnp.where(pick, ends[None, :], 0), axis=1)
     meta = jnp.concatenate([tile_ends[-1:], tile_start, tile_end]).astype(jnp.int32)
     return tiles, order, meta
+
+
+MESH = pl.DeviceIdType.MESH
+SLOW = 4
+
+
+def flip(index, bit):
+    return index + bit * (1 - 2 * ((index // bit) % 2))
+
+
+def bits_of(count):
+    bits = []
+    while count > 1:
+        count //= 2
+        bits.append(count)
+    return bits
+
+
+def lane_rows(start, size):
+    return pl.ds(pl.multiple_of(start, 16), size)
+
+
+class Place:
+    def __init__(self, n_seq, n_ray):
+        self.seq = lax.axis_index("seq")
+        self.ray = lax.axis_index("ray")
+        self.n_fast = n_ray // SLOW
+        self.core = self.seq % 2
+        self.slow = self.ray // self.n_fast
+        self.fast = self.ray % self.n_fast
+        self.x_bits = [("seq", 2 * b) for b in bits_of(n_seq // 2)]
+        self.fast_bits = [("ray", b) for b in bits_of(self.n_fast)]
+        self.slow_bits = [("ray", self.n_fast * b) for b in bits_of(SLOW)]
+        self.spots = (self.slow, SLOW - 1 - self.slow)
+
+    def across(self, axis, bit):
+        if axis == "seq":
+            return (flip(self.seq, bit), self.ray)
+        return (self.seq, flip(self.ray, bit))
+
+    def value(self, axis, bit):
+        return ((self.seq if axis == "seq" else self.ray) // bit) % 2
+
+    def along(self, way):
+        return (self.seq, self.ray + (self.n_fast if way == 0 else -self.n_fast))
+
+    def mirrored(self, way, chunk):
+        return chunk if way == 0 else SLOW - 1 - chunk
+
+
+def remote(src, dst, send_sem, recv_sem, device):
+    return pltpu.make_async_remote_copy(
+        src_ref=src,
+        dst_ref=dst,
+        send_sem=send_sem,
+        recv_sem=recv_sem,
+        device_id=device,
+        device_id_type=MESH,
+    )
+
+
+def greet(place, exchanges):
+    barrier = pltpu.get_barrier_semaphore()
+    for axis, bit in exchanges:
+        pl.semaphore_signal(barrier, inc=1, device_id=place.across(axis, bit), device_id_type=MESH)
+    for step in (1, SLOW - 1):
+        beside = (place.seq, (place.slow + step) % SLOW * place.n_fast + place.fast)
+        pl.semaphore_signal(barrier, inc=1, device_id=beside, device_id_type=MESH)
+    pl.semaphore_wait(barrier, len(exchanges) + 2)
+
+
+class Line:
+    def __init__(self, place, stage, recv, send_sem, recv_sem):
+        self.place, self.stage, self.recv, self.send_sem, self.recv_sem = place, stage, recv, send_sem, recv_sem
+
+    def copy(self, way, t):
+        return remote(
+            self.stage(way, t), self.recv(way, t), self.send_sem(way, t), self.recv_sem(way, t), self.place.along(way)
+        )
+
+    def landed(self, way, t):
+        remote(
+            self.stage(way, t), self.recv(way, t), self.send_sem(way, t), self.recv_sem(way, t), self.place.along(1 - way)
+        ).wait_recv()
+        return self.recv(way, t)[...].astype(f32)
+
+    def step(self, t, own):
+        for way in range(2):
+            spot = self.place.spots[way]
+            chunk = self.place.mirrored(way, SLOW - 1 - (t - spot))
+
+            @pl.when((spot <= t) & (spot < SLOW - 1))
+            def _(way=way, spot=spot, chunk=chunk):
+                if t == 0:
+                    self.stage(way, t)[...] = own(chunk).astype(bf16)
+                else:
+
+                    @pl.when(spot == 0)
+                    def _():
+                        self.stage(way, t)[...] = own(chunk).astype(bf16)
+
+                    @pl.when(spot > 0)
+                    def _():
+                        self.stage(way, t)[...] = (own(chunk) + self.landed(way, t - 1)).astype(bf16)
+
+                self.copy(way, t).start()
+
+    def last(self, total):
+        for way in range(2):
+
+            @pl.when(self.place.spots[way] > 0)
+            def _(way=way):
+                total[...] += self.landed(way, SLOW - 2)
+
+    def drain(self):
+        for way in range(2):
+            for t in range(SLOW - 1):
+                spot = self.place.spots[way]
+
+                @pl.when((spot <= t) & (spot < SLOW - 1))
+                def _(way=way, t=t):
+                    self.copy(way, t).wait_send()
+
+
+class Spread:
+    def __init__(self, place, block, send_sem, recv_sem):
+        self.place, self.block, self.send_sem, self.recv_sem = place, block, send_sem, recv_sem
+
+    def copy(self, way, t, to):
+        chunk = self.place.mirrored(way, self.place.spots[way] - t)
+        block = self.block(chunk)
+        return remote(block, block, self.send_sem(way, t), self.recv_sem(way, t), self.place.along(to))
+
+    def step(self, t):
+        for way in range(2):
+            spot = self.place.spots[way]
+
+            @pl.when(spot >= t)
+            def _(way=way, spot=spot):
+                if t > 0:
+                    block = self.block(self.place.mirrored(way, spot - t))
+                    remote(
+                        block, block, self.send_sem(way, t - 1), self.recv_sem(way, t - 1), self.place.along(1 - way)
+                    ).wait_recv()
+                if t < SLOW - 1:
+
+                    @pl.when(spot < SLOW - 1)
+                    def _():
+                        self.copy(way, t, way).start()
+
+    def drain(self):
+        for way in range(2):
+            for t in range(SLOW - 1):
+                spot = self.place.spots[way]
+
+                @pl.when((spot >= t) & (spot < SLOW - 1))
+                def _(way=way, t=t):
+                    self.copy(way, t, way).wait_send()
+
+
+def units_of(rows, n_x, n_fast):
+    share = n_x * n_fast * SLOW * 16
+    return max(1, min(12, rows // share))
+
+
+def sum_kernel(
+    n_seq,
+    n_ray,
+    units,
+    beat,
+    g_ref,
+    lat_ref,
+    small_ref,
+    out_ref,
+    glat_ref,
+    small_out,
+    rc,
+    held,
+    rx,
+    z_stage,
+    z_recv,
+    z_total,
+    full,
+    lat_recv,
+    lat_own,
+    lz_stage,
+    lz_recv,
+    small_now,
+    small_recv,
+    core_sem,
+    halve_sem,
+    z_sem,
+    zg_sem,
+    double_sem,
+    core_back_sem,
+    out_sem,
+    lat_sem,
+    lz_sem,
+    small_sem,
+):
+    place = Place(n_seq, n_ray)
+    core_pair = ("seq", 1)
+    halvings = place.x_bits + place.fast_bits
+    exchanges = [core_pair] + halvings + place.slow_bits
+    greet(place, exchanges)
+
+    rows = g_ref.shape[1]
+    unit_rows = rows // units
+    core = place.core
+    sizes = [unit_rows >> i for i in range(len(halvings) + 1)]
+    share = sizes[-1]
+    line = share % (16 * SLOW) == 0
+    piece = share // SLOW if line else share
+
+    def base(u, stages):
+        start = u * unit_rows
+        for i in range(stages):
+            start = start + place.value(*halvings[i]) * sizes[i + 1]
+        return start
+
+    def unit(u):
+        return lane_rows(u * unit_rows, unit_rows)
+
+    def core_copy(u):
+        return remote(
+            g_ref.at[1 - core, unit(u)], rc.at[unit(u)], core_sem.at[0, u], core_sem.at[1, u], place.across(*core_pair)
+        )
+
+    def halve_copy(i, u):
+        size = sizes[i + 1]
+        sent = base(u, i) + (1 - place.value(*halvings[i])) * size
+        return remote(
+            held.at[lane_rows(sent, size)],
+            rx[i].at[lane_rows(u * size, size)],
+            halve_sem.at[0, i, u],
+            halve_sem.at[1, i, u],
+            place.across(*halvings[i]),
+        )
+
+    def start_core(u):
+        core_copy(u).start()
+
+    def join_core(u):
+        core_copy(u).wait()
+        held[unit(u), :] = (g_ref[core, unit(u), :].astype(f32) + rc[unit(u), :].astype(f32)).astype(bf16)
+        halve_copy(0, u).start()
+
+    def join_half(i):
+        def run(u):
+            size = sizes[i + 1]
+            halve_copy(i, u).wait()
+            kept = lane_rows(base(u, i + 1), size)
+            held[kept, :] = (held[kept, :].astype(f32) + rx[i][lane_rows(u * size, size), :].astype(f32)).astype(bf16)
+            if i + 1 < len(halvings):
+                halve_copy(i + 1, u).start()
+
+        return run
+
+    def z_line(u):
+        return Line(
+            place,
+            lambda way, t: z_stage.at[u, way, t],
+            lambda way, t: z_recv.at[u, way, t],
+            lambda way, t: z_sem.at[0, u, way, t],
+            lambda way, t: z_sem.at[1, u, way, t],
+        )
+
+    def z_rows(u, chunk):
+        return lane_rows(base(u, len(halvings)) + chunk * piece, piece)
+
+    def z_own(u):
+        return lambda chunk: held[z_rows(u, chunk), :].astype(f32)
+
+    def z_spread(u):
+        return Spread(
+            place,
+            lambda chunk: full.at[core, z_rows(u, chunk)],
+            lambda way, t: zg_sem.at[0, u, way, t],
+            lambda way, t: zg_sem.at[1, u, way, t],
+        )
+
+    def z_step(t):
+        return lambda u: z_line(u).step(t, z_own(u))
+
+    def z_finish(u):
+        z_total[...] = z_own(u)(place.slow)
+        z_line(u).last(z_total)
+        full[core, z_rows(u, place.slow), :] = z_total[...].astype(bf16)
+        z_spread(u).step(0)
+
+    def spread_step(t):
+        return lambda u: z_spread(u).step(t)
+
+    def whole_copy(i, u):
+        return remote(
+            held.at[lane_rows(base(u, len(halvings)), share)],
+            z_recv.at[u, 0, i],
+            z_sem.at[0, u, 0, i],
+            z_sem.at[1, u, 0, i],
+            place.across(*place.slow_bits[i]),
+        )
+
+    def whole_step(i):
+        def run(u):
+            mine = lane_rows(base(u, len(halvings)), share)
+            if i > 0:
+                whole_copy(i - 1, u).wait()
+                held[mine, :] = (held[mine, :].astype(f32) + z_recv[u, 0, i - 1].astype(f32)).astype(bf16)
+            if i < len(place.slow_bits):
+                whole_copy(i, u).start()
+            else:
+                full[core, mine, :] = held[mine, :]
+
+        return run
+
+    def double_copy(i, u):
+        block = full.at[core, lane_rows(base(u, i + 1), sizes[i + 1])]
+        return remote(block, block, double_sem.at[0, i, u], double_sem.at[1, i, u], place.across(*halvings[i]))
+
+    def core_back(u):
+        block = full.at[core, unit(u)]
+        return remote(block, block, core_back_sem.at[0, u], core_back_sem.at[1, u], place.across(*core_pair))
+
+    def out_copy(half, u):
+        return pltpu.make_async_copy(full.at[half, unit(u)], out_ref.at[half, unit(u)], out_sem.at[half, u])
+
+    def start_double(u):
+        double_copy(len(halvings) - 1, u).start()
+
+    def join_double(i):
+        def run(u):
+            double_copy(i, u).wait()
+            if i > 0:
+                double_copy(i - 1, u).start()
+            else:
+                core_back(u).start()
+                out_copy(core, u).start()
+
+        return run
+
+    def finish_unit(u):
+        core_back(u).wait()
+        out_copy(1 - core, u).start()
+        if line:
+            z_line(u).drain()
+            z_spread(u).drain()
+
+    stages = [[start_core], [join_core]] + [[join_half(i)] for i in range(len(halvings))]
+    if line:
+        stages[-1].append(z_step(0))
+        stages += [[z_step(t)] for t in range(1, SLOW - 1)]
+        stages += [[z_finish]] + [[spread_step(t)] for t in range(1, SLOW)]
+    else:
+        stages[-1].append(whole_step(0))
+        stages += [[whole_step(i)] for i in range(1, len(place.slow_bits) + 1)]
+    stages[-1].append(start_double)
+    stages += [[join_double(i)] for i in reversed(range(len(halvings)))]
+    stages += [[finish_unit]]
+
+    half_rows = lat_ref.shape[1] // 2
+    n_fast = place.n_fast
+    fast_sizes = [n_fast >> i for i in range(len(place.fast_bits) + 1)]
+
+    def chunk_of(k):
+        near = jnp.minimum(place.slow, SLOW - 1 - place.slow)
+        ahead = SLOW - 1 - near
+        chunk = jnp.where(k < ahead, SLOW - 1 - k, jnp.where(k - ahead < near, k - ahead, near))
+        return jnp.where(place.slow == near, chunk, SLOW - 1 - chunk)
+
+    def lat_base(i):
+        start = 0
+        for n in range(i):
+            start = start + place.value(*place.fast_bits[n]) * fast_sizes[n + 1]
+        return start
+
+    def lat_half(m):
+        return lane_rows((m % 2) * half_rows, half_rows)
+
+    def lat_copy(i, m):
+        size = fast_sizes[i + 1]
+        other = (1 - place.value(*place.fast_bits[i])) * size
+        if i == 0:
+            source = lat_ref.at[pl.ds(chunk_of(m // 2) * n_fast + other, size), lat_half(m)]
+        else:
+            source = lat_recv[i - 1].at[m, pl.ds(other, size)]
+        return remote(
+            source, lat_recv[i].at[m], lat_sem.at[0, i, m], lat_sem.at[1, i, m], place.across(*place.fast_bits[i])
+        )
+
+    def start_lat(m):
+        lat_copy(0, m).start()
+
+    def lat_line(m):
+        half = m % 2
+        return Line(
+            place,
+            lambda way, t: lz_stage.at[half, way, t],
+            lambda way, t: lz_recv.at[half, way, t],
+            lambda way, t: lz_sem.at[0, half, way, t],
+            lambda way, t: lz_sem.at[1, half, way, t],
+        )
+
+    def join_lat(i):
+        def run(m):
+            size = fast_sizes[i + 1]
+            lat_copy(i, m).wait()
+            mine = place.value(*place.fast_bits[i]) * size
+            if i == 0:
+                kept = lat_ref[pl.ds(chunk_of(m // 2) * n_fast + mine, size), lat_half(m), :]
+            else:
+                kept = lat_recv[i - 1][m, pl.ds(mine, size)]
+            joined = (kept.astype(f32) + lat_recv[i][m].astype(f32)).astype(bf16)
+            if i + 1 < len(place.fast_bits):
+                lat_recv[i][m] = joined
+                lat_copy(i + 1, m).start()
+            else:
+                lat_own[chunk_of(m // 2), m % 2] = joined[0]
+                walk_lat(m)
+
+        return run
+
+    def walk_lat(m):
+        half = m % 2
+
+        def own(chunk):
+            return lat_own[chunk, half].astype(f32)
+
+        for t in range(SLOW - 1):
+
+            @pl.when(m // 2 == t)
+            def _(t=t):
+                lat_line(m).step(t, own)
+
+    def finish_lat(m):
+        @pl.when(m // 2 == SLOW - 1)
+        def _():
+            mine = glat_ref.at[lat_half(m)]
+            mine[...] = lat_own[place.slow, m % 2].astype(f32)
+            lat_line(m).last(mine)
+            lat_line(m).drain()
+
+    lat_stages = [start_lat] + [join_lat(i) for i in range(len(place.fast_bits))] + [finish_lat]
+    lat_steps = 2 * SLOW
+
+    def small_copy(i):
+        axis, bit = exchanges[i]
+        return remote(
+            small_now.at[i], small_recv.at[i], small_sem.at[0, i], small_sem.at[1, i], place.across(axis, bit)
+        )
+
+    small_now[0] = small_ref[...]
+    small_copy(0).start()
+
+    lat_span = beat * (lat_steps - 1 + len(lat_stages) - 1) + 1
+    beats = max(units + len(stages) - 1, lat_span, len(exchanges) + 1)
+
+    def one_beat(now, carry):
+        for s in reversed(range(len(stages))):
+            u = now - s
+
+            @pl.when((u >= 0) & (u < units))
+            def _(u=u, s=s):
+                for run in stages[s]:
+                    run(u)
+
+        for s in reversed(range(len(lat_stages))):
+            ahead = now - beat * s
+            m = ahead // beat
+
+            @pl.when((ahead >= 0) & (ahead % beat == 0) & (m < lat_steps))
+            def _(m=m, s=s):
+                lat_stages[s](m)
+
+        for i in range(len(exchanges)):
+
+            @pl.when(now == i + 1)
+            def _(i=i):
+                small_copy(i).wait()
+                small_now[i + 1] = small_now[i] + small_recv[i]
+                if i + 1 < len(exchanges):
+                    small_copy(i + 1).start()
+
+        return carry
+
+    lax.fori_loop(0, beats, one_beat, 0)
+    small_out[...] = small_now[len(exchanges)]
+
+    def end_out(u, carry):
+        out_copy(0, u).wait()
+        out_copy(1, u).wait()
+        return carry
+
+    lax.fori_loop(0, units, end_out, 0)
+
+
+def sum_over_devices(n_seq, n_ray, grads, lat, small):
+    place_fast = n_ray // SLOW
+    rows, width = grads.shape[1:]
+    n_x = n_seq // 2
+    units = units_of(rows, n_x, place_fast)
+    halvings = len(bits_of(n_x)) + len(bits_of(place_fast))
+    fast_bits = len(bits_of(place_fast))
+    exchanges = 1 + halvings + len(bits_of(SLOW))
+    unit_rows = rows // units
+    share = unit_rows >> halvings
+    piece = share // SLOW if share % (16 * SLOW) == 0 else share
+    block = lat.shape[1]
+    half = block // 2
+    vmem = pltpu.VMEM
+    sem = pltpu.SemaphoreType.DMA
+    return pl.pallas_call(
+        functools.partial(sum_kernel, n_seq, n_ray, units, 2),
+        out_shape=(
+            jax.ShapeDtypeStruct((2, rows, width), bf16),
+            jax.ShapeDtypeStruct((block, width), f32),
+            jax.ShapeDtypeStruct(small.shape, f32),
+        ),
+        in_specs=[pl.BlockSpec(memory_space=vmem)] * 3,
+        out_specs=(pl.BlockSpec(memory_space=pl.ANY), pl.BlockSpec(memory_space=vmem), pl.BlockSpec(memory_space=vmem)),
+        scratch_shapes=[
+            vmem((rows, width), bf16),
+            vmem((rows, width), bf16),
+            [vmem((rows >> (i + 1), width), bf16) for i in range(halvings)],
+            vmem((units, 2, SLOW - 1, piece, width), bf16),
+            vmem((units, 2, SLOW - 1, piece, width), bf16),
+            vmem((piece, width), f32),
+            vmem((2, rows, width), bf16),
+            [vmem((2 * SLOW, place_fast >> (i + 1), half, width), bf16) for i in range(fast_bits)],
+            vmem((SLOW, 2, half, width), bf16),
+            vmem((2, 2, SLOW - 1, half, width), bf16),
+            vmem((2, 2, SLOW - 1, half, width), bf16),
+            vmem((exchanges + 1,) + small.shape, f32),
+            vmem((exchanges,) + small.shape, f32),
+            sem((2, units)),
+            sem((2, halvings, units)),
+            sem((2, units, 2, SLOW - 1)),
+            sem((2, units, 2, SLOW - 1)),
+            sem((2, halvings, units)),
+            sem((2, units)),
+            sem((2, units)),
+            sem((2, fast_bits, 2 * SLOW)),
+            sem((2, 2, 2, SLOW - 1)),
+            sem((2, exchanges)),
+        ],
+        compiler_params=pltpu.CompilerParams(collective_id=1, has_side_effects=True, vmem_limit_bytes=60 << 20),
+        name="sum_over_devices",
+    )(grads, lat, small)
 
 
 def local(
@@ -244,9 +791,6 @@
     grad_w_out = matmul(attended, grad_branch, 0, 0)
     grad_b_out = jnp.sum(grad_branch.astype(f32), axis=0)
     grad_attended = matmul(grad_branch, w_out, 1, 1).astype(bf16)
-    early = lax.psum(
-        tuple(g.astype(bf16) for g in (grad_w_out, grad_w_up, grad_w_down)), ("seq", "ray")
-    )
     g_sorted = matmul(order, grad_attended, 1, 0).astype(bf16)
 
     gq_sorted, grad_keys, grad_values = pl.pallas_call(
@@ -283,36 +827,41 @@
     grad_w_key = matmul(gathered, grad_keys, 0, 0)
     grad_w_value = matmul(gathered, grad_values, 0, 0)
     grad_b_value = jnp.sum(grad_values.astype(f32), axis=0)
-    grad_latents = lax.psum_scatter(
-        (matmul(grad_keys, w_key, 1, 1) + matmul(grad_values, w_value, 1, 1)).astype(bf16),
-        "ray",
-        scatter_dimension=0,
-        tiled=True,
-    ).astype(f32)
-    late = lax.psum(
-        tuple(g.astype(bf16) for g in (grad_w_query, grad_w_key, grad_w_value)), ("seq", "ray")
+    partial_latents = (matmul(grad_keys, w_key, 1, 1) + matmul(grad_values, w_value, 1, 1)).astype(bf16)
+    n_seq, n_ray = lax.axis_size("seq"), lax.axis_size("ray")
+    grads = jnp.stack(
+        [
+            jnp.concatenate([g.astype(bf16) for g in half], axis=0)
+            for half in (
+                (grad_w_query, grad_w_key, grad_w_up[:, :width], grad_w_down[:width]),
+                (grad_w_value, grad_w_out, grad_w_up[:, width:], grad_w_down[width:]),
+            )
+        ]
     )
-    rows = lax.psum(
-        (grad_gain, grad_bias, grad_b_query, grad_b_value, grad_b_out, grad_b_up, grad_b_down),
-        ("seq", "ray"),
+    small = jnp.stack(
+        [grad_gain, grad_bias, grad_b_query, grad_b_value, grad_b_out, grad_b_up[:width], grad_b_up[width:], grad_b_down]
     )
+    sums, grad_latents, rows = sum_over_devices(
+        n_seq, n_ray, grads, partial_latents.reshape(n_ray, latents.shape[0], width), small
+    )
+    pieces = sums.reshape(2, 4, width, width)
     return (
         result.astype(bf16),
         grad_rays,
         grad_latents,
         rows[0],
         rows[1],
-        late[0].astype(f32),
+        pieces[0, 0].astype(f32),
         rows[2],
-        late[1].astype(f32),
-        late[2].astype(f32),
+        pieces[0, 1].astype(f32),
+        pieces[1, 0].astype(f32),
         rows[3],
-        early[0].astype(f32),
+        pieces[1, 1].astype(f32),
         rows[4],
-        early[1].astype(f32),
-        rows[5],
-        early[2].astype(f32),
-        rows[6],
+        jnp.concatenate([pieces[0, 2], pieces[1, 2]], axis=1).astype(f32),
+        rows[5:7].reshape(-1),
+        jnp.concatenate([pieces[0, 3], pieces[1, 3]], axis=0).astype(f32),
+        rows[7],
     )
 
 

time: 619 us -> 536 us (0.87)
  waiting for transfers between devices: 283 us -> 69.4 us
  Pallas kernels: 116 us -> 303 us
  blocking collectives: 73.4 us -> 0 us
  other arithmetic: 26.2 us -> 40.9 us
    pallas_call x0 -> x1, Pallas kernels: none -> 169 us  [sum_over_devices(): pl.pallas_call(functools.partial(sum_kernel, n_seq, n_ray, units, 2), out...]
    psum x1 -> x0, waiting for transfers between devices: 127 us -> none  [local(): lax.psum(tuple((g.astype(bf16) for g in (grad_w_query, grad_w_key, grad_w...]
    reduce_scatter x1 -> x0, waiting for transfers between devices: 84.2 us -> none  [local(): lax.psum_scatter((matmul(grad_keys, w_key, 1, 1) + matmul(grad_values, w_...]
    psum x1 -> x0, blocking collectives: 73.4 us -> none  [local(): lax.psum((grad_gain, grad_bias, grad_b_query, grad_b_value, grad_b_out, g...]
    another operation x2 -> x4, other arithmetic: 1.01 us -> 13.3 us  [the longest x2 12.2 us: local(): jnp.stack([jnp.concatenate([g.astype(bf16) for g in half], axis=0) for ha...]
    pallas_call x1, Pallas kernels: 68.6 us -> 79.6 us  [local(): pl.pallas_call(functools.partial(attend_back_kernel, tiles), grid=(groups...]
    pallas_call x1, Pallas kernels: 47.2 us -> 55.1 us  [local(): pl.pallas_call(functools.partial(attend_kernel, tiles), grid=(groups,), o...]
    squeeze x0 -> x1, other arithmetic: none -> 7.36 us  [local(): pieces[0, 3]]
  transfers between devices with their start and end apart: 3 -> 1, of which waited for: 3 -> 1; matrix products, arithmetic and copies ran while one was open for 9% -> 3% of each run, Pallas kernels for 0% -> 0%
where the time goes in v2:
time: 536 us; the launch traced here: 531 us
  Pallas kernels  303 us (57%)
  matrix products  87.8 us (16%)
  waiting for transfers between devices  69.4 us (13%)
  other arithmetic  40.9 us (8%)
  between operations  14.9 us (3%)
  local copies, waits for them, and re-layouts  14.2 us (3%)
    pallas_call x1, Pallas kernels, sum_over_devices(): pl.pallas_call(functools.partial(sum_kernel, n_seq, n_ray, units, 2), out...  169 us
    dot_general x23, matrix products, matmul(): lax.dot_general(first_arg, second_arg, (((first_dim,), (second_dim,)), ((...  87.8 us
    pallas_call x1, Pallas kernels, local(): pl.pallas_call(functools.partial(attend_back_kernel, tiles), grid=(groups...  79.6 us
    all_gather x1, waiting for transfers between devices, local(): gathered = lax.all_gather(latents, 'ray', axis=0, tiled=True)  68.8 us
    pallas_call x1, Pallas kernels, local(): pl.pallas_call(functools.partial(attend_kernel, tiles), grid=(groups,), o...  55.1 us
    another operation x2, other arithmetic, local(): jnp.stack([jnp.concatenate([g.astype(bf16) for g in half], axis=0) for ha...  12.2 us
  transfers between devices with their start and end apart: 1, of which 1 were waited for; matrix products, arithmetic and copies ran while one was open for 3% of the time, Pallas kernels for 0%

profile of v2, /device:TPU:0, one launch (start us, length us, event | category | flops | bytes accessed | tf_op | source)
XLA Modules:
  0.0 530.8 jit_solution(6169349564521589877)
XLA Ops:
  7.3 0.7 all-gather.2.cloned.1.call-update
  7.9 0.9 reduce-window.9
  8.8 0.8 convert_reduce_fusion.6
  9.8 0.6 slice.73
  10.4 0.7 convert_element_type.164
  11.1 0.7 convert_element_type.162
  11.8 0.7 convert_element_type.161
  12.5 0.7 convert_element_type.168
  13.1 0.7 convert_element_type.172
  13.8 0.7 convert_element_type.174
  14.5 1.3 convert_element_type.176
  15.8 1.2 convert_reduce_fusion.3
  17.1 0.7 fusion.47
  17.8 0.7 pad_add_fusion.meta
  18.6 1.1 fusion.32
  19.6 1.3 convert_reduce_fusion.2
  21.2 2.9 multiply_convert_fusion.1.q_ref
  24.1 68.8 %all-gather.2.cloned.1.call-done = bf16[3072,768]{1,0:T(8,128)(2,1)} async-done(((bf16[384,768]{1,0:T(8,128)(2,1)}), bf16[3072,768]{1,0:T(8,128)(2,1)}) %all-gather.2.cloned.1.call-update) | async-done | bytes 4718608 | tf_op jit(solution)/shard_map/all_gather | solution.py:737
  92.8 8.9 %convolution_convert_fusion.1.k_ref = bf16[3072,768]{1,0:T(8,128)(2,1)} fusion(bf16[3072,768]{1,0:T(8,128)(2,1)} %all-gather.2.cloned.1.call-done, bf16[768,768]{1,0:T(8,128)(2,1)} %param.26), kind=kOutput, calls=%fused_computation.6 | convolution fusion | flops 3626237952 | bytes 10616832 | tf_op jit(solution)/shard_map/dot_general | solution.py:23
  101.7 5.8 %add_convert_fusion.2.vt_ref = bf16[768,3072]{1,0:T(8,128)(2,1)} fusion(bf16[768,768]{1,0:T(8,128)(2,1)S(1)} %copy-done.29, bf16[3072,768]{1,0:T(8,128)(2,1)S(1)} %copy-done.24, f32[768]{0:T(1024)S(1)} %convert_element_type.168), kind=kOutput, calls=%fused_computation.4 | convolution fusion | flops 3628597248 | bytes 10619904 | tf_op jit(solution)/shard_map/dot_general | solution.py:23
  107.5 55.1 %attend.1 = (f32[512,768]{1,0:T(8,128)S(1)}, f32[3,8,256]{2,1,0:T(8,128)S(1)}) custom-call(s32[17]{0:T(128)S(1)} %pad_add_fusion.meta, bf16[512,768]{1,0:T(8,128)(2,1)S(1)} %multiply_convert_fusion.1.q_ref, bf16[3072,768]{1,0:T(8,128)(2,1)} %convolution_convert_fusion.1.k_ref, bf16[768,3072]{1,0:T(8,128)(2,1)} %add_convert_fusion.2.vt_ref), custom_call_target="tpu_custom_call" | custom-call | tf_op jit(solution)/shard_map/attend/pallas_call | solution.py:761
  162.6 0.5 convolution_convert_fusion.11
  163.2 0.6 fusion.12
  163.8 1.2 copy-done.25
  165.1 1.1 convolution_add_fusion
  166.5 8.3 %convert_reduce_fusion.1 = (f32[1536]{0:T(1024)}, bf16[384,1536]{1,0:T(8,128)(2,1)S(1)}, f32[384,1536]{1,0:T(8,128)}) fusion(f32[384,1536]{1,0:T(8,128)S(1)} %convolution_add_fusion, bf16[384,768]{1,0:T(8,128)(2,1)S(1)} %copy-done.16, bf16[1536,768]{1,0:T(8,128)(2,1)S(1)} %copy-done), kind=kOutput, calls=%fused_computation.16 | convolution fusion | flops 949615104 | bytes 8853504 | tf_op jit(solution)/shard_map/dot_general | solution.py:23
  174.8 2.1 convert_add_fusion.1
  177.0 2.8 convolution_convert_fusion.3
  179.8 3.7 convolution_convert_fusion.8.g_ref
  183.5 8.9 %convolution_convert_fusion.kt_ref = bf16[768,3072]{1,0:T(8,128)(2,1)} fusion(bf16[768,768]{1,0:T(8,128)(2,1)} %param.26, bf16[3072,768]{1,0:T(8,128)(2,1)} %all-gather.2.cloned.1.call-done), kind=kOutput, calls=%fused_computation.5 | convolution fusion | flops 3626237952 | bytes 10616832 | tf_op jit(solution)/shard_map/dot_general | solution.py:23
  192.3 8.0 %add_convert_fusion.1.v_ref = bf16[3072,768]{1,0:T(8,128)(2,1)} fusion(bf16[3072,768]{1,0:T(8,128)(2,1)} %all-gather.2.cloned.1.call-done, bf16[768,768]{1,0:T(8,128)(2,1)S(1)} %copy-done.30, f32[768]{0:T(1024)S(1)} %convert_element_type.168), kind=kOutput, calls=%fused_computation.3 | convolution fusion | flops 3628597248 | bytes 10619904 | tf_op jit(solution)/shard_map/dot_general | solution.py:23
  200.3 79.6 %attend_back.1 = (bf16[512,768]{1,0:T(8,128)(2,1)S(1)}, bf16[3072,768]{1,0:T(8,128)(2,1)}, bf16[3072,768]{1,0:T(8,128)(2,1)}) custom-call(s32[17]{0:T(128)S(1)} %pad_add_fusion.meta, bf16[512,768]{1,0:T(8,128)(2,1)S(1)} %multiply_convert_fusion.1.q_ref, bf16[3072,768]{1,0:T(8,128)(2,1)} %convolution_convert_fusion.1.k_ref, ...), custom_call_target="tpu_custom_call" | custom-call | tf_op jit(solution)/shard_map/attend_back/pallas_call | solution.py:796
  280.0 0.5 convert_reduce_fusion.5
  280.5 0.9 fusion.24
  281.5 1.0 convolution_convert_fusion.7
  282.9 0.8 convolution_convert_fusion.4
  283.9 0.5 multiply_convert_fusion
  284.4 0.5 copy-done.17
  284.9 1.4 convolution_convert_fusion.2
  286.5 1.5 copy-done.9
  288.4 6.3 %fusion.60 = f32[3072,768]{1,0:T(8,128)} fusion(bf16[3072,768]{1,0:T(8,128)(2,1)S(1)} %bitcast.100, bf16[768,768]{1,0:T(8,128)(2,1)S(1)} %copy-done.28), kind=kOutput, calls=%fused_computation.140 | convolution fusion | flops 3623878656 | bytes 15335424 | tf_op jit(solution)/shard_map/dot_general | solution.py:23
  294.6 0.7 convert_reduce_fusion
  295.4 8.9 %add_convert_fusion = bf16[3072,768]{1,0:T(8,128)(2,1)} fusion(f32[3072,768]{1,0:T(8,128)} %fusion.60, bf16[3072,768]{1,0:T(8,128)(2,1)S(1)} %bitcast.94, bf16[768,768]{1,0:T(8,128)(2,1)} %param.27), kind=kOutput, calls=%fused_computation.2 | convolution fusion | flops 3628597248 | bytes 20054016 | tf_op jit(solution)/shard_map/dot_general | solution.py:23
  304.3 0.6 stack.40
  304.9 0.6 stack.41
  305.5 0.6 stack.42
  306.1 1.4 convert_reduce_fusion.4
  307.5 0.6 stack.43
  308.1 0.6 stack.44
  308.7 0.6 stack.45
  309.3 6.2 %fusion.13 = bf16[768,768]{1,0:T(8,128)(2,1)S(1)} fusion(bf16[3072,768]{1,0:T(8,128)(2,1)} %get-tuple-element.27, bf16[3072,768]{1,0:T(8,128)(2,1)S(1)} %bitcast.98), kind=kOutput, calls=%fused_computation.50 | convolution fusion | flops 3624468480 | bytes 10616832 | tf_op jit(solution)/shard_map/dot_general | solution.py:23
  315.5 4.0 fusion.14
  319.5 3.9 maximum_bitcast_fusion
  323.4 8.3 %pad_maximum_fusion.g_ref = bf16[2,3072,768]{2,1,0:T(8,128)(2,1)} fusion(bf16[1,3072,768]{2,1,0:T(8,128)(2,1)} %get-tuple-element.69, bf16[1,3072,768]{2,1,0:T(8,128)(2,1)} %get-tuple-element.68), kind=kLoop, calls=%fused_computation | loop fusion | flops 4718592 | bytes 18874368 | tf_op jit(solution)/shard_map/stack | solution.py:832
  331.7 1.4 stack.47.small_ref
  333.1 168.7 %sum_over_devices.1 = (bf16[2,3072,768]{2,1,0:T(8,128)(2,1)}, f32[384,768]{1,0:T(8,128)}, f32[8,768]{1,0:T(8,128)}) custom-call(bf16[2,3072,768]{2,1,0:T(8,128)(2,1)} %pad_maximum_fusion.g_ref, bf16[8,384,768]{2,1,0:T(8,128)(2,1)} %bitcast.95, f32[8,768]{1,0:T(8,128)} %stack.47.small_ref), custom_call_target="tpu_custom_call" | custom-call | tf_op jit(solution)/shard_map/sum_over_devices/pallas_call | solution.py:675
  501.9 1.6 slice_reduce_fusion
  503.5 0.7 slice.92
  504.2 3.2 fusion.16
  507.4 7.4 %slice_bitcast_fusion.1 = (bf16[768,768]{1,0:T(8,128)(2,1)S(1)}, bf16[768,768]{1,0:T(8,128)(2,1)}, bf16[768,768]{1,0:T(8,128)(2,1)}, bf16[768,768]{1,0:T(8,128)(...) fusion(bf16[2,4,768,768]{3,2,1,0:T(8,128)(2,1)} %bitcast.92), kind=kLoop, calls=%fused_computation.69 | loop fusion | flops 2359296 | bytes 23592960 | tf_op jit(solution)/shard_map/squeeze | solution.py:863
  514.8 0.6 reshape.180
  515.4 4.5 maximum_convert_fusion
  519.9 2.5 maximum_convert_fusion.1
  522.5 1.0 copy.35
  (92 shorter events, 2.3 us)
Async XLA Ops:
  7.2 159.0 %copy-start = (bf16[1536,768]{1,0:T(8,128)(2,1)S(1)}, bf16[1536,768]{1,0:T(8,128)(2,1)}, u32[]{:S(2)}) copy-start(bf16[1536,768]{1,0:T(8,128)(2,1)} %param.33) | copy-start | bytes 7077892
  7.2 13.7 %copy-start.4 = (bf16[384,768]{1,0:T(8,128)(2,1)S(1)}, bf16[384,768]{1,0:T(8,128)(2,1)}, u32[]{:S(2)}) copy-start(bf16[384,768]{1,0:T(8,128)(2,1)} %param.18) | copy-start | bytes 1769476
  7.2 85.6 %all-gather.2.cloned.1.call-start = ((), (), s32[]{:S(2)}) async-start(), calls=%async_computation | async-start | bytes 5308416 | tf_op jit(solution)/shard_map/all_gather | solution.py:737
  21.2 260.3 %copy-start.20 = (f32[384]{0:T(512)}, f32[384]{0:T(512)S(1)}, u32[]{:S(2)}) copy-start(f32[384]{0:T(512)S(1)} %add_rsqrt_fusion) | copy-start | bytes 4612
  92.8 8.9 %copy-start.24 = (bf16[3072,768]{1,0:T(8,128)(2,1)S(1)}, bf16[3072,768]{1,0:T(8,128)(2,1)}, u32[]{:S(2)}) copy-start(bf16[3072,768]{1,0:T(8,128)(2,1)} %all-gather.2.cloned.1.call-done) | copy-start | bytes 14155780
  92.8 8.9 %copy-start.29 = (bf16[768,768]{1,0:T(8,128)(2,1)S(1)}, bf16[768,768]{1,0:T(8,128)(2,1)}, u32[]{:S(2)}) copy-start(bf16[768,768]{1,0:T(8,128)(2,1)} %param.27) | copy-start | bytes 3538948
  107.5 55.6 %copy-start.5 = (bf16[384,768]{1,0:T(8,128)(2,1)S(1)}, bf16[384,768]{1,0:T(8,128)(2,1)}, u32[]{:S(2)}) copy-start(bf16[384,768]{1,0:T(8,128)(2,1)} %param.18) | copy-start | bytes 1769476
  107.5 55.6 %copy-start.26 = (bf16[768,768]{1,0:T(8,128)(2,1)S(1)}, bf16[768,768]{1,0:T(8,128)(2,1)}, u32[]{:S(2)}) copy-start(bf16[768,768]{1,0:T(8,128)(2,1)} %param.29) | copy-start | bytes 3538948
  162.6 1.2 copy-start.1
  163.2 3.0 copy-start.10
  163.2 1.9 copy-start.25
  165.1 11.9 %copy-start.31 = (f32[384,768]{1,0:T(8,128)}, f32[384,768]{1,0:T(8,128)S(1)}, u32[]{:S(2)}) copy-start(f32[384,768]{1,0:T(8,128)S(1)} %fusion.12) | copy-start | bytes 3538948
  165.1 1.5 copy-start.16
  166.5 8.3 %copy-start.12 = (f32[384,1536]{1,0:T(8,128)}, f32[384,1536]{1,0:T(8,128)S(1)}, u32[]{:S(2)}) copy-start(f32[384,1536]{1,0:T(8,128)S(1)} %convolution_add_fusion) | copy-start | bytes 7077892
  183.5 8.9 %copy-start.30 = (bf16[768,768]{1,0:T(8,128)(2,1)S(1)}, bf16[768,768]{1,0:T(8,128)(2,1)}, u32[]{:S(2)}) copy-start(bf16[768,768]{1,0:T(8,128)(2,1)} %param.27) | copy-start | bytes 3538948
  192.3 8.0 %copy-start.2 = (f32[512,768]{1,0:T(8,128)S(1)}, f32[512,768]{1,0:T(8,128)}, u32[]{:S(2)}) copy-start(f32[512,768]{1,0:T(8,128)} %copy-done.1) | copy-start | bytes 4718596
  192.3 8.0 %copy-start.3 = (bf16[512,768]{1,0:T(8,128)(2,1)S(1)}, bf16[512,768]{1,0:T(8,128)(2,1)}, u32[]{:S(2)}) copy-start(bf16[512,768]{1,0:T(8,128)(2,1)} %convolution_convert_fusion.8.g_ref) | copy-start | bytes 2359300
  200.3 80.2 %copy-start.6 = (bf16[384,768]{1,0:T(8,128)(2,1)S(1)}, bf16[384,768]{1,0:T(8,128)(2,1)}, u32[]{:S(2)}) copy-start(bf16[384,768]{1,0:T(8,128)(2,1)} %param.18) | copy-start | bytes 1769476
  200.3 80.2 %copy-start.27 = (bf16[768,768]{1,0:T(8,128)(2,1)S(1)}, bf16[768,768]{1,0:T(8,128)(2,1)}, u32[]{:S(2)}) copy-start(bf16[768,768]{1,0:T(8,128)(2,1)} %param.24) | copy-start | bytes 3538948
  280.5 3.2 copy-start.14
  281.5 1.3 copy-start.8
  281.5 1.4 copy-start.11
  281.5 2.3 copy-start.13
  283.8 1.1 copy-start.17
  283.8 4.3 slice-start.4
  284.9 3.3 slice-start.5
  286.3 1.7 copy-start.9
  286.4 2.0 copy-start.28
  288.0 6.6 %slice-start = ((s8[4718592]{0:T(1024)(128)(4,1)}), s8[4194304]{0:T(1024)(128)(4,1)S(1)}, s32[]{:S(2)}) async-start(s8[4718592]{0:T(1024)(128)(4,1)} %bitcast.93), calls=%async_computation.1 | async-start | bytes 8388608
  288.4 6.3 %slice-start.1 = ((s8[4718592]{0:T(1024)(128)(4,1)}), s8[524288]{0:T(1024)(128)(4,1)S(1)}, s32[]{:S(2)}) async-start(s8[4718592]{0:T(1024)(128)(4,1)} %bitcast.93), calls=%async_computation.2 | async-start | bytes 1048576
  294.6 14.6 %slice-start.2 = ((s8[4718592]{0:T(1024)(128)(4,1)}), s8[4194304]{0:T(1024)(128)(4,1)S(1)}, s32[]{:S(2)}) async-start(s8[4718592]{0:T(1024)(128)(4,1)} %bitcast.97), calls=%async_computation.3 | async-start | bytes 8388608
  295.3 10.7 %copy-start.21 = (f32[384]{0:T(512)S(1)}, f32[384]{0:T(512)}, u32[]{:S(2)}) copy-start(f32[384]{0:T(512)} %copy-done.20) | copy-start | bytes 4612
  295.4 13.9 %slice-start.3 = ((s8[4718592]{0:T(1024)(128)(4,1)}), s8[524288]{0:T(1024)(128)(4,1)S(1)}, s32[]{:S(2)}) async-start(s8[4718592]{0:T(1024)(128)(4,1)} %bitcast.97), calls=%async_computation.4 | async-start | bytes 1048576
  304.3 3.8 copy-start.22
  323.4 8.3 %copy-start.18 = (f32[1,768]{1,0:T(1,128)S(1)}, f32[1,768]{1,0:T(1,128)}, u32[]{:S(2)}) copy-start(f32[1,768]{1,0:T(1,128)} %stack.40) | copy-start | bytes 9220
  323.4 8.3 %copy-start.19 = (f32[1,768]{1,0:T(1,128)S(1)}, f32[1,768]{1,0:T(1,128)}, u32[]{:S(2)}) copy-start(f32[1,768]{1,0:T(1,128)} %stack.41) | copy-start | bytes 9220
  333.1 171.1 %copy-start.23 = (f32[768]{0:T(1024)S(1)}, f32[768]{0:T(1024)}, u32[]{:S(2)}) copy-start(f32[768]{0:T(1024)} %convert_element_type.176) | copy-start | bytes 9220
  515.4 4.6 copy-start.7
  519.9 2.5 copy-start.15
Sparse Core Ops, SparseCore 0:
  10.2 82.5 all-gather.1

commit v3 on v2

--- a/solution.py
+++ b/solution.py
@@ -12,7 +12,7 @@
 TILE = 64
 WIDE = 256
 PACK = WIDE // HEAD
-CHUNK = 256
+CHUNK = 512
 
 masked_score = -1e30
 f32 = jnp.float32
@@ -60,108 +60,178 @@
     return pl.ds(pl.multiple_of(chunk * CHUNK, CHUNK), CHUNK)
 
 
-def attend_kernel(tiles, meta, q_ref, k_ref, vt_ref, att_ref, lse_ref, s_ref):
+def group_at(g):
+    return slice(g * WIDE, (g + 1) * WIDE)
+
+
+def attend_kernel(counts, lengths, q_ref, k_ref, vt_ref, att_ref, lse_ref, s_ref, mixed_ref):
+    groups = q_ref.shape[1] // WIDE
+    used_tiles, bounds = scene_tiles(counts, lengths)
     att_ref[...] = jnp.zeros_like(att_ref)
     lse_ref[...] = jnp.zeros_like(lse_ref)
 
     def one_tile(t, carry):
-        start, end = meta[1 + t], meta[1 + tiles + t]
+        start, end = bounds(t)
         first, last = start // CHUNK, (end + CHUNK - 1) // CHUNK
         ray_rows = pl.ds(pl.multiple_of(t * TILE, TILE), TILE)
-        spread = spread_heads(q_ref[ray_rows, :])
-
-        def score(j, top):
-            s = matmul(k_ref[chunk_at(j), :], spread, 1, 1)
-            s = jnp.where(in_scene(j, start, end), s, masked_score)
-            s_ref[chunk_at(j), :] = s
-            return jnp.maximum(top, fold_rows(s, jnp.max))
-
-        top = lax.fori_loop(first, last, score, jnp.full((8, WIDE), masked_score, f32))
-        top = jnp.max(top, axis=0, keepdims=True)
-
-        def expo(j, total):
-            e = jnp.exp(s_ref[chunk_at(j), :] - top)
-            s_ref[chunk_at(j), :] = e
-            return total + fold_rows(e, jnp.sum)
-
-        total = lax.fori_loop(first, last, expo, jnp.zeros((8, WIDE), f32))
-        total = jnp.sum(total, axis=0, keepdims=True)
-        rest = 1.0 / total
-
-        def mix(j, mixed):
-            w = (s_ref[chunk_at(j), :] * rest).astype(bf16)
-            return mixed + matmul(vt_ref[:, chunk_at(j)], w, 1, 0)
-
-        mixed = lax.fori_loop(first, last, mix, jnp.zeros((WIDE, WIDE), f32))
-        att_ref[ray_rows, :] = fold_heads(mixed.T)
-        lse_ref[0, pl.ds(t, 1), :] = top + jnp.log(total)
+        spread = [spread_heads(q_ref[ray_rows, group_at(g)]) for g in range(groups)]
+
+        def score(j, tops):
+            seen = in_scene(j, start, end)
+            new = []
+            for g in range(groups):
+                s = matmul(k_ref[chunk_at(j), group_at(g)], spread[g], 1, 1)
+                s = jnp.where(seen, s, masked_score)
+                s_ref[g, chunk_at(j), :] = s
+                new.append(jnp.maximum(tops[g], fold_rows(s, jnp.max)))
+            return tuple(new)
+
+        tops = lax.fori_loop(first, last, score, (jnp.full((8, WIDE), masked_score, f32),) * groups)
+        tops = [jnp.max(top, axis=0, keepdims=True) for top in tops]
+
+        def expo(j, totals):
+            new = []
+            for g in range(groups):
+                e = jnp.exp(s_ref[g, chunk_at(j), :] - tops[g])
+                s_ref[g, chunk_at(j), :] = e
+                new.append(totals[g] + fold_rows(e, jnp.sum))
+            return tuple(new)
+
+        totals = lax.fori_loop(first, last, expo, (jnp.zeros((8, WIDE), f32),) * groups)
+        totals = [jnp.sum(total, axis=0, keepdims=True) for total in totals]
+        rests = [1.0 / total for total in totals]
+
+        def mix(j, carry):
+            for g in range(groups):
+                w = (s_ref[g, chunk_at(j), :] * rests[g]).astype(bf16)
+                mixed_ref[g] += matmul(vt_ref[group_at(g), chunk_at(j)], w, 1, 0)
+            return carry
+
+        mixed_ref[...] = jnp.zeros_like(mixed_ref)
+        lax.fori_loop(first, last, mix, 0)
+        for g in range(groups):
+            att_ref[ray_rows, group_at(g)] = fold_heads(mixed_ref[g].T)
+            lse_ref[pl.ds(t, 1), group_at(g)] = tops[g] + jnp.log(totals[g])
         return carry
 
-    lax.fori_loop(0, meta[0], one_tile, 0)
-
-
-def attend_back_kernel(tiles, meta, q_ref, k_ref, kt_ref, v_ref, g_ref, att_ref, lse_ref, gq_ref, gk_ref, gv_ref, gk_sum, gv_sum, gqt_sum):
+    lax.fori_loop(0, used_tiles, one_tile, 0)
+
+
+def attend_back_kernel(counts, lengths, q_ref, k_ref, kt_ref, v_ref, g_ref, att_ref, lse_ref, gq_ref, gk_ref, gv_ref, gk_sum, gv_sum, gqt_sum):
+    groups = q_ref.shape[1] // WIDE
+    used_tiles, bounds = scene_tiles(counts, lengths)
     gq_ref[...] = jnp.zeros_like(gq_ref)
     gk_sum[...] = jnp.zeros_like(gk_sum)
     gv_sum[...] = jnp.zeros_like(gv_sum)
 
     def one_tile(t, carry):
-        start, end = meta[1 + t], meta[1 + tiles + t]
+        start, end = bounds(t)
         first, last = start // CHUNK, (end + CHUNK - 1) // CHUNK
         ray_rows = pl.ds(pl.multiple_of(t * TILE, TILE), TILE)
-        q_spread = spread_heads(q_ref[ray_rows, :])
-        g_tile = g_ref[ray_rows, :]
-        g_spread = spread_heads(g_tile)
-        product = spread_heads(g_tile.astype(f32) * att_ref[ray_rows, :])
-        dots = lax.dot_general(
-            jnp.ones((8, WIDE), f32),
-            product,
-            (((1,), (1,)), ((), ())),
-            precision=lax.Precision.HIGHEST,
-            preferred_element_type=f32,
-        )[0:1, :]
-        lse = lse_ref[0, pl.ds(t, 1), :]
+        q_spread, g_spread, dots, lse = [], [], [], []
+        for g in range(groups):
+            q_spread.append(spread_heads(q_ref[ray_rows, group_at(g)]))
+            g_tile = g_ref[ray_rows, group_at(g)]
+            g_spread.append(spread_heads(g_tile))
+            product = spread_heads(g_tile.astype(f32) * att_ref[ray_rows, group_at(g)])
+            dots.append(
+                lax.dot_general(
+                    jnp.ones((8, WIDE), f32),
+                    product,
+                    (((1,), (1,)), ((), ())),
+                    precision=lax.Precision.HIGHEST,
+                    preferred_element_type=f32,
+                )[0:1, :]
+            )
+            lse.append(lse_ref[pl.ds(t, 1), group_at(g)])
         gqt_sum[...] = jnp.zeros_like(gqt_sum)
 
         def step(j, carry):
             at = chunk_at(j)
-            s = matmul(k_ref[at, :], q_spread, 1, 1)
-            p = jnp.where(in_scene(j, start, end), jnp.exp(s - lse), 0.0)
-            gv_sum[at, :] += matmul(p.astype(bf16), g_spread, 1, 0)
-            gp = matmul(v_ref[at, :], g_spread, 1, 1)
-            gs = (p * (gp - dots)).astype(bf16)
-            gk_sum[at, :] += matmul(gs, q_spread, 1, 0)
-            gqt_sum[...] += matmul(kt_ref[:, at], gs, 1, 0)
+            seen = in_scene(j, start, end)
+            for g in range(groups):
+                to = group_at(g)
+                s = matmul(k_ref[at, to], q_spread[g], 1, 1)
+                p = jnp.where(seen, jnp.exp(s - lse[g]), 0.0)
+                gv_sum[at, to] += matmul(p.astype(bf16), g_spread[g], 1, 0)
+                gp = matmul(v_ref[at, to], g_spread[g], 1, 1)
+                gs = (p * (gp - dots[g])).astype(bf16)
+                gk_sum[at, to] += matmul(gs, q_spread[g], 1, 0)
+                gqt_sum[g] += matmul(kt_ref[to, at], gs, 1, 0)
             return carry
 
         lax.fori_loop(first, last, step, 0)
-        gq_ref[ray_rows, :] = (fold_heads(gqt_sum[...].T) * HEAD ** (-0.5)).astype(bf16)
+        for g in range(groups):
+            gq_ref[ray_rows, group_at(g)] = (fold_heads(gqt_sum[g].T) * HEAD ** (-0.5)).astype(bf16)
         return carry
 
-    lax.fori_loop(0, meta[0], one_tile, 0)
+    lax.fori_loop(0, used_tiles, one_tile, 0)
     gk_ref[...] = gk_sum[...].astype(bf16)
     gv_ref[...] = gv_sum[...].astype(bf16)
 
 
-def scene_plan(lengths, scenes, rays):
-    tiles = rays // TILE + lengths.shape[0] - 1
-    kinds = jnp.arange(lengths.shape[0], dtype=jnp.int32)
-    one_hot = scenes[:, None] == kinds[None, :]
-    before = jnp.tril(jnp.ones((rays, rays), bf16), -1)
-    rank = matmul(before, one_hot.astype(bf16), 1, 0).astype(jnp.int32)
-    counts = jnp.sum(one_hot.astype(jnp.int32), axis=0)
-    scene_tiles = (counts + TILE - 1) // TILE
-    tile_ends = jnp.cumsum(scene_tiles)
-    first_slot = (tile_ends - scene_tiles) * TILE
-    slot = jnp.sum(jnp.where(one_hot, rank + first_slot[None, :], 0), axis=1)
-    order = (jnp.arange(tiles * TILE, dtype=jnp.int32)[:, None] == slot[None, :]).astype(bf16)
-    ends = jnp.cumsum(lengths)
-    tile_scene = jnp.sum(jnp.arange(tiles, dtype=jnp.int32)[:, None] >= tile_ends[None, :], axis=1)
-    pick = tile_scene[:, None] == kinds[None, :]
-    tile_start = jnp.sum(jnp.where(pick, (ends - lengths)[None, :], 0), axis=1)
-    tile_end = jnp.sum(jnp.where(pick, ends[None, :], 0), axis=1)
-    meta = jnp.concatenate([tile_ends[-1:], tile_start, tile_end]).astype(jnp.int32)
-    return tiles, order, meta
+def attend(counts, lengths, q_sorted, keys, values_t):
+    slots, width = q_sorted.shape
+    key_total = keys.shape[0]
+    vmem = pl.BlockSpec(memory_space=pltpu.VMEM)
+    return pl.pallas_call(
+        attend_kernel,
+        out_shape=(
+            jax.ShapeDtypeStruct((slots, width), f32),
+            jax.ShapeDtypeStruct((slots // TILE, width), f32),
+        ),
+        in_specs=[pl.BlockSpec(memory_space=pltpu.SMEM)] * 2 + [vmem] * 3,
+        out_specs=(vmem, vmem),
+        scratch_shapes=[
+            pltpu.VMEM((width // WIDE, key_total, WIDE), f32),
+            pltpu.VMEM((width // WIDE, WIDE, WIDE), f32),
+        ],
+        compiler_params=pltpu.CompilerParams(vmem_limit_bytes=56 << 20),
+        name="attend",
+    )(counts, lengths, q_sorted, keys, values_t)
+
+
+def attend_back(counts, lengths, q_sorted, keys, keys_t, values, g_sorted, att_sorted, lse):
+    slots, width = q_sorted.shape
+    key_total = keys.shape[0]
+    vmem = pl.BlockSpec(memory_space=pltpu.VMEM)
+    return pl.pallas_call(
+        attend_back_kernel,
+        out_shape=(
+            jax.ShapeDtypeStruct((slots, width), bf16),
+            jax.ShapeDtypeStruct((key_total, width), bf16),
+            jax.ShapeDtypeStruct((key_total, width), bf16),
+        ),
+        in_specs=[pl.BlockSpec(memory_space=pltpu.SMEM)] * 2 + [vmem] * 7,
+        out_specs=(vmem,) * 3,
+        scratch_shapes=[
+            pltpu.VMEM((key_total, width), f32),
+            pltpu.VMEM((key_total, width), f32),
+            pltpu.VMEM((width // WIDE, WIDE, WIDE), f32),
+        ],
+        compiler_params=pltpu.CompilerParams(vmem_limit_bytes=60 << 20),
+        name="attend_back",
+    )(counts, lengths, q_sorted, keys, keys_t, values, g_sorted, att_sorted, lse)
+
+
+def scene_tiles(counts, lengths):
+    kinds = lengths.shape[1]
+    tile_ends, scene_ends, tiles, latents = [], [], 0, 0
+    for c in range(kinds):
+        tiles = tiles + (counts[c, 0] + TILE - 1) // TILE
+        latents = latents + lengths[0, c]
+        tile_ends.append(tiles)
+        scene_ends.append(latents)
+
+    def bounds(t):
+        start, end = 0, scene_ends[0]
+        for c in range(1, kinds):
+            later = t >= tile_ends[c - 1]
+            start = jnp.where(later, scene_ends[c - 1], start)
+            end = jnp.where(later, scene_ends[c], end)
+        return start, end
+
+    return tiles, bounds
 
 
 MESH = pl.DeviceIdType.MESH
@@ -518,7 +588,9 @@
         stages[-1].append(whole_step(0))
         stages += [[whole_step(i)] for i in range(1, len(place.slow_bits) + 1)]
     stages[-1].append(start_double)
+    stages.insert(2, [])
     stages += [[join_double(i)] for i in reversed(range(len(halvings)))]
+    stages.insert(-1, [])
     stages += [[finish_unit]]
 
     half_rows = lat_ref.shape[1] // 2
@@ -619,7 +691,7 @@
     beats = max(units + len(stages) - 1, lat_span, len(exchanges) + 1)
 
     def one_beat(now, carry):
-        for s in reversed(range(len(stages))):
+        for s in range(len(stages)):
             u = now - s
 
             @pl.when((u >= 0) & (u < units))
@@ -627,7 +699,7 @@
                 for run in stages[s]:
                     run(u)
 
-        for s in reversed(range(len(lat_stages))):
+        for s in range(len(lat_stages)):
             ahead = now - beat * s
             m = ahead // beat
 
@@ -673,7 +745,7 @@
     vmem = pltpu.VMEM
     sem = pltpu.SemaphoreType.DMA
     return pl.pallas_call(
-        functools.partial(sum_kernel, n_seq, n_ray, units, 2),
+        functools.partial(sum_kernel, n_seq, n_ray, units, 3),
         out_shape=(
             jax.ShapeDtypeStruct((2, rows, width), bf16),
             jax.ShapeDtypeStruct((block, width), f32),
@@ -711,6 +783,201 @@
     )(grads, lat, small)
 
 
+def gather_kernel(
+    n_seq,
+    n_ray,
+    kinds,
+    rays_ref,
+    lat_ref,
+    scenes_ref,
+    rows_ref,
+    wq_ref,
+    wk_ref,
+    wv_ref,
+    all_ref,
+    k_ref,
+    kt_ref,
+    v_ref,
+    vt_ref,
+    qs_ref,
+    order_ref,
+    shifted_ref,
+    counts_ref,
+    full,
+    k_own,
+    kt_own,
+    v_own,
+    vt_own,
+    z_sem,
+    y_sem,
+    out_sem,
+):
+    place = Place(n_seq, n_ray)
+    fast_bits = place.fast_bits[::-1]
+    greet(place, place.fast_bits)
+    block, width = lat_ref.shape
+    half_rows = block // 2
+    group = place.n_fast * block
+    full[place.slow, place.fast] = lat_ref[...]
+
+    def half_at(half):
+        return pl.ds(half * half_rows, half_rows)
+
+    def spread(half):
+        return Spread(
+            place,
+            lambda chunk: full.at[chunk, place.fast, half_at(half)],
+            lambda way, t: z_sem.at[0, half, way, t],
+            lambda way, t: z_sem.at[1, half, way, t],
+        )
+
+    def fast_copy(i, chunk, half):
+        axis, bit = fast_bits[i]
+        mine = full.at[chunk, pl.ds(place.fast // bit * bit, bit), half_at(half)]
+        return remote(mine, mine, y_sem.at[0, i, chunk, half], y_sem.at[1, i, chunk, half], place.across(axis, bit))
+
+    def chunk_of(way, t):
+        return place.mirrored(way, place.spots[way] - t)
+
+    for half in range(2):
+        fast_copy(0, place.slow, half).start()
+        spread(half).step(0)
+
+    inputs = rays_ref[...].astype(f32)
+    centred = inputs - jnp.mean(inputs, axis=1, keepdims=True)
+    inverse = lax.rsqrt(jnp.mean(centred * centred, axis=1, keepdims=True) + 1e-05)
+    shifted = (centred * inverse * rows_ref[0:1, :] + rows_ref[1:2, :]).astype(bf16)
+    shifted_ref[...] = shifted
+    queries = (matmul(shifted, wq_ref[...], 1, 0) + rows_ref[2:3, :]).astype(bf16)
+    n_rays = rays_ref.shape[0]
+    slots = order_ref.shape[0]
+    scenes = scenes_ref[...]
+    same = scenes == lax.broadcasted_iota(jnp.int32, (8, n_rays), 0)
+    one_hot = same.astype(f32)
+    before = (
+        lax.broadcasted_iota(jnp.int32, (n_rays, n_rays), 0) < lax.broadcasted_iota(jnp.int32, (n_rays, n_rays), 1)
+    ).astype(bf16)
+    rank = matmul(one_hot.astype(bf16), before, 1, 0)
+    counts = jnp.sum(one_hot, axis=1, keepdims=True)
+    counts_ref[...] = jnp.broadcast_to(counts, counts_ref.shape).astype(jnp.int32)
+    scene_tiles = jnp.floor((counts + (TILE - 1)) * (1.0 / TILE))
+    slot = jnp.zeros((1, n_rays), f32)
+    first = jnp.zeros((1, 1), f32)
+    for c in range(kinds):
+        slot = slot + jnp.where(same[c : c + 1, :], rank[c : c + 1, :] + first, 0.0)
+        first = first + scene_tiles[c : c + 1, :] * TILE
+    order = (lax.broadcasted_iota(jnp.int32, (slots, n_rays), 0) == slot.astype(jnp.int32)).astype(f32).astype(bf16)
+    order_ref[...] = order
+    qs_ref[...] = (matmul(order, queries, 1, 0) * HEAD ** (-0.5)).astype(bf16)
+
+    def results(chunk):
+        rows = pl.ds(pl.multiple_of(chunk * group, 16), group)
+        columns = pl.ds(pl.multiple_of(chunk * group, 128), group)
+        return [
+            (k_own.at[chunk], k_ref.at[rows]),
+            (kt_own.at[chunk], kt_ref.at[:, columns]),
+            (v_own.at[chunk], v_ref.at[rows]),
+            (vt_own.at[chunk], vt_ref.at[:, columns]),
+        ] + [
+            (full.at[chunk, f], all_ref.at[pl.ds(pl.multiple_of(chunk * group + f * block, 16), block)])
+            for f in range(place.n_fast)
+        ]
+
+    def project(chunk):
+        for half in range(2):
+            for i in range(len(fast_bits)):
+                fast_copy(i, chunk, half).wait()
+                if i + 1 < len(fast_bits):
+                    fast_copy(i + 1, chunk, half).start()
+        latents = full[chunk].reshape(group, width)
+        keys = matmul(latents, wk_ref[...], 1, 0).astype(bf16)
+        k_own[chunk] = keys
+        kt_own[chunk] = keys.T
+        values = (matmul(latents, wv_ref[...], 1, 0) + rows_ref[3:4, :]).astype(bf16)
+        v_own[chunk] = values
+        vt_own[chunk] = values.T
+        for n, (source, target) in enumerate(results(chunk)):
+            pltpu.make_async_copy(source, target, out_sem.at[n, chunk]).start()
+
+    def visit(index, carry):
+        t, way = index // 2, index % 2
+        for later in range(1, SLOW):
+
+            @pl.when(index == 2 * (later - 1))
+            def _(later=later):
+                for half in range(2):
+                    spread(half).step(later)
+                    for to in range(2):
+
+                        @pl.when(place.spots[to] >= later)
+                        def _(half=half, to=to):
+                            fast_copy(0, chunk_of(to, later), half).start()
+
+        spot = jnp.where(way == 0, place.slow, SLOW - 1 - place.slow)
+        chunk = jnp.where(way == 0, spot - t, SLOW - 1 - spot + t)
+
+        @pl.when((spot >= t) & (index != 1))
+        def _():
+            project(chunk)
+
+        return carry
+
+    lax.fori_loop(0, 2 * SLOW, visit, 0)
+
+    def end(chunk, carry):
+        for n, (source, target) in enumerate(results(chunk)):
+            pltpu.make_async_copy(source, target, out_sem.at[n, chunk]).wait()
+        return carry
+
+    lax.fori_loop(0, SLOW, end, 0)
+    for half in range(2):
+        spread(half).drain()
+
+
+def gather_and_project(n_seq, n_ray, kinds, rays, latents, scenes, rows, w_query, w_key, w_value):
+    block, width = latents.shape
+    n_rays = rays.shape[0]
+    n_fast = n_ray // SLOW
+    group = n_fast * block
+    total = n_ray * block
+    tiles = n_rays // TILE + kinds - 1
+    fast_bits = len(bits_of(n_fast))
+    vmem = pltpu.VMEM
+    sem = pltpu.SemaphoreType.DMA
+    in_vmem = pl.BlockSpec(memory_space=vmem)
+    anywhere = pl.BlockSpec(memory_space=pl.ANY)
+    tall = jax.ShapeDtypeStruct((total, width), bf16)
+    wide = jax.ShapeDtypeStruct((width, total), bf16)
+    return pl.pallas_call(
+        functools.partial(gather_kernel, n_seq, n_ray, kinds),
+        out_shape=(
+            tall,
+            tall,
+            wide,
+            tall,
+            wide,
+            jax.ShapeDtypeStruct((tiles * TILE, width), bf16),
+            jax.ShapeDtypeStruct((tiles * TILE, n_rays), bf16),
+            jax.ShapeDtypeStruct((n_rays, width), bf16),
+            jax.ShapeDtypeStruct((8, 128), jnp.int32),
+        ),
+        in_specs=[in_vmem] * 7,
+        out_specs=(anywhere,) * 5 + (in_vmem,) * 4,
+        scratch_shapes=[
+            vmem((SLOW, n_fast, block, width), bf16),
+            vmem((SLOW, group, width), bf16),
+            vmem((SLOW, width, group), bf16),
+            vmem((SLOW, group, width), bf16),
+            vmem((SLOW, width, group), bf16),
+            sem((2, 2, 2, SLOW - 1)),
+            sem((2, fast_bits, SLOW, 2)),
+            sem((4 + n_fast, SLOW)),
+        ],
+        compiler_params=pltpu.CompilerParams(collective_id=0, has_side_effects=True, vmem_limit_bytes=48 << 20),
+        name="gather_and_project",
+    )(rays, latents, scenes, rows, w_query, w_key, w_value)
+
+
 def local(
     rays,
     latents,
@@ -731,46 +998,28 @@
     b_down,
     cotangent,
 ):
-    scale = HEAD ** (-0.5)
     width = rays.shape[1]
-    groups = width // WIDE
-    gathered = lax.all_gather(latents, "ray", axis=0, tiled=True)
-    key_total = gathered.shape[0]
-    tiles, order, meta = scene_plan(lengths[0], scenes, rays.shape[0])
-    slots = tiles * TILE
+    n_seq, n_ray = lax.axis_size("seq"), lax.axis_size("ray")
+    vectors = (ln_gain, ln_bias, b_query, b_value)
+    gathered, keys, keys_t, values, values_t, q_sorted, order, shifted, counts = gather_and_project(
+        n_seq,
+        n_ray,
+        lengths.shape[1],
+        rays,
+        latents,
+        scenes.reshape(1, -1),
+        jnp.concatenate([v.reshape(1, width) for v in vectors] * 2).astype(f32),
+        w_query,
+        w_key,
+        w_value,
+    )
     inputs = rays.astype(f32)
     row_mean = jnp.mean(inputs, axis=1, keepdims=True)
     centred = inputs - row_mean
     inverse = lax.rsqrt(jnp.mean(centred * centred, axis=1, keepdims=True) + 1e-05)
     normed = centred * inverse
     gain_full = ln_gain.astype(f32)
-    shifted = (normed * gain_full + ln_bias.astype(f32)).astype(bf16)
-    queries = (matmul(shifted, w_query, 1, 0) + b_query.astype(f32)).astype(bf16)
-    q_sorted = (matmul(order, queries, 1, 0) * scale).astype(bf16)
-    keys = matmul(gathered, w_key, 1, 0).astype(bf16)
-    keys_t = matmul(w_key, gathered, 0, 1).astype(bf16)
-    values = (matmul(gathered, w_value, 1, 0) + b_value.astype(f32)).astype(bf16)
-    values_t = (matmul(w_value, gathered, 0, 1) + b_value.astype(f32)[:, None]).astype(bf16)
-
-    smem = pl.BlockSpec(memory_space=pltpu.SMEM)
-    slot_spec = pl.BlockSpec((slots, WIDE), lambda g: (0, g))
-    key_spec = pl.BlockSpec((key_total, WIDE), lambda g: (0, g))
-    turned_spec = pl.BlockSpec((WIDE, key_total), lambda g: (g, 0))
-    lse_spec = pl.BlockSpec((1, tiles, WIDE), lambda g: (g, 0, 0))
-    params = pltpu.CompilerParams(vmem_limit_bytes=48 << 20)
-    att_sorted, lse = pl.pallas_call(
-        functools.partial(attend_kernel, tiles),
-        grid=(groups,),
-        out_shape=(
-            jax.ShapeDtypeStruct((slots, width), f32),
-            jax.ShapeDtypeStruct((groups, tiles, WIDE), f32),
-        ),
-        in_specs=[smem, slot_spec, key_spec, turned_spec],
-        out_specs=(slot_spec, lse_spec),
-        scratch_shapes=[pltpu.VMEM((key_total, WIDE), f32)],
-        compiler_params=params,
-        name="attend",
-    )(meta, q_sorted, keys, values_t)
+    att_sorted, lse = attend(counts, lengths, q_sorted, keys, values_t)
     attended = matmul(order, att_sorted.astype(bf16), 0, 0).astype(bf16)
 
     hidden = inputs + matmul(attended, w_out, 1, 0) + b_out.astype(f32)
@@ -793,24 +1042,9 @@
     grad_attended = matmul(grad_branch, w_out, 1, 1).astype(bf16)
     g_sorted = matmul(order, grad_attended, 1, 0).astype(bf16)
 
-    gq_sorted, grad_keys, grad_values = pl.pallas_call(
-        functools.partial(attend_back_kernel, tiles),
-        grid=(groups,),
-        out_shape=(
-            jax.ShapeDtypeStruct((slots, width), bf16),
-            jax.ShapeDtypeStruct((key_total, width), bf16),
-            jax.ShapeDtypeStruct((key_total, width), bf16),
-        ),
-        in_specs=[smem, slot_spec, key_spec, turned_spec, key_spec, slot_spec, slot_spec, lse_spec],
-        out_specs=(slot_spec, key_spec, key_spec),
-        scratch_shapes=[
-            pltpu.VMEM((key_total, WIDE), f32),
-            pltpu.VMEM((key_total, WIDE), f32),
-            pltpu.VMEM((WIDE, WIDE), f32),
-        ],
-        compiler_params=params,
-        name="attend_back",
-    )(meta, q_sorted, keys, keys_t, values, g_sorted, att_sorted, lse)
+    gq_sorted, grad_keys, grad_values = attend_back(
+        counts, lengths, q_sorted, keys, keys_t, values, g_sorted, att_sorted, lse
+    )
     grad_queries = matmul(order, gq_sorted, 0, 0).astype(bf16)
 
     grad_w_query = matmul(shifted, grad_queries, 0, 0)
@@ -828,7 +1062,6 @@
     grad_w_value = matmul(gathered, grad_values, 0, 0)
     grad_b_value = jnp.sum(grad_values.astype(f32), axis=0)
     partial_latents = (matmul(grad_keys, w_key, 1, 1) + matmul(grad_values, w_value, 1, 1)).astype(bf16)
-    n_seq, n_ray = lax.axis_size("seq"), lax.axis_size("ray")
     grads = jnp.stack(
         [
             jnp.concatenate([g.astype(bf16) for g in half], axis=0)

time: 536 us -> 376 us (0.70)
  waiting for transfers between devices: 69.4 us -> 0 us
  matrix products: 87.8 us -> 45 us
  Pallas kernels: 303 us -> 276 us
  between operations: 14.9 us -> 1.63 us
  other arithmetic: 40.9 us -> 29.8 us
  local copies, waits for them, and re-layouts: 14.2 us -> 19.6 us
    all_gather x1 -> x0, waiting for transfers between devices: 68.8 us -> none  [local(): gathered = lax.all_gather(latents, 'ray', axis=0, tiled=True)]
    dot_general x23 -> x17, matrix products: 87.8 us -> 45 us  [matmul(): lax.dot_general(first_arg, second_arg, (((first_dim,), (second_dim,)), ((...]
    pallas_call x3 -> x4, Pallas kernels: 303 us -> 276 us  [the longest x1 141 us: sum_over_devices(): pl.pallas_call(functools.partial(sum_kernel, n_seq, n_ray, units, 3), out...]
    unnamed x77 -> x93, local copies, waits for them, and re-layouts: 5.48 us -> 12 us
  transfers between devices with their start and end apart: 1 -> 0, of which waited for: 1 -> 0; matrix products, arithmetic and copies ran while one was open for 3% -> 0% of each run, Pallas kernels for 0% -> 0%
where the time goes in v3:
time: 376 us; the launch traced here: 372 us
  Pallas kernels  276 us (73%)
  matrix products  45 us (12%)
  other arithmetic  29.8 us (8%)
  local copies, waits for them, and re-layouts  19.6 us (5%)
    pallas_call x1, Pallas kernels, sum_over_devices(): pl.pallas_call(functools.partial(sum_kernel, n_seq, n_ray, units, 3), out...  141 us
    pallas_call x1, Pallas kernels, gather_and_project(): pl.pallas_call(functools.partial(gather_kernel, n_seq, n_ray, kinds), out...  63.4 us
    pallas_call x1, Pallas kernels, attend_back(): pl.pallas_call(attend_back_kernel, out_shape=(jax.ShapeDtypeStruct((slots...  46.3 us
    dot_general x17, matrix products, matmul(): lax.dot_general(first_arg, second_arg, (((first_dim,), (second_dim,)), ((...  45 us
    pallas_call x1, Pallas kernels, attend(): pl.pallas_call(attend_kernel, out_shape=(jax.ShapeDtypeStruct((slots, wid...  25.5 us
    another operation x2, other arithmetic, local(): jnp.stack([jnp.concatenate([g.astype(bf16) for g in half], axis=0) for ha...  12.7 us
    unnamed x93, local copies, waits for them, and re-layouts  12 us

profile of v3, /device:TPU:0, one launch (start us, length us, event | category | flops | bytes accessed | tf_op | source)
XLA Modules:
  0.0 371.9 jit_solution(6027405511576963382)
XLA Ops:
  0.6 0.0 copy-start
  0.7 0.8 reshape.88.scenes_ref
  1.5 0.7 reshape.89
  2.2 0.7 reshape.90
  2.9 0.7 reshape.91
  3.6 0.7 reshape.92
  4.3 0.0 copy-start.2
  4.3 1.1 copy-done.2
  5.4 1.3 copy-done.5
  6.6 1.3 copy-done.7
  7.9 1.1 copy-done.9
  9.0 63.4 %gather_and_project.1 = (bf16[3072,768]{1,0:T(8,128)(2,1)}, bf16[3072,768]{1,0:T(8,128)(2,1)}, bf16[768,3072]{1,0:T(8,128)(2,1)}, bf16[3072,768]{1,0:T(8,128)(2,...) custom-call(bf16[384,768]{1,0:T(8,128)(2,1)S(1)} %copy-done.2, ...), custom_call_target="tpu_custom_call" | custom-call | tf_op jit(solution)/shard_map/gather_and_project/pallas_call | solution.py:951
  72.4 0.9 copy-done.4
  73.3 0.6 copy-done.10
  73.9 0.8 copy-done.11
  74.7 25.5 %attend.1 = (f32[512,768]{1,0:T(8,128)}, f32[8,768]{1,0:T(8,128)}) custom-call(s32[8,128]{1,0:T(8,128)} %copy-done.10, s32[1,3]{1,0:T(1,128)} %lengths.3, bf16[512,768]{1,0:T(8,128)(2,1)} %copy-done.4, bf16[3072,768]{1,0:T(8,128)(2,1)} %get-tuple-element.36.k_ref, bf16[768,3072]{1,0:T(8,128)(2,1)} %get-tuple-element.37.vt_ref), custom_call_target="tpu_custom_call" | custom-call | tf_op jit(solution)/shard_map/attend/pallas_call | solution.py:177
  100.2 2.0 convolution_convert_fusion.9
  102.3 0.8 copy-done.15
  103.1 0.6 fusion.11
  103.8 0.4 copy-done.31
  104.2 1.1 convolution_add_fusion
  105.3 7.9 %convert_reduce_fusion.1 = (f32[1536]{0:T(1024)}, bf16[384,1536]{1,0:T(8,128)(2,1)S(1)}, f32[384,1536]{1,0:T(8,128)S(1)}) fusion(f32[384,1536]{1,0:T(8,128)S(1)} %convolution_add_fusion, bf16[384,768]{1,0:T(8,128)(2,1)S(1)} %copy-done.21, bf16[1536,768]{1,0:T(8,128)(2,1)S(1)} %copy-done), kind=kOutput, calls=%fused_computation.12 | convolution fusion | flops 949615104 | bytes 8853504 | tf_op jit(solution)/shard_map/dot_general | solution.py:23
  113.2 0.5 multiply_convert_fusion
  113.7 0.2 copy-done.30
  113.9 1.9 fusion.13
  115.8 1.1 convert_add_fusion.1
  116.9 0.2 convert_reduce_fusion.2
  117.1 0.3 fusion.19
  117.5 2.1 convolution_convert_fusion.6.g_ref
  119.5 46.3 %attend_back.1 = (bf16[512,768]{1,0:T(8,128)(2,1)}, bf16[3072,768]{1,0:T(8,128)(2,1)}, bf16[3072,768]{1,0:T(8,128)(2,1)}) custom-call(s32[8,128]{1,0:T(8,128)} %copy-done.10, s32[1,3]{1,0:T(1,128)} %lengths.3, bf16[512,768]{1,0:T(8,128)(2,1)} %copy-done.4, bf16[3072,768]{1,0:T(8,128)(2,1)} %get-tuple-element.36.k_ref, ...), custom_call_target="tpu_custom_call" | custom-call | tf_op jit(solution)/shard_map/attend_back/pallas_call | solution.py:198
  165.8 2.2 convert_reduce_fusion.5
  168.0 1.5 fusion.18
  169.5 1.4 convert_reduce_fusion.4
  170.9 0.1 copy-done.22
  171.1 1.4 convolution_convert_fusion
  172.5 0.2 fusion.32
  172.7 0.0 slice-start.7
  172.7 1.4 convolution_convert_fusion.1
  174.2 0.2 fusion.31
  174.3 0.4 slice-done.4
  174.7 1.2 slice-done.6
  176.0 0.0 slice-done.5
  176.0 0.2 slice-done.7
  176.2 4.0 %convolution_convert_fusion.4 = bf16[768,768]{1,0:T(8,128)(2,1)S(1)} fusion(bf16[3072,768]{1,0:T(8,128)(2,1)S(1)} %bitcast.71, bf16[3072,768]{1,0:T(8,128)(2,1)S(1)} %bitcast.73), kind=kOutput, calls=%fused_computation.33 | convolution fusion | flops 3624468480 | bytes 10616832 | tf_op jit(solution)/shard_map/dot_general | solution.py:23
  180.2 0.8 convolution_convert_fusion.5
  181.1 0.4 copy-done.14
  181.5 0.1 copy-done.16
  181.6 0.8 convolution_convert_fusion.2
  182.5 4.3 %convolution_convert_fusion.3 = bf16[768,768]{1,0:T(8,128)(2,1)S(1)} fusion(bf16[3072,768]{1,0:T(8,128)(2,1)S(1)} %bitcast.71, bf16[3072,768]{1,0:T(8,128)(2,1)S(1)} %bitcast.66), kind=kOutput, calls=%fused_computation.32 | convolution fusion | flops 3624468480 | bytes 10616832 | tf_op jit(solution)/shard_map/dot_general | solution.py:23
  186.8 4.3 %maximum_bitcast_fusion = (bf16[1,3072,768]{2,1,0:T(8,128)(2,1)}, bf16[1,3072,768]{2,1,0:T(8,128)(2,1)}) fusion(bf16[768,768]{1,0:T(8,128)(2,1)S(1)} %get-tuple-element.73, bf16[768,768]{1,0:T(8,128)(2,1)S(1)} %get-tuple-element.71, bf16[768,768]{1,0:T(8,128)(2,1)S(1)} %convolution_convert_fusion.4, bf16[768,768]{1,0:T(8,128)(2,1)S(1)} %convolution_convert_fusion.5, ...), kind=kLoop, calls=%fused_computation.3 | loop fusion | flops 37748736 | bytes 18874368 | tf_op jit(solution)/shard_map/stack | solution.py:1065
  191.1 8.4 %pad_maximum_fusion.g_ref = bf16[2,3072,768]{2,1,0:T(8,128)(2,1)} fusion(bf16[1,3072,768]{2,1,0:T(8,128)(2,1)} %get-tuple-element.85, bf16[1,3072,768]{2,1,0:T(8,128)(2,1)} %get-tuple-element.84), kind=kLoop, calls=%fused_computation | loop fusion | flops 4718592 | bytes 18874368 | tf_op jit(solution)/shard_map/stack | solution.py:1065
  199.5 6.0 %fusion.34 = f32[3072,768]{1,0:T(8,128)S(1)} fusion(bf16[3072,768]{1,0:T(8,128)(2,1)} %get-tuple-element.45, bf16[768,768]{1,0:T(8,128)(2,1)S(1)} %copy-done.8), kind=kOutput, calls=%fused_computation.89 | convolution fusion | flops 3623878656 | bytes 15335424 | tf_op jit(solution)/shard_map/dot_general | solution.py:23
  205.6 5.7 %add_convert_fusion = bf16[3072,768]{1,0:T(8,128)(2,1)} fusion(f32[3072,768]{1,0:T(8,128)S(1)} %fusion.34, bf16[3072,768]{1,0:T(8,128)(2,1)S(1)} %bitcast.68, bf16[768,768]{1,0:T(8,128)(2,1)S(1)} %copy-done.18), kind=kOutput, calls=%fused_computation.2 | convolution fusion | flops 3628597248 | bytes 20054016 | tf_op jit(solution)/shard_map/dot_general | solution.py:23
  211.4 0.7 convert_reduce_fusion
  212.2 0.1 convert_reduce_fusion.3
  212.3 0.7 stack.47.small_ref
  212.9 140.7 %sum_over_devices.1 = (bf16[2,3072,768]{2,1,0:T(8,128)(2,1)}, f32[384,768]{1,0:T(8,128)}, f32[8,768]{1,0:T(8,128)}) custom-call(bf16[2,3072,768]{2,1,0:T(8,128)(2,1)} %pad_maximum_fusion.g_ref, bf16[8,384,768]{2,1,0:T(8,128)(2,1)} %bitcast.69, f32[8,768]{1,0:T(8,128)} %stack.47.small_ref), custom_call_target="tpu_custom_call" | custom-call | tf_op jit(solution)/shard_map/sum_over_devices/pallas_call | solution.py:747
  353.7 1.6 slice_reduce_fusion
  355.3 6.9 %slice_bitcast_fusion.1 = (bf16[768,768]{1,0:T(8,128)(2,1)S(1)}, bf16[768,768]{1,0:T(8,128)(2,1)}, bf16[768,768]{1,0:T(8,128)(2,1)S(1)}, bf16[768,768]{1,0:T(8,1...) fusion(bf16[2,4,768,768]{3,2,1,0:T(8,128)(2,1)} %bitcast.64), kind=kLoop, calls=%fused_computation.57 | loop fusion | flops 2359296 | bytes 23592960 | tf_op jit(solution)/shard_map/squeeze | solution.py:1096
  362.3 2.8 maximum_convert_fusion
  365.1 0.7 slice.84
  365.8 0.6 reshape.95
  366.4 4.0 %maximum_convert_fusion.1 = f32[1536,768]{1,0:T(8,128)} fusion(bf16[768,768]{1,0:T(8,128)(2,1)} %get-tuple-element.64, bf16[768,768]{1,0:T(8,128)(2,1)S(1)} %get-tuple-element.63), kind=kLoop, calls=%fused_computation.11 | loop fusion | flops 4718592 | bytes 7077888 | tf_op jit(solution)/shard_map/convert_element_type | solution.py:1096
  370.4 1.0 copy.35
  (94 shorter events, 0.3 us)
Async XLA Ops:
  0.6 104.6 %copy-start = (bf16[1536,768]{1,0:T(8,128)(2,1)S(1)}, bf16[1536,768]{1,0:T(8,128)(2,1)}, u32[]{:S(2)}) copy-start(bf16[1536,768]{1,0:T(8,128)(2,1)} %param.33) | copy-start | bytes 7077892
  4.3 1.1 copy-start.2
  5.4 1.3 copy-start.5
  6.6 1.3 copy-start.7
  7.9 1.1 copy-start.9
  72.4 0.9 copy-start.4
  73.3 0.6 copy-start.10
  73.9 0.8 copy-start.11
  100.2 2.1 copy-start.29
  100.2 2.9 copy-start.3
  100.2 2.9 copy-start.32
  102.3 0.8 copy-start.15
  102.3 1.5 copy-start.25
  102.3 1.9 copy-start.31
  103.8 10.1 %copy-start.34 = (f32[384,768]{1,0:T(8,128)}, f32[384,768]{1,0:T(8,128)S(1)}, u32[]{:S(2)}) copy-start(f32[384,768]{1,0:T(8,128)S(1)} %fusion.11) | copy-start | bytes 3538948
  104.2 1.1 copy-start.21
  113.2 2.6 copy-start.36
  113.2 0.7 copy-start.30
  113.9 1.9 copy-start.19
  115.8 1.6 copy-start.23
  115.8 1.7 copy-start.33
  116.9 52.6 %copy-start.13 = (f32[384,768]{1,0:T(8,128)}, f32[384,768]{1,0:T(8,128)S(1)}, u32[]{:S(2)}) copy-start(f32[384,768]{1,0:T(8,128)S(1)} %convert_add_fusion.1) | copy-start | bytes 3538948
  119.5 48.5 %copy-start.6 = (bf16[768,768]{1,0:T(8,128)(2,1)S(1)}, bf16[768,768]{1,0:T(8,128)(2,1)}, u32[]{:S(2)}) copy-start(bf16[768,768]{1,0:T(8,128)(2,1)} %wq_ref.1) | copy-start | bytes 3538948
  169.5 1.5 copy-start.20
  169.5 1.6 copy-start.22
  171.1 1.6 copy-start.35
  171.1 1.6 copy-start.37
  172.5 2.2 slice-start.4
  172.5 3.5 slice-start.6
  172.7 3.3 slice-start.5
  172.7 3.4 slice-start.7
  174.3 8.1 %slice-start = ((s8[4718592]{0:T(1024)(128)(4,1)}), s8[4194304]{0:T(1024)(128)(4,1)S(1)}, s32[]{:S(2)}) async-start(s8[4718592]{0:T(1024)(128)(4,1)} %bitcast.65), calls=%async_computation | async-start | bytes 8388608
  176.2 4.1 %copy-start.12 = (bf16[384,768]{1,0:T(8,128)(2,1)S(1)}, bf16[384,768]{1,0:T(8,128)(2,1)}, u32[]{:S(2)}) copy-start(bf16[384,768]{1,0:T(8,128)(2,1)} %copy-done.11) | copy-start | bytes 1769476
  176.2 6.3 %slice-start.1 = ((s8[4718592]{0:T(1024)(128)(4,1)}), s8[524288]{0:T(1024)(128)(4,1)S(1)}, s32[]{:S(2)}) async-start(s8[4718592]{0:T(1024)(128)(4,1)} %bitcast.65), calls=%async_computation.1 | async-start | bytes 1048576
  180.2 1.3 copy-start.14
  180.2 1.4 copy-start.16
  191.1 8.4 %copy-start.8 = (bf16[768,768]{1,0:T(8,128)(2,1)S(1)}, bf16[768,768]{1,0:T(8,128)(2,1)}, u32[]{:S(2)}) copy-start(bf16[768,768]{1,0:T(8,128)(2,1)} %wk_ref.1) | copy-start | bytes 3538948
  191.1 14.4 %slice-start.2 = ((s8[4718592]{0:T(1024)(128)(4,1)}), s8[524288]{0:T(1024)(128)(4,1)S(1)}, s32[]{:S(2)}) async-start(s8[4718592]{0:T(1024)(128)(4,1)} %bitcast.67), calls=%async_computation.2 | async-start | bytes 1048576
  199.5 6.0 %slice-start.3 = ((s8[4718592]{0:T(1024)(128)(4,1)}), s8[4194304]{0:T(1024)(128)(4,1)S(1)}, s32[]{:S(2)}) async-start(s8[4718592]{0:T(1024)(128)(4,1)} %bitcast.67), calls=%async_computation.3 | async-start | bytes 8388608
  199.5 6.0 %copy-start.18 = (bf16[768,768]{1,0:T(8,128)(2,1)S(1)}, bf16[768,768]{1,0:T(8,128)(2,1)}, u32[]{:S(2)}) copy-start(bf16[768,768]{1,0:T(8,128)(2,1)} %wv_ref.1) | copy-start | bytes 3538948
  205.6 5.8 %copy-start.28 = (f32[768]{0:T(1024)S(1)}, f32[768]{0:T(1024)}, u32[]{:S(2)}) copy-start(f32[768]{0:T(1024)} %get-tuple-element.50) | copy-start | bytes 9220
  205.6 5.8 %copy-start.27 = (f32[768]{0:T(1024)S(1)}, f32[768]{0:T(1024)}, u32[]{:S(2)}) copy-start(f32[768]{0:T(1024)} %get-tuple-element.53) | copy-start | bytes 9220
  205.6 5.8 %copy-start.26 = (f32[768]{0:T(1024)S(1)}, f32[768]{0:T(1024)}, u32[]{:S(2)}) copy-start(f32[768]{0:T(1024)} %get-tuple-element.80) | copy-start | bytes 9220
  211.4 0.7 copy-start.24
  366.4 4.0 %copy-start.17 = (f32[384,768]{1,0:T(8,128)S(1)}, f32[384,768]{1,0:T(8,128)}, u32[]{:S(2)}) copy-start(f32[384,768]{1,0:T(8,128)} %get-tuple-element.104) | copy-start | bytes 3538948
  366.4 5.0 %copy-start.1 = (bf16[1536,768]{1,0:T(8,128)(2,1)S(1)}, bf16[1536,768]{1,0:T(8,128)(2,1)}, u32[]{:S(2)}) copy-start(bf16[1536,768]{1,0:T(8,128)(2,1)} %param.33) | copy-start | bytes 7077892

commit v4 on v3

v4 whole, which is shorter than its diff:
```python
import functools
import math

import jax
import jax.numpy as jnp
from jax import lax
from jax.experimental import pallas as pl
from jax.experimental.pallas import tpu as pltpu
from jax.sharding import PartitionSpec as P

HEADS = 12
HEAD = 64
TILE = 64
WIDE = 256
PACK = WIDE // HEAD
CHUNK = 512

masked_score = -1e30
f32 = jnp.float32
bf16 = jnp.bfloat16


def matmul(first_arg, second_arg, first_dim, second_dim):
    return lax.dot_general(
        first_arg,
        second_arg,
        (((first_dim,), (second_dim,)), ((), ())),
        preferred_element_type=jnp.float32,
    )


def own_block():
    row = lax.broadcasted_iota(jnp.int32, (WIDE, WIDE), 0) // TILE
    column = lax.broadcasted_iota(jnp.int32, (WIDE, WIDE), 1) // HEAD
    return row == column


def spread_heads(tile):
    return jnp.where(own_block(), jnp.concatenate([tile] * PACK, axis=0), jnp.zeros((), tile.dtype))


def fold_heads(square):
    kept = jnp.where(own_block(), square, 0.0)
    return sum(kept[TILE * h : TILE * (h + 1), :] for h in range(PACK))


def fold_rows(block, combine):
    return combine(block.reshape(block.shape[0] // 8, 8, WIDE), axis=0)


def in_scene(chunk, start, end):
    rows = lax.broadcasted_iota(jnp.int32, (CHUNK, WIDE), 0) + chunk * CHUNK
    return (rows >= start) & (rows < end)


def chunk_at(chunk):
    return pl.ds(pl.multiple_of(chunk * CHUNK, CHUNK), CHUNK)


def group_at(g):
    return slice(g * WIDE, (g + 1) * WIDE)


def scene_tiles(counts, lengths):
    kinds = lengths.shape[1]
    tile_ends, scene_ends, tiles, latents = [], [], 0, 0
    for c in range(kinds):
        tiles = tiles + (counts[c, 0] + TILE - 1) // TILE
        latents = latents + lengths[0, c]
        tile_ends.append(tiles)
        scene_ends.append(latents)

    def bounds(t):
        start, end = 0, scene_ends[0]
        for c in range(1, kinds):
            later = t >= tile_ends[c - 1]
            start = jnp.where(later, scene_ends[c - 1], start)
            end = jnp.where(later, scene_ends[c], end)
        return start, end

    return tiles, bounds


def gelu_both(pre):
    half = 0.5 * (1.0 + lax.erf(pre * math.sqrt(0.5)))
    return pre * half, half + pre * jnp.exp(-0.5 * pre * pre) * (1.0 / math.sqrt(2.0 * math.pi))


def attend(used_tiles, bounds, q_ref, k_ref, vt_ref, att_ref, lse_ref, s_ref, mixed_ref):
    groups = q_ref.shape[1] // WIDE
    att_ref[...] = jnp.zeros_like(att_ref)

    def one_tile(t, carry):
        start, end = bounds(t)
        first, last = start // CHUNK, (end + CHUNK - 1) // CHUNK
        ray_rows = pl.ds(pl.multiple_of(t * TILE, TILE), TILE)
        spread = [spread_heads(q_ref[ray_rows, group_at(g)]) for g in range(groups)]

        def score(j, tops):
            seen = in_scene(j, start, end)
            new = []
            for g in range(groups):
                s = matmul(k_ref[chunk_at(j), group_at(g)], spread[g], 1, 1)
                s = jnp.where(seen, s, masked_score)
                s_ref[chunk_at(j), group_at(g)] = s
                new.append(jnp.maximum(tops[g], fold_rows(s, jnp.max)))
            return tuple(new)

        tops = lax.fori_loop(first, last, score, (jnp.full((8, WIDE), masked_score, f32),) * groups)
        tops = [jnp.max(top, axis=0, keepdims=True) for top in tops]

        def expo(j, totals):
            new = []
            for g in range(groups):
                e = jnp.exp(s_ref[chunk_at(j), group_at(g)] - tops[g])
                s_ref[chunk_at(j), group_at(g)] = e
                new.append(totals[g] + fold_rows(e, jnp.sum))
            return tuple(new)

        totals = lax.fori_loop(first, last, expo, (jnp.zeros((8, WIDE), f32),) * groups)
        totals = [jnp.sum(total, axis=0, keepdims=True) for total in totals]
        rests = [1.0 / total for total in totals]

        def mix(j, carry):
            for g in range(groups):
                w = (s_ref[chunk_at(j), group_at(g)] * rests[g]).astype(bf16)
                mixed_ref[g] += matmul(vt_ref[group_at(g), chunk_at(j)], w, 1, 0)
            return carry

        mixed_ref[...] = jnp.zeros_like(mixed_ref)
        lax.fori_loop(first, last, mix, 0)
        for g in range(groups):
            att_ref[ray_rows, group_at(g)] = fold_heads(mixed_ref[g].T)
            lse_ref[pl.ds(t, 1), group_at(g)] = tops[g] + jnp.log(totals[g])
        return carry

    lax.fori_loop(0, used_tiles, one_tile, 0)


def attend_back(
    used_tiles, bounds, q_ref, k_ref, kt_ref, v_ref, g_ref, att_ref, lse_ref, gq_ref, gk_sum, gv_sum, gqt_sum
):
    groups = q_ref.shape[1] // WIDE
    gq_ref[...] = jnp.zeros_like(gq_ref)
    gk_sum[...] = jnp.zeros_like(gk_sum)
    gv_sum[...] = jnp.zeros_like(gv_sum)

    def one_tile(t, carry):
        start, end = bounds(t)
        first, last = start // CHUNK, (end + CHUNK - 1) // CHUNK
        ray_rows = pl.ds(pl.multiple_of(t * TILE, TILE), TILE)
        q_spread, g_spread, dots, lse = [], [], [], []
        for g in range(groups):
            q_spread.append(spread_heads(q_ref[ray_rows, group_at(g)]))
            g_tile = g_ref[ray_rows, group_at(g)]
            g_spread.append(spread_heads(g_tile))
            product = spread_heads(g_tile.astype(f32) * att_ref[ray_rows, group_at(g)])
            dots.append(
                lax.dot_general(
                    jnp.ones((8, WIDE), f32),
                    product,
                    (((1,), (1,)), ((), ())),
                    precision=lax.Precision.HIGHEST,
                    preferred_element_type=f32,
                )[0:1, :]
            )
            lse.append(lse_ref[pl.ds(t, 1), group_at(g)])
        gqt_sum[...] = jnp.zeros_like(gqt_sum)

        def step(j, carry):
            at = chunk_at(j)
            seen = in_scene(j, start, end)
            for g in range(groups):
                to = group_at(g)
                s = matmul(k_ref[at, to], q_spread[g], 1, 1)
                p = jnp.where(seen, jnp.exp(s - lse[g]), 0.0)
                gv_sum[at, to] += matmul(p.astype(bf16), g_spread[g], 1, 0)
                gp = matmul(v_ref[at, to], g_spread[g], 1, 1)
                gs = (p * (gp - dots[g])).astype(bf16)
                gk_sum[at, to] += matmul(gs, q_spread[g], 1, 0)
                gqt_sum[g] += matmul(kt_ref[to, at], gs, 1, 0)
            return carry

        lax.fori_loop(first, last, step, 0)
        for g in range(groups):
            gq_ref[ray_rows, group_at(g)] = (fold_heads(gqt_sum[g].T) * HEAD ** (-0.5)).astype(bf16)
        return carry

    lax.fori_loop(0, used_tiles, one_tile, 0)


def middle_kernel(
    counts,
    lengths,
    q_ref,
    order_ref,
    rays_ref,
    cot_ref,
    rows_ref,
    k_hbm,
    kt_hbm,
    v_hbm,
    vt_hbm,
    wo_hbm,
    wu_hbm,
    wd_hbm,
    result_ref,
    gh_ref,
    gq_out,
    small_ref,
    early_hbm,
    go_hbm,
    gk_hbm,
    gv_hbm,
    k_ref,
    v_ref,
    turned_ref,
    wo_ref,
    wu_ref,
    wd_ref,
    gk_sum,
    gv_sum,
    square_ref,
    lse_ref,
    att_ref,
    gs_ref,
    gq_ref,
    active_ref,
    gpre_ref,
    gu_slot,
    gd_slot,
    go_slot,
    in_sem,
    out_sem,
    early_sem,
):
    used_tiles, bounds = scene_tiles(counts, lengths)
    loads = [
        pltpu.make_async_copy(source, target, in_sem.at[n])
        for n, (source, target) in enumerate(
            (
                (k_hbm, k_ref),
                (vt_hbm, turned_ref),
                (wo_hbm, wo_ref),
                (wu_hbm, wu_ref),
                (wd_hbm, wd_ref),
                (v_hbm, v_ref),
                (kt_hbm, turned_ref),
            )
        )
    ]
    for load in loads[:6]:
        load.start()
    loads[0].wait()
    loads[1].wait()
    attend(used_tiles, bounds, q_ref, k_ref, turned_ref, att_ref, lse_ref, gk_sum, square_ref)
    loads[6].start()

    order = order_ref[...]
    attended = matmul(order, att_ref[...].astype(bf16), 0, 0).astype(bf16)
    loads[2].wait()
    hidden = rays_ref[...].astype(f32) + matmul(attended, wo_ref[...], 1, 0) + rows_ref[0:1, :]
    hidden_low = hidden.astype(bf16)
    hidden_turned = hidden_low.T
    cot = cot_ref[...]
    width, inner = wu_ref.shape
    blocks = inner // WIDE
    per_half = blocks // 2
    loads[3].wait()
    loads[4].wait()

    def early_copies(n):
        half, part = n // per_half, n % per_half
        slot = n % 2
        return (
            pltpu.make_async_copy(
                gu_slot.at[slot], early_hbm.at[half, pl.ds(0, width), pl.ds(part * WIDE, WIDE)], early_sem.at[0, slot]
            ),
            pltpu.make_async_copy(
                gd_slot.at[slot], early_hbm.at[half, pl.ds(width + part * WIDE, WIDE)], early_sem.at[1, slot]
            ),
        )

    for n in range(blocks):
        at = slice(n * WIDE, (n + 1) * WIDE)
        bias_row, bias_at = 1 + n * WIDE // width, slice(n * WIDE % width, n * WIDE % width + WIDE)
        pre = matmul(hidden_low, wu_ref[:, at], 1, 0) + rows_ref[bias_row : bias_row + 1, bias_at]
        active, slope = gelu_both(pre)
        active = active.astype(bf16)
        active_ref[:, at] = active
        grad_pre = (matmul(cot, wd_ref[at, :], 1, 1) * slope).astype(bf16)
        gpre_ref[:, at] = grad_pre
        small_ref[bias_row : bias_row + 1, bias_at] = jnp.sum(grad_pre.astype(f32), axis=0, keepdims=True)
        if n >= 2:
            for copy in early_copies(n - 2):
                copy.wait()
        gu_slot[n % 2] = matmul(hidden_turned, grad_pre, 1, 0).astype(bf16)
        gd_slot[n % 2] = matmul(active, cot, 0, 0).astype(bf16)
        for copy in early_copies(n):
            copy.start()
    result_ref[...] = (hidden + matmul(active_ref[...], wd_ref[...], 1, 0) + rows_ref[3:4, :]).astype(bf16)
    grad_top = cot.astype(f32)
    small_ref[3:4, :] = jnp.sum(grad_top, axis=0, keepdims=True)
    grad_hidden = grad_top + matmul(gpre_ref[...], wu_ref[...], 1, 1)
    gh_ref[...] = grad_hidden
    grad_branch = grad_hidden.astype(bf16)
    small_ref[0:1, :] = jnp.sum(grad_branch.astype(f32), axis=0, keepdims=True)
    small_ref[4:8, :] = jnp.zeros((4, width), f32)
    go_slot[...] = matmul(attended, grad_branch, 0, 0).astype(bf16)
    go_copy = pltpu.make_async_copy(go_slot, go_hbm, out_sem.at[0])
    go_copy.start()
    grad_attended = matmul(grad_branch, wo_ref[...], 1, 1).astype(bf16)
    gs_ref[...] = matmul(order, grad_attended, 1, 0).astype(bf16)

    loads[5].wait()
    loads[6].wait()
    attend_back(
        used_tiles,
        bounds,
        q_ref,
        k_ref,
        turned_ref,
        v_ref,
        gs_ref,
        att_ref,
        lse_ref,
        gq_ref,
        gk_sum,
        gv_sum,
        square_ref,
    )
    k_ref[...] = gk_sum[...].astype(bf16)
    gk_copy = pltpu.make_async_copy(k_ref, gk_hbm, out_sem.at[1])
    gk_copy.start()
    v_ref[...] = gv_sum[...].astype(bf16)
    gv_copy = pltpu.make_async_copy(v_ref, gv_hbm, out_sem.at[2])
    gv_copy.start()
    gq_out[...] = matmul(order, gq_ref[...], 0, 0).astype(bf16)
    for copy in early_copies(blocks - 2) + early_copies(blocks - 1) + (go_copy, gk_copy, gv_copy):
        copy.wait()


def attend_and_mlp(counts, lengths, q_sorted, order, rays, cotangent, rows, keys, keys_t, values, values_t, w_out, w_up, w_down):
    slots, width = q_sorted.shape
    n_rays = rays.shape[0]
    inner = w_up.shape[1]
    total = keys.shape[0]
    vmem = pltpu.VMEM
    smem = pl.BlockSpec(memory_space=pltpu.SMEM)
    in_vmem = pl.BlockSpec(memory_space=vmem)
    anywhere = pl.BlockSpec(memory_space=pl.ANY)
    struct = jax.ShapeDtypeStruct
    return pl.pallas_call(
        middle_kernel,
        out_shape=(
            struct((n_rays, width), bf16),
            struct((n_rays, width), f32),
            struct((n_rays, width), bf16),
            struct((8, width), f32),
            struct((2, 2 * width, width), bf16),
            struct((width, width), bf16),
            struct((total, width), bf16),
            struct((total, width), bf16),
        ),
        in_specs=[smem] * 2 + [in_vmem] * 5 + [anywhere] * 7,
        out_specs=(in_vmem,) * 4 + (anywhere,) * 4,
        scratch_shapes=[
            vmem((total, width), bf16),
            vmem((total, width), bf16),
            vmem((width, total), bf16),
            vmem((width, width), bf16),
            vmem((width, inner), bf16),
            vmem((inner, width), bf16),
            vmem((total, width), f32),
            vmem((total, width), f32),
            vmem((width // WIDE, WIDE, WIDE), f32),
            vmem((slots // TILE, width), f32),
            vmem((slots, width), f32),
            vmem((slots, width), bf16),
            vmem((slots, width), bf16),
            vmem((n_rays, inner), bf16),
            vmem((n_rays, inner), bf16),
            vmem((2, width, WIDE), bf16),
            vmem((2, WIDE, width), bf16),
            vmem((width, width), bf16),
            pltpu.SemaphoreType.DMA((7,)),
            pltpu.SemaphoreType.DMA((3,)),
            pltpu.SemaphoreType.DMA((2, 2)),
        ],
        compiler_params=pltpu.CompilerParams(vmem_limit_bytes=62 << 20),
        name="attend_and_mlp",
    )(counts, lengths, q_sorted, order, rays, cotangent, rows, keys, keys_t, values, values_t, w_out, w_up, w_down)


MESH = pl.DeviceIdType.MESH
BLOCK = 256
SLOW = 4


def flip(index, bit):
    return index + bit * (1 - 2 * ((index // bit) % 2))


def bits_of(count):
    bits = []
    while count > 1:
        count //= 2
        bits.append(count)
    return bits


def lane_rows(start, size):
    return pl.ds(pl.multiple_of(start, 16), size)


class Place:
    def __init__(self, n_seq, n_ray):
        self.seq = lax.axis_index("seq")
        self.ray = lax.axis_index("ray")
        self.n_fast = n_ray // SLOW
        self.core = self.seq % 2
        self.slow = self.ray // self.n_fast
        self.fast = self.ray % self.n_fast
        self.x_bits = [("seq", 2 * b) for b in bits_of(n_seq // 2)]
        self.fast_bits = [("ray", b) for b in bits_of(self.n_fast)]
        self.slow_bits = [("ray", self.n_fast * b) for b in bits_of(SLOW)]
        self.spots = (self.slow, SLOW - 1 - self.slow)

    def across(self, axis, bit):
        if axis == "seq":
            return (flip(self.seq, bit), self.ray)
        return (self.seq, flip(self.ray, bit))

    def value(self, axis, bit):
        return ((self.seq if axis == "seq" else self.ray) // bit) % 2

    def along(self, way):
        return (self.seq, self.ray + (self.n_fast if way == 0 else -self.n_fast))

    def mirrored(self, way, chunk):
        return chunk if way == 0 else SLOW - 1 - chunk


def remote(src, dst, send_sem, recv_sem, device):
    return pltpu.make_async_remote_copy(
        src_ref=src,
        dst_ref=dst,
        send_sem=send_sem,
        recv_sem=recv_sem,
        device_id=device,
        device_id_type=MESH,
    )


def greet(place, exchanges):
    barrier = pltpu.get_barrier_semaphore()
    for axis, bit in exchanges:
        pl.semaphore_signal(barrier, inc=1, device_id=place.across(axis, bit), device_id_type=MESH)
    for step in (1, SLOW - 1):
        beside = (place.seq, (place.slow + step) % SLOW * place.n_fast + place.fast)
        pl.semaphore_signal(barrier, inc=1, device_id=beside, device_id_type=MESH)
    pl.semaphore_wait(barrier, len(exchanges) + 2)


class Line:
    def __init__(self, place, block, recv, send_sem, recv_sem):
        self.place, self.block, self.recv, self.send_sem, self.recv_sem = place, block, recv, send_sem, recv_sem

    def copy(self, way, t, to):
        chunk = self.place.mirrored(way, SLOW - 1 - (t - self.place.spots[way]))
        return remote(
            self.block(chunk), self.recv(way, t), self.send_sem(way, t), self.recv_sem(way, t), self.place.along(to)
        )

    def landed(self, way, t):
        remote(
            self.recv(way, t), self.recv(way, t), self.send_sem(way, t), self.recv_sem(way, t), self.place.along(1 - way)
        ).wait_recv()
        return self.recv(way, t)[...].astype(f32)

    def step(self, t):
        for way in range(2):
            spot = self.place.spots[way]

            @pl.when((spot <= t) & (spot < SLOW - 1))
            def _(way=way, spot=spot):
                if t > 0:

                    @pl.when(spot > 0)
                    def _():
                        block = self.block(self.place.mirrored(way, SLOW - 1 - (t - spot)))
                        block[...] = (block[...].astype(f32) + self.landed(way, t - 1)).astype(bf16)

                self.copy(way, t, way).start()

    def last(self, total):
        total[...] = self.block(self.place.slow)[...].astype(f32)
        for way in range(2):

            @pl.when(self.place.spots[way] > 0)
            def _(way=way):
                total[...] += self.landed(way, SLOW - 2)

    def drain(self):
        for way in range(2):
            for t in range(SLOW - 1):
                spot = self.place.spots[way]

                @pl.when((spot <= t) & (spot < SLOW - 1))
                def _(way=way, t=t):
                    self.copy(way, t, way).wait_send()


class Spread:
    def __init__(self, place, block, send_sem, recv_sem):
        self.place, self.block, self.send_sem, self.recv_sem = place, block, send_sem, recv_sem

    def copy(self, way, t, to):
        chunk = self.place.mirrored(way, self.place.spots[way] - t)
        block = self.block(chunk)
        return remote(block, block, self.send_sem(way, t), self.recv_sem(way, t), self.place.along(to))

    def step(self, t):
        for way in range(2):
            spot = self.place.spots[way]

            @pl.when(spot >= t)
            def _(way=way, spot=spot):
                if t > 0:
                    block = self.block(self.place.mirrored(way, spot - t))
                    remote(
                        block, block, self.send_sem(way, t - 1), self.recv_sem(way, t - 1), self.place.along(1 - way)
                    ).wait_recv()
                if t < SLOW - 1:

                    @pl.when(spot < SLOW - 1)
                    def _():
                        self.copy(way, t, way).start()

    def drain(self):
        for way in range(2):
            for t in range(SLOW - 1):
                spot = self.place.spots[way]

                @pl.when((spot >= t) & (spot < SLOW - 1))
                def _(way=way, t=t):
                    self.copy(way, t, way).wait_send()


def units_of(rows, n_x, n_fast):
    share = n_x * n_fast * SLOW * 16
    return rows // BLOCK if BLOCK % share == 0 else 1


def sum_kernel(
    n_seq,
    n_ray,
    units,
    lat_start,
    lat_beat,
    wq_ref,
    wk_ref,
    wv_ref,
    shifted_ref,
    gq_ref,
    rays_ref,
    gh_ref,
    rows_ref,
    small_ref,
    early_hbm,
    go_hbm,
    gk_hbm,
    gv_hbm,
    all_hbm,
    o_q,
    o_k,
    o_v,
    o_o,
    o_u,
    o_d,
    glat_ref,
    grays_ref,
    small_out,
    grads_kv,
    all_ref,
    go_gq,
    own,
    other,
    rc,
    rx,
    z_recv,
    z_total,
    full,
    lat,
    lat_recv,
    lz_recv,
    small_now,
    small_recv,
    load_sem,
    core_sem,
    halve_sem,
    z_sem,
    zg_sem,
    double_sem,
    back_sem,
    out_sem,
    lat_sem,
    lz_sem,
    small_sem,
):
    place = Place(n_seq, n_ray)
    core_pair = ("seq", 1)
    halvings = place.x_bits + place.fast_bits
    exchanges = [core_pair] + halvings + place.slow_bits
    core = place.core
    rows, width = own.shape
    late_from = rows // 2
    unit_rows = rows // units
    sizes = [unit_rows >> i for i in range(len(halvings) + 1)]
    share = sizes[-1]
    line = share % (16 * SLOW) == 0
    piece = share // SLOW if line else share

    loads = [
        pltpu.make_async_copy(source, target, load_sem.at[n])
        for n, (source, target) in enumerate(
            (
                (early_hbm.at[core], own.at[pl.ds(0, late_from)]),
                (go_hbm, go_gq.at[0]),
                (gk_hbm, grads_kv.at[0]),
                (gv_hbm, grads_kv.at[1]),
                (all_hbm, all_ref),
            )
        )
    ]
    for load in loads:
        load.start()
    greet(place, exchanges)

    def base(u, stages):
        start = u * unit_rows
        for i in range(stages):
            start = start + place.value(*halvings[i]) * sizes[i + 1]
        return start

    def unit(u):
        return lane_rows(u * unit_rows, unit_rows)

    def core_parts(u):
        if units == 1:
            rows_of = (pl.ds(0, late_from), pl.ds(0, late_from))
            when = (u == 0, u == 0)
            into = (pl.ds(0, late_from), pl.ds(late_from, late_from))
        else:
            rows_of = (unit(u), lane_rows(u * unit_rows - late_from, unit_rows))
            when = (u < units // 2, u >= units // 2)
            into = (unit(u), unit(u))
        sources = (early_hbm.at[1 - core, rows_of[0]], other.at[rows_of[1]])
        return [
            (
                when[n],
                remote(
                    sources[n], rc.at[into[n]], core_sem.at[0, n, u], core_sem.at[1, n, u], place.across(*core_pair)
                ),
            )
            for n in range(2)
        ]

    def halve_copy(i, u):
        size = sizes[i + 1]
        sent = base(u, i) + (1 - place.value(*halvings[i])) * size
        return remote(
            own.at[lane_rows(sent, size)],
            rx[i].at[lane_rows(u * size, size)],
            halve_sem.at[0, i, u],
            halve_sem.at[1, i, u],
            place.across(*halvings[i]),
        )

    def start_core(u):
        for when, copy in core_parts(u):

            @pl.when(when)
            def _(copy=copy):
                copy.start()

    def join_core(u):
        for when, copy in core_parts(u):

            @pl.when(when)
            def _(copy=copy):
                copy.wait()

        own[unit(u), :] = (own[unit(u), :].astype(f32) + rc[unit(u), :].astype(f32)).astype(bf16)
        halve_copy(0, u).start()

    def join_half(i):
        def run(u):
            size = sizes[i + 1]
            halve_copy(i, u).wait()
            kept = lane_rows(base(u, i + 1), size)
            own[kept, :] = (own[kept, :].astype(f32) + rx[i][lane_rows(u * size, size), :].astype(f32)).astype(bf16)
            if i + 1 < len(halvings):
                halve_copy(i + 1, u).start()

        return run

    def z_rows(u, chunk):
        return lane_rows(base(u, len(halvings)) + chunk * piece, piece)

    def z_line(u):
        return Line(
            place,
            lambda chunk: own.at[z_rows(u, chunk)],
            lambda way, t: z_recv.at[u, way, t],
            lambda way, t: z_sem.at[0, u, way, t],
            lambda way, t: z_sem.at[1, u, way, t],
        )

    def z_spread(u):
        return Spread(
            place,
            lambda chunk: full.at[z_rows(u, chunk)],
            lambda way, t: zg_sem.at[0, u, way, t],
            lambda way, t: zg_sem.at[1, u, way, t],
        )

    def z_step(t):
        return lambda u: z_line(u).step(t)

    def z_finish(u):
        z_line(u).last(z_total)
        full[z_rows(u, place.slow), :] = z_total[...].astype(bf16)
        z_spread(u).step(0)

    def spread_step(t):
        return lambda u: z_spread(u).step(t)

    def whole_copy(i, u):
        return remote(
            own.at[lane_rows(base(u, len(halvings)), share)],
            z_recv.at[u, 0, i],
            z_sem.at[0, u, 0, i],
            z_sem.at[1, u, 0, i],
            place.across(*place.slow_bits[i]),
        )

    def whole_step(i):
        def run(u):
            mine = lane_rows(base(u, len(halvings)), share)
            if i > 0:
                whole_copy(i - 1, u).wait()
                own[mine, :] = (own[mine, :].astype(f32) + z_recv[u, 0, i - 1].astype(f32)).astype(bf16)
            if i < len(place.slow_bits):
                whole_copy(i, u).start()
            else:
                full[mine, :] = own[mine, :]

        return run

    def double_copy(i, u):
        block = full.at[lane_rows(base(u, i + 1), sizes[i + 1])]
        return remote(block, block, double_sem.at[0, i, u], double_sem.at[1, i, u], place.across(*halvings[i]))

    def targets(n, c):
        per = width // BLOCK
        part, at = n // per, n % per
        rows_at = pl.ds(pl.multiple_of(at * BLOCK, BLOCK), BLOCK)
        half_at = pl.ds(pl.multiple_of(c * width, 128), width)
        lower = pl.ds(pl.multiple_of(c * width + at * BLOCK, BLOCK), BLOCK)
        even = (at + c) % 2 == 0
        return [
            (part == 0, o_u.at[rows_at, half_at]),
            (part == 1, o_d.at[lower]),
            ((part == 2) & even, o_o.at[rows_at]),
            ((part == 2) & ((at + c) % 2 == 1), o_q.at[rows_at]),
            ((part == 3) & (c == 0), o_k.at[rows_at]),
            ((part == 3) & (c == 1), o_v.at[rows_at]),
        ]

    def block_rows(n):
        return lane_rows(n * BLOCK, BLOCK)

    def blocks_of(u):
        return [u] if units > 1 else list(range(rows // BLOCK))

    def send_block(n):
        for when, target in targets(n, core):

            @pl.when(when)
            def _(target=target):
                source = full.at[block_rows(n)]
                remote(source, target, back_sem.at[0, n], back_sem.at[1, n], place.across(*core_pair)).start()
                pltpu.make_async_copy(source, target, out_sem.at[n]).start()

    def end_block(n):
        for when, target in targets(n, core):

            @pl.when(when)
            def _(target=target):
                source = full.at[block_rows(n)]
                remote(source, target, back_sem.at[0, n], back_sem.at[1, n], place.across(*core_pair)).wait_send()
                pltpu.make_async_copy(source, target, out_sem.at[n]).wait()

        for when, target in targets(n, 1 - core):

            @pl.when(when)
            def _(target=target):
                source = full.at[block_rows(n)]
                remote(source, target, back_sem.at[0, n], back_sem.at[1, n], place.across(*core_pair)).wait_recv()

    def start_double(u):
        double_copy(len(halvings) - 1, u).start()

    def join_double(i):
        def run(u):
            double_copy(i, u).wait()
            if i > 0:
                double_copy(i - 1, u).start()
            else:
                for n in blocks_of(u):
                    send_block(n)

        return run

    def finish_unit(u):
        for n in blocks_of(u):
            end_block(n)
        if line:
            z_line(u).drain()
            z_spread(u).drain()

    stages = [[start_core], [join_core], []] + [[join_half(i)] for i in range(len(halvings))]
    if line:
        stages[-1].append(z_step(0))
        stages += [[z_step(t)] for t in range(1, SLOW - 1)]
        stages += [[z_finish]] + [[spread_step(t)] for t in range(1, SLOW)]
    else:
        stages[-1].append(whole_step(0))
        stages += [[whole_step(i)] for i in range(1, len(place.slow_bits) + 1)]
    stages[-1].append(start_double)
    stages += [[join_double(i)] for i in reversed(range(len(halvings)))]
    stages += [[], [finish_unit]]

    n_fast, block = lat.shape[1:3]
    group = n_fast * block
    half_rows = block // 2
    fast_sizes = [n_fast >> i for i in range(len(place.fast_bits) + 1)]

    def chunk_of(k):
        near = jnp.minimum(place.slow, SLOW - 1 - place.slow)
        ahead = SLOW - 1 - near
        chunk = jnp.where(k < ahead, SLOW - 1 - k, jnp.where(k - ahead < near, k - ahead, near))
        return jnp.where(place.slow == near, chunk, SLOW - 1 - chunk)

    def lat_base(stages):
        start = 0
        for i in range(stages):
            start = start + place.value(*place.fast_bits[i]) * fast_sizes[i + 1]
        return start

    def lat_half(m):
        return lane_rows((m % 2) * half_rows, half_rows)

    def lat_copy(i, m):
        size = fast_sizes[i + 1]
        sent = lat_base(i) + (1 - place.value(*place.fast_bits[i])) * size
        return remote(
            lat.at[chunk_of(m // 2), pl.ds(sent, size), lat_half(m)],
            lat_recv[i].at[m],
            lat_sem.at[0, i, m],
            lat_sem.at[1, i, m],
            place.across(*place.fast_bits[i]),
        )

    def start_lat(m):
        lat_copy(0, m).start()

    def lat_line(m):
        half = m % 2
        return Line(
            place,
            lambda chunk: lat.at[chunk, place.fast, lat_half(m)],
            lambda way, t: lz_recv.at[half, way, t],
            lambda way, t: lz_sem.at[0, half, way, t],
            lambda way, t: lz_sem.at[1, half, way, t],
        )

    def join_lat(i):
        def run(m):
            lat_copy(i, m).wait()
            kept = lat.at[chunk_of(m // 2), pl.ds(lat_base(i + 1), fast_sizes[i + 1]), lat_half(m)]
            kept[...] = (kept[...].astype(f32) + lat_recv[i][m].astype(f32)).astype(bf16)
            if i + 1 < len(place.fast_bits):
                lat_copy(i + 1, m).start()
            else:
                for t in range(SLOW - 1):

                    @pl.when(m // 2 == t)
                    def _(t=t):
                        lat_line(m).step(t)

        return run

    def finish_lat(m):
        @pl.when(m // 2 == SLOW - 1)
        def _():
            lat_line(m).last(glat_ref.at[lat_half(m)])
            lat_line(m).drain()

    lat_stages = [start_lat] + [join_lat(i) for i in range(len(place.fast_bits))] + [finish_lat]
    lat_steps = 2 * SLOW

    def small_copy(i):
        axis, bit = exchanges[i]
        return remote(
            small_now.at[i], small_recv.at[i], small_sem.at[0, i], small_sem.at[1, i], place.across(axis, bit)
        )

    def start_small():
        small_copy(0).start()

    def join_small(i):
        def run():
            small_copy(i).wait()
            small_now[i + 1] = small_now[i] + small_recv[i]
            if i + 1 < len(exchanges):
                small_copy(i + 1).start()

        return run

    def query_terms():
        loads[1].wait()
        go_gq[1] = matmul(shifted_ref[...], gq_ref[...], 0, 0).astype(bf16)
        for b in range(width // BLOCK):
            at = slice(b * BLOCK, (b + 1) * BLOCK)
            own[slice(late_from + at.start, late_from + at.stop), :] = go_gq[(b + core) % 2, at, :]
            other[at, :] = go_gq[(b + 1 - core) % 2, at, :]

    def ray_terms():
        inputs = rays_ref[...].astype(f32)
        centred = inputs - jnp.mean(inputs, axis=1, keepdims=True)
        inverse = lax.rsqrt(jnp.mean(centred * centred, axis=1, keepdims=True) + 1e-05)
        normed = centred * inverse
        grad_shifted = matmul(gq_ref[...], wq_ref[...], 1, 1)
        grad_normed = grad_shifted * rows_ref[0:1, :]
        grays_ref[...] = gh_ref[...] + inverse * (
            grad_normed
            - jnp.mean(grad_normed, axis=1, keepdims=True)
            - normed * jnp.mean(grad_normed * normed, axis=1, keepdims=True)
        )
        small_now[0] = small_ref[...]
        small_now[0, 4:5] = jnp.sum(grad_shifted * normed, axis=0, keepdims=True)
        small_now[0, 5:6] = jnp.sum(grad_shifted, axis=0, keepdims=True)
        small_now[0, 6:7] = jnp.sum(gq_ref[...].astype(f32), axis=0, keepdims=True)

    def lat_terms(k):
        def run():
            if k == 0:
                loads[2].wait()
                loads[3].wait()
            at = lane_rows(chunk_of(k) * group, group)
            total = matmul(grads_kv[0, at, :], wk_ref[...], 1, 1) + matmul(grads_kv[1, at, :], wv_ref[...], 1, 1)
            lat[chunk_of(k)] = total.astype(bf16).reshape(n_fast, block, width)

        return run

    def own_key_terms():
        loads[4].wait()
        own[late_from + width :, :] = matmul(all_ref[...], grads_kv[core], 1, 0).astype(bf16)

    def other_key_terms():
        other[width:, :] = matmul(all_ref[...], grads_kv[1 - core], 1, 0).astype(bf16)
        small_now[0, 7:8] = jnp.sum(grads_kv[1].astype(f32), axis=0, keepdims=True)

    work = {6 + 2 * i: [join_small(i)] for i in range(len(exchanges))}
    terms = [query_terms, ray_terms, lat_terms(0), own_key_terms, other_key_terms]
    late_lat = [lat_terms(k) for k in range(1, SLOW)]
    if units == 1:
        work[-1] = terms + late_lat + [start_small]
    else:
        for beat, run in enumerate(terms):
            work.setdefault(beat, []).append(run)
        work[len(terms) - 1].append(start_small)
        for k, run in enumerate(late_lat):
            work.setdefault(min(6 + 2 * k, lat_start + 2 * (k + 1) * lat_beat), []).append(run)
    lat_span = lat_start + lat_beat * (lat_steps - 1 + len(lat_stages) - 1) + 1
    beats = max(units + len(stages) - 1, lat_span, max(work) + 1)
    loads[0].wait()
    for run in work.pop(-1, []):
        run()

    def one_beat(now, carry):
        for s in range(len(stages)):
            u = now - s

            @pl.when((u >= 0) & (u < units))
            def _(u=u, s=s):
                for run in stages[s]:
                    run(u)

        for beat, runs in work.items():

            @pl.when(now == beat)
            def _(runs=runs):
                for run in runs:
                    run()

        for s in range(len(lat_stages)):
            ahead = now - lat_start - lat_beat * s
            m = ahead // lat_beat

            @pl.when((ahead >= 0) & (ahead % lat_beat == 0) & (m < lat_steps))
            def _(m=m, s=s):
                lat_stages[s](m)

        return carry

    lax.fori_loop(0, beats, one_beat, 0)
    small_out[...] = small_now[len(exchanges)]


def back_and_sum(n_seq, n_ray, block, w_query, w_key, w_value, shifted, gq, rays, gh, rows, small, early, go, gk, gv, all_t):
    n_fast = n_ray // SLOW
    n_x = n_seq // 2
    width = w_query.shape[0]
    sum_rows = 2 * early.shape[1]
    total = gk.shape[0]
    units = units_of(sum_rows, n_x, n_fast)
    halvings = len(bits_of(n_x)) + len(bits_of(n_fast))
    fast_bits = len(bits_of(n_fast))
    exchanges = 1 + halvings + len(bits_of(SLOW))
    share = sum_rows // units >> halvings
    piece = share // SLOW if share % (16 * SLOW) == 0 else share
    half = block // 2
    vmem = pltpu.VMEM
    sem = pltpu.SemaphoreType.DMA
    struct = jax.ShapeDtypeStruct
    in_vmem = pl.BlockSpec(memory_space=vmem)
    anywhere = pl.BlockSpec(memory_space=pl.ANY)
    return pl.pallas_call(
        functools.partial(sum_kernel, n_seq, n_ray, units, 2, 3),
        out_shape=(
            struct((width, width), bf16),
            struct((width, width), bf16),
            struct((width, width), bf16),
            struct((width, width), bf16),
            struct((width, 2 * width), bf16),
            struct((2 * width, width), bf16),
            struct((block, width), f32),
            struct(rays.shape, f32),
            struct(small.shape, f32),
        ),
        in_specs=[in_vmem] * 9 + [anywhere] * 5,
        out_specs=(anywhere,) * 6 + (in_vmem,) * 3,
        scratch_shapes=[
            vmem((2, total, width), bf16),
            vmem((width, total), bf16),
            vmem((2, width, width), bf16),
            vmem((sum_rows, width), bf16),
            vmem((sum_rows // 2, width), bf16),
            vmem((sum_rows, width), bf16),
            [vmem((sum_rows >> (i + 1), width), bf16) for i in range(halvings)],
            vmem((units, 2, SLOW - 1, piece, width), bf16),
            vmem((piece, width), f32),
            vmem((sum_rows, width), bf16),
            vmem((SLOW, n_fast, block, width), bf16),
            [vmem((2 * SLOW, n_fast >> (i + 1), half, width), bf16) for i in range(fast_bits)],
            vmem((2, 2, SLOW - 1, half, width), bf16),
            vmem((exchanges + 1,) + small.shape, f32),
            vmem((exchanges,) + small.shape, f32),
            sem((5,)),
            sem((2, 2, units)),
            sem((2, halvings, units)),
            sem((2, units, 2, SLOW - 1)),
            sem((2, units, 2, SLOW - 1)),
            sem((2, halvings, units)),
            sem((2, sum_rows // BLOCK)),
            sem((sum_rows // BLOCK,)),
            sem((2, fast_bits, 2 * SLOW)),
            sem((2, 2, 2, SLOW - 1)),
            sem((2, exchanges)),
        ],
        compiler_params=pltpu.CompilerParams(collective_id=1, has_side_effects=True, vmem_limit_bytes=62 << 20),
        name="back_and_sum",
    )(w_query, w_key, w_value, shifted, gq, rays, gh, rows, small, early, go, gk, gv, all_t)


def gather_kernel(
    n_seq,
    n_ray,
    kinds,
    rays_ref,
    lat_ref,
    scenes_ref,
    rows_ref,
    wq_ref,
    wk_ref,
    wv_ref,
    all_ref,
    k_ref,
    kt_ref,
    v_ref,
    vt_ref,
    qs_ref,
    order_ref,
    shifted_ref,
    counts_ref,
    full,
    all_own,
    k_own,
    kt_own,
    v_own,
    vt_own,
    z_sem,
    y_sem,
    out_sem,
):
    place = Place(n_seq, n_ray)
    fast_bits = place.fast_bits[::-1]
    greet(place, place.fast_bits)
    block, width = lat_ref.shape
    half_rows = block // 2
    group = place.n_fast * block
    full[place.slow, place.fast] = lat_ref[...]

    def half_at(half):
        return pl.ds(half * half_rows, half_rows)

    def spread(half):
        return Spread(
            place,
            lambda chunk: full.at[chunk, place.fast, half_at(half)],
            lambda way, t: z_sem.at[0, half, way, t],
            lambda way, t: z_sem.at[1, half, way, t],
        )

    def fast_copy(i, chunk, half):
        axis, bit = fast_bits[i]
        mine = full.at[chunk, pl.ds(place.fast // bit * bit, bit), half_at(half)]
        return remote(mine, mine, y_sem.at[0, i, chunk, half], y_sem.at[1, i, chunk, half], place.across(axis, bit))

    def chunk_of(way, t):
        return place.mirrored(way, place.spots[way] - t)

    for half in range(2):
        fast_copy(0, place.slow, half).start()
        spread(half).step(0)

    inputs = rays_ref[...].astype(f32)
    centred = inputs - jnp.mean(inputs, axis=1, keepdims=True)
    inverse = lax.rsqrt(jnp.mean(centred * centred, axis=1, keepdims=True) + 1e-05)
    shifted = (centred * inverse * rows_ref[0:1, :] + rows_ref[1:2, :]).astype(bf16)
    shifted_ref[...] = shifted
    queries = (matmul(shifted, wq_ref[...], 1, 0) + rows_ref[2:3, :]).astype(bf16)
    n_rays = rays_ref.shape[0]
    slots = order_ref.shape[0]
    scenes = scenes_ref[...]
    same = scenes == lax.broadcasted_iota(jnp.int32, (8, n_rays), 0)
    one_hot = same.astype(f32)
    before = (
        lax.broadcasted_iota(jnp.int32, (n_rays, n_rays), 0) < lax.broadcasted_iota(jnp.int32, (n_rays, n_rays), 1)
    ).astype(bf16)
    rank = matmul(one_hot.astype(bf16), before, 1, 0)
    counts = jnp.sum(one_hot, axis=1, keepdims=True)
    counts_ref[...] = jnp.broadcast_to(counts, counts_ref.shape).astype(jnp.int32)
    scene_tiles = jnp.floor((counts + (TILE - 1)) * (1.0 / TILE))
    slot = jnp.zeros((1, n_rays), f32)
    first = jnp.zeros((1, 1), f32)
    for c in range(kinds):
        slot = slot + jnp.where(same[c : c + 1, :], rank[c : c + 1, :] + first, 0.0)
        first = first + scene_tiles[c : c + 1, :] * TILE
    order = (lax.broadcasted_iota(jnp.int32, (slots, n_rays), 0) == slot.astype(jnp.int32)).astype(f32).astype(bf16)
    order_ref[...] = order
    qs_ref[...] = (matmul(order, queries, 1, 0) * HEAD ** (-0.5)).astype(bf16)

    def results(chunk):
        rows = pl.ds(pl.multiple_of(chunk * group, 16), group)
        columns = pl.ds(pl.multiple_of(chunk * group, 128), group)
        return [
            (k_own.at[chunk], k_ref.at[rows]),
            (kt_own.at[chunk], kt_ref.at[:, columns]),
            (v_own.at[chunk], v_ref.at[rows]),
            (vt_own.at[chunk], vt_ref.at[:, columns]),
            (all_own.at[chunk], all_ref.at[:, columns]),
        ]

    def project(chunk):
        for half in range(2):
            for i in range(len(fast_bits)):
                fast_copy(i, chunk, half).wait()
                if i + 1 < len(fast_bits):
                    fast_copy(i + 1, chunk, half).start()
        latents = full[chunk].reshape(group, width)
        keys = matmul(latents, wk_ref[...], 1, 0).astype(bf16)
        k_own[chunk] = keys
        all_own[chunk] = latents.T
        kt_own[chunk] = keys.T
        values = (matmul(latents, wv_ref[...], 1, 0) + rows_ref[3:4, :]).astype(bf16)
        v_own[chunk] = values
        vt_own[chunk] = values.T
        for n, (source, target) in enumerate(results(chunk)):
            pltpu.make_async_copy(source, target, out_sem.at[n, chunk]).start()

    def visit(index, carry):
        t, way = index // 2, index % 2
        for later in range(1, SLOW):

            @pl.when(index == 2 * (later - 1))
            def _(later=later):
                for half in range(2):
                    spread(half).step(later)
                    for to in range(2):

                        @pl.when(place.spots[to] >= later)
                        def _(half=half, to=to):
                            fast_copy(0, chunk_of(to, later), half).start()

        spot = jnp.where(way == 0, place.slow, SLOW - 1 - place.slow)
        chunk = jnp.where(way == 0, spot - t, SLOW - 1 - spot + t)

        @pl.when((spot >= t) & (index != 1))
        def _():
            project(chunk)

        return carry

    lax.fori_loop(0, 2 * SLOW, visit, 0)

    def end(chunk, carry):
        for n, (source, target) in enumerate(results(chunk)):
            pltpu.make_async_copy(source, target, out_sem.at[n, chunk]).wait()
        return carry

    lax.fori_loop(0, SLOW, end, 0)
    for half in range(2):
        spread(half).drain()


def gather_and_project(n_seq, n_ray, kinds, rays, latents, scenes, rows, w_query, w_key, w_value):
    block, width = latents.shape
    n_rays = rays.shape[0]
    n_fast = n_ray // SLOW
    group = n_fast * block
    total = n_ray * block
    tiles = n_rays // TILE + kinds - 1
    fast_bits = len(bits_of(n_fast))
    vmem = pltpu.VMEM
    sem = pltpu.SemaphoreType.DMA
    in_vmem = pl.BlockSpec(memory_space=vmem)
    anywhere = pl.BlockSpec(memory_space=pl.ANY)
    tall = jax.ShapeDtypeStruct((total, width), bf16)
    wide = jax.ShapeDtypeStruct((width, total), bf16)
    return pl.pallas_call(
        functools.partial(gather_kernel, n_seq, n_ray, kinds),
        out_shape=(
            wide,
            tall,
            wide,
            tall,
            wide,
            jax.ShapeDtypeStruct((tiles * TILE, width), bf16),
            jax.ShapeDtypeStruct((tiles * TILE, n_rays), bf16),
            jax.ShapeDtypeStruct((n_rays, width), bf16),
            jax.ShapeDtypeStruct((8, 128), jnp.int32),
        ),
        in_specs=[in_vmem] * 7,
        out_specs=(anywhere,) * 5 + (in_vmem,) * 4,
        scratch_shapes=[
            vmem((SLOW, n_fast, block, width), bf16),
            vmem((SLOW, width, group), bf16),
            vmem((SLOW, group, width), bf16),
            vmem((SLOW, width, group), bf16),
            vmem((SLOW, group, width), bf16),
            vmem((SLOW, width, group), bf16),
            sem((2, 2, 2, SLOW - 1)),
            sem((2, fast_bits, SLOW, 2)),
            sem((5, SLOW)),
        ],
        compiler_params=pltpu.CompilerParams(collective_id=0, has_side_effects=True, vmem_limit_bytes=48 << 20),
        name="gather_and_project",
    )(rays, latents, scenes, rows, w_query, w_key, w_value)


def local(
    rays,
    latents,
    lengths,
    scenes,
    ln_gain,
    ln_bias,
    w_query,
    b_query,
    w_key,
    w_value,
    b_value,
    w_out,
    b_out,
    w_up,
    b_up,
    w_down,
    b_down,
    cotangent,
):
    width = rays.shape[1]
    n_seq, n_ray = lax.axis_size("seq"), lax.axis_size("ray")
    rows = jnp.concatenate([v.reshape(1, width) for v in (ln_gain, ln_bias, b_query, b_value)] * 2).astype(f32)
    all_t, keys, keys_t, values, values_t, q_sorted, order, shifted, counts = gather_and_project(
        n_seq,
        n_ray,
        lengths.shape[1],
        rays,
        latents,
        scenes.reshape(1, -1),
        rows,
        w_query,
        w_key,
        w_value,
    )
    result, grad_hidden, grad_queries, small, early, grad_w_out, grad_keys, grad_values = attend_and_mlp(
        counts,
        lengths,
        q_sorted,
        order,
        rays,
        cotangent,
        jnp.concatenate([b_out.reshape(1, width), b_up.reshape(2, width), b_down.reshape(1, width)] * 2).astype(f32),
        keys,
        keys_t,
        values,
        values_t,
        w_out,
        w_up,
        w_down,
    )

    sum_q, sum_k, sum_v, sum_o, sum_u, sum_d, grad_latents, grad_rays, vectors = back_and_sum(
        n_seq,
        n_ray,
        latents.shape[0],
        w_query,
        w_key,
        w_value,
        shifted,
        grad_queries,
        rays,
        grad_hidden,
        rows,
        small,
        early,
        grad_w_out,
        grad_keys,
        grad_values,
        all_t,
    )
    return (
        result,
        grad_rays,
        grad_latents,
        vectors[4],
        vectors[5],
        sum_q.astype(f32),
        vectors[6],
        sum_k.astype(f32),
        sum_v.astype(f32),
        vectors[7],
        sum_o.astype(f32),
        vectors[0],
        sum_u.astype(f32),
        vectors[1:3].reshape(-1),
        sum_d.astype(f32),
        vectors[3],
    )


def solution(mesh):
    whole = P(("seq", "ray"), None)
    in_specs = (whole, whole, P("seq", None), P(("seq", "ray"))) + (P(),) * 13 + (whole,)
    out_specs = (whole,) * 3 + (P(),) * 13
    return jax.shard_map(local, mesh=mesh, in_specs=in_specs, out_specs=out_specs, check_vma=False)
```

time: 376 us -> 328 us (0.87)
  matrix products: 45 us -> 0 us
  other arithmetic: 29.8 us -> 13.6 us
  Pallas kernels: 276 us -> 292 us
    dot_general x17 -> x0, matrix products: 45 us -> none  [matmul(): lax.dot_general(first_arg, second_arg, (((first_dim,), (second_dim,)), ((...]
    pallas_call x3 -> x2, Pallas kernels: 213 us -> 228 us  [the longest x1 149 us: back_and_sum(): pl.pallas_call(functools.partial(sum_kernel, n_seq, n_ray, units, 2, 3),...]
    another operation x2 -> x0, other arithmetic: 12.7 us -> none  [local(): jnp.stack([jnp.concatenate([g.astype(bf16) for g in half], axis=0) for ha...]
    squeeze x1 -> x0, other arithmetic: 6.95 us -> none  [local(): pieces[0, 3]]
    convert_element_type x8, other arithmetic: 7.32 us -> 13.6 us  [the longest x1 2.85 us: local(): sum_q.astype(f32)]
    unnamed x93 -> x34, local copies, waits for them, and re-layouts: 12 us -> 11.5 us
where the time goes in v4:
time: 328 us; the launch traced here: 326 us
  Pallas kernels  292 us (89%)
  local copies, waits for them, and re-layouts  20.2 us (6%)
  other arithmetic  13.6 us (4%)
    pallas_call x1, Pallas kernels, back_and_sum(): pl.pallas_call(functools.partial(sum_kernel, n_seq, n_ray, units, 2, 3),...  149 us
    pallas_call x1, Pallas kernels, attend_and_mlp(): pl.pallas_call(middle_kernel, out_shape=(struct((n_rays, width), bf16), s...  78.9 us
    pallas_call x1, Pallas kernels, gather_and_project(): pl.pallas_call(functools.partial(gather_kernel, n_seq, n_ray, kinds), out...  63.8 us
    unnamed x34, local copies, waits for them, and re-layouts  11.5 us

profile of v4, /device:TPU:0, one launch (start us, length us, event | category | flops | bytes accessed | tf_op | source)
XLA Modules:
  0.0 326.4 jit_solution(929289157670366457)
XLA Ops:
  0.6 0.7 reshape.59.scenes_ref
  1.3 0.7 reshape.60
  2.0 0.7 reshape.61
  2.7 0.7 reshape.62
  3.4 0.7 reshape.63
  4.1 0.7 reshape.64
  4.8 0.7 reshape.65
  5.5 0.7 reshape.66
  6.2 0.0 copy-start.7
  6.3 0.6 convert_element_type.25.rows_ref
  6.9 0.0 copy-start
  6.9 1.1 copy-done
  7.9 0.0 copy-start.1
  7.9 1.3 copy-done.1
  9.2 0.0 copy-start.2
  9.2 1.3 copy-done.2
  10.5 0.0 copy-start.5
  10.5 1.1 copy-done.5
  11.5 63.8 %gather_and_project.1 = (bf16[768,3072]{1,0:T(8,128)(2,1)}, bf16[3072,768]{1,0:T(8,128)(2,1)}, bf16[768,3072]{1,0:T(8,128)(2,1)}, bf16[3072,768]{1,0:T(8,128)(2,...) custom-call(bf16[384,768]{1,0:T(8,128)(2,1)S(1)} %copy-done, ...), custom_call_target="tpu_custom_call" | custom-call | tf_op jit(solution)/shard_map/gather_and_project/pallas_call | solution.py:1254
  75.4 0.0 copy-done.7
  75.4 0.0 copy-start.3
  75.4 0.9 copy-done.3
  76.3 0.0 copy-start.4
  76.3 0.8 copy-done.4
  77.1 0.0 copy-start.6
  77.1 0.7 copy-done.6
  77.8 0.0 copy-start.8
  77.8 0.6 copy-done.8
  78.4 78.9 %attend_and_mlp.1 = (bf16[384,768]{1,0:T(8,128)(2,1)}, f32[384,768]{1,0:T(8,128)}, bf16[384,768]{1,0:T(8,128)(2,1)}, f32[8,768]{1,0:T(8,128)}, bf16[2,1536,768]{...) custom-call(s32[8,128]{1,0:T(8,128)} %copy-done.8, ...), custom_call_target="tpu_custom_call" | custom-call | tf_op jit(solution)/shard_map/attend_and_mlp/pallas_call | solution.py:353
  157.3 149.2 %back_and_sum.1 = (bf16[768,768]{1,0:T(8,128)(2,1)}, bf16[768,768]{1,0:T(8,128)(2,1)}, bf16[768,768]{1,0:T(8,128)(2,1)}, bf16[768,768]{1,0:T(8,128)(2,1)}, bf16[...) custom-call(bf16[768,768]{1,0:T(8,128)(2,1)} %wq_ref.3, ...), custom_call_target="tpu_custom_call" | custom-call | tf_op jit(solution)/shard_map/back_and_sum/pallas_call | solution.py:1041
  306.5 0.0 copy-start.13
  306.5 0.8 slice.26
  307.4 1.6 slice_reduce_fusion
  309.0 0.6 reshape.67
  309.6 2.8 convert_element_type.26
  312.4 0.0 copy-done.13
  312.4 0.0 copy-start.12
  312.4 1.6 convert_element_type.27
  314.0 0.1 copy-done.12
  314.1 0.0 copy-start.11
  314.1 1.6 convert_element_type.28
  315.7 0.1 copy-done.11
  315.8 0.0 copy-start.10
  315.8 1.6 convert_element_type.29
  317.4 0.9 copy-done.10
  318.3 0.0 copy-start.9
  318.3 2.8 convert_element_type.30
  321.1 0.0 copy-done.9
  321.1 0.0 copy-start.15
  321.1 2.5 convert_element_type.31
  323.7 0.0 copy-done.15
  323.7 0.0 copy-start.14
  323.7 1.0 copy.36
  324.7 0.7 copy-done.14
  325.4 1.0 copy.37
  (3 shorter events, 0.1 us)
Async XLA Ops:
  6.2 69.1 %copy-start.7 = (f32[8,768]{1,0:T(8,128)}, f32[8,768]{1,0:T(8,128)S(1)}, u32[]{:S(2)}) copy-start(f32[8,768]{1,0:T(8,128)S(1)} %convert_element_type.24.rows_ref) | copy-start | bytes 73732
  6.9 1.1 copy-start
  7.9 1.3 copy-start.1
  9.2 1.3 copy-start.2
  10.5 1.1 copy-start.5
  75.4 0.9 copy-start.3
  76.3 0.8 copy-start.4
  77.1 0.7 copy-start.6
  77.8 0.6 copy-start.8
  306.5 5.9 %copy-start.13 = (bf16[768,768]{1,0:T(8,128)(2,1)S(1)}, bf16[768,768]{1,0:T(8,128)(2,1)}, u32[]{:S(2)}) copy-start(bf16[768,768]{1,0:T(8,128)(2,1)} %get-tuple-element.63) | copy-start | bytes 3538948
  312.4 1.7 copy-start.12
  314.1 1.7 copy-start.11
  315.8 2.5 copy-start.10
  318.3 2.8 copy-start.9
  321.1 2.5 copy-start.15
  323.7 1.7 copy-start.14

commit v5 on v4

v5 whole, which is shorter than its diff:
```python
import functools
import math

import jax
import jax.numpy as jnp
from jax import lax
from jax.experimental import pallas as pl
from jax.experimental.pallas import tpu as pltpu
from jax.sharding import PartitionSpec as P

HEADS = 12
HEAD = 64
TILE = 64
WIDE = 256
PACK = WIDE // HEAD
EARLY_WAIT = 2
LATE_CORE, LATE_X, LATE_STEP = 1, 2, 1
LAT_WAIT = 3
PAIR = 2
STEP = 384

masked_score = -1e30
f32 = jnp.float32
bf16 = jnp.bfloat16


def matmul(first_arg, second_arg, first_dim, second_dim):
    return lax.dot_general(
        first_arg,
        second_arg,
        (((first_dim,), (second_dim,)), ((), ())),
        preferred_element_type=jnp.float32,
    )


def own_block():
    row = lax.broadcasted_iota(jnp.int32, (WIDE, WIDE), 0) // TILE
    column = lax.broadcasted_iota(jnp.int32, (WIDE, WIDE), 1) // HEAD
    return row == column


def spread_heads(tile):
    return jnp.where(own_block(), jnp.concatenate([tile] * PACK, axis=0), jnp.zeros((), tile.dtype))


def fold_heads(turned):
    kept = jnp.where(own_block(), turned, 0.0)
    folded = (kept[:, : WIDE // 2] + kept[:, WIDE // 2 :]).T
    return folded[:TILE, :] + folded[TILE:, :]


def fold_rows(block, combine):
    return combine(block.reshape(block.shape[0] // 8, 8, block.shape[1]), axis=0)


def group_at(g):
    return slice(g * WIDE, (g + 1) * WIDE)


def segments(lengths, first, count):
    at = lax.broadcasted_iota(jnp.int32, (count, WIDE), 0) + first
    end, scene = 0, jnp.zeros((count, WIDE), f32)
    for c in range(lengths.shape[1] - 1):
        end = end + lengths[0, c]
        scene = scene + (at >= end).astype(f32)
    return scene


def gelu_both(pre):
    half = 0.5 * (1.0 + lax.erf(pre * math.sqrt(0.5)))
    return pre * half, half + pre * jnp.exp(-0.5 * pre * pre) * (1.0 / math.sqrt(2.0 * math.pi))


def mlp_kernel(
    att_ref,
    rays_ref,
    cot_ref,
    rows_ref,
    wo_ref,
    wu_ref,
    wd_ref,
    result_ref,
    gh_ref,
    ga_ref,
    dots_ref,
    small_ref,
    early_hbm,
    rest_ref,
    active_ref,
    gpre_ref,
    gu_slot,
    gd_slot,
    go_slot,
    early_sem,
    go_sem,
):
    attended = att_ref[...].astype(bf16)
    hidden = rays_ref[...].astype(f32) + matmul(attended, wo_ref[...], 1, 0) + rows_ref[4:5, :]
    hidden_low = hidden.astype(bf16)
    hidden_turned = hidden_low.T
    cot = cot_ref[...]
    width, inner = wu_ref.shape
    blocks = inner // WIDE
    per_half = blocks // 2

    def early_copies(n):
        half, part = n // per_half, n % per_half
        slot = n % 2
        return (
            pltpu.make_async_copy(
                gu_slot.at[slot], early_hbm.at[half, pl.ds(0, width), pl.ds(part * WIDE, WIDE)], early_sem.at[0, slot]
            ),
            pltpu.make_async_copy(
                gd_slot.at[slot], early_hbm.at[half, pl.ds(width + part * WIDE, WIDE)], early_sem.at[1, slot]
            ),
        )

    for n in range(blocks):
        at = slice(n * WIDE, (n + 1) * WIDE)
        bias_row, bias_at = 5 + n * WIDE // width, slice(n * WIDE % width, n * WIDE % width + WIDE)
        pre = matmul(hidden_low, wu_ref[:, at], 1, 0) + rows_ref[bias_row : bias_row + 1, bias_at]
        active, slope = gelu_both(pre)
        active = active.astype(bf16)
        active_ref[:, at] = active
        grad_pre = (matmul(cot, wd_ref[at, :], 1, 1) * slope).astype(bf16)
        gpre_ref[:, at] = grad_pre
        small_ref[bias_row - 4 : bias_row - 3, bias_at] = jnp.sum(grad_pre.astype(f32), axis=0, keepdims=True)
        if n >= 2:
            for copy in early_copies(n - 2):
                copy.wait()
        gu_slot[n % 2] = matmul(hidden_turned, grad_pre, 1, 0).astype(bf16)
        gd_slot[n % 2] = matmul(active, cot, 0, 0).astype(bf16)
        for copy in early_copies(n):
            copy.start()
    result_ref[...] = (hidden + matmul(active_ref[...], wd_ref[...], 1, 0) + rows_ref[7:8, :]).astype(bf16)
    grad_top = cot.astype(f32)
    small_ref[3:4, :] = jnp.sum(grad_top, axis=0, keepdims=True)
    grad_hidden = grad_top + matmul(gpre_ref[...], wu_ref[...], 1, 1)
    gh_ref[...] = grad_hidden
    grad_branch = grad_hidden.astype(bf16)
    small_ref[0:1, :] = jnp.sum(grad_branch.astype(f32), axis=0, keepdims=True)
    small_ref[4:8, :] = jnp.zeros((4, width), f32)
    grad_out = matmul(attended, grad_branch, 0, 0).astype(bf16)
    go_slot[...] = grad_out[: 2 * BLOCK]
    go_copies = [
        pltpu.make_async_copy(
            go_slot.at[pl.ds(c * BLOCK, BLOCK)], early_hbm.at[c, pl.ds(2 * width, BLOCK)], go_sem.at[c]
        )
        for c in range(2)
    ]
    for copy in go_copies:
        copy.start()
    rest_ref[...] = grad_out[2 * BLOCK :]
    grad_attended = matmul(grad_branch, wo_ref[...], 1, 1).astype(bf16)
    ga_ref[...] = grad_attended
    product = grad_attended.astype(f32) * att_ref[...]
    for t in range(dots_ref.shape[0]):
        for g in range(width // WIDE):
            dots_ref[t : t + 1, group_at(g)] = lax.dot_general(
                jnp.ones((8, WIDE), f32),
                spread_heads(product[t * TILE : (t + 1) * TILE, group_at(g)]),
                (((1,), (1,)), ((), ())),
                precision=lax.Precision.HIGHEST,
                preferred_element_type=f32,
            )[0:1, :]
    for copy in early_copies(blocks - 2) + early_copies(blocks - 1) + tuple(go_copies):
        copy.wait()


def mlp(attended, rays, cotangent, rows, w_out, w_up, w_down):
    n_rays, width = rays.shape
    inner = w_up.shape[1]
    vmem = pltpu.VMEM
    in_vmem = pl.BlockSpec(memory_space=vmem)
    struct = jax.ShapeDtypeStruct
    return pl.pallas_call(
        mlp_kernel,
        out_shape=(
            struct((n_rays, width), bf16),
            struct((n_rays, width), f32),
            struct((n_rays, width), bf16),
            struct((n_rays // TILE, width), f32),
            struct((8, width), f32),
            struct((2, 2 * width + BLOCK, width), bf16),
            struct((width - 2 * BLOCK, width), bf16),
        ),
        in_specs=[in_vmem] * 7,
        out_specs=(in_vmem,) * 5 + (pl.BlockSpec(memory_space=pl.ANY), in_vmem),
        scratch_shapes=[
            vmem((n_rays, inner), bf16),
            vmem((n_rays, inner), bf16),
            vmem((2, width, WIDE), bf16),
            vmem((2, WIDE, width), bf16),
            vmem((2 * BLOCK, width), bf16),
            pltpu.SemaphoreType.DMA((2, 2)),
            pltpu.SemaphoreType.DMA((2,)),
        ],
        compiler_params=pltpu.CompilerParams(vmem_limit_bytes=40 << 20),
        name="mlp",
    )(attended, rays, cotangent, rows, w_out, w_up, w_down)


MESH = pl.DeviceIdType.MESH
BLOCK = 256
SLOW = 4


def flip(index, bit):
    return index + bit * (1 - 2 * ((index // bit) % 2))


def bits_of(count):
    bits = []
    while count > 1:
        count //= 2
        bits.append(count)
    return bits


def lane_rows(start, size):
    return pl.ds(pl.multiple_of(start, 16), size)


class Place:
    def __init__(self, n_seq, n_ray):
        self.seq = lax.axis_index("seq")
        self.ray = lax.axis_index("ray")
        self.n_fast = n_ray // SLOW
        self.core = self.seq % 2
        self.slow = self.ray // self.n_fast
        self.fast = self.ray % self.n_fast
        self.x_bits = [("seq", 2 * b) for b in bits_of(n_seq // 2)]
        self.fast_bits = [("ray", b) for b in bits_of(self.n_fast)]
        self.slow_bits = [("ray", self.n_fast * b) for b in bits_of(SLOW)]
        self.spots = (self.slow, SLOW - 1 - self.slow)

    def across(self, axis, bit):
        if axis == "seq":
            return (flip(self.seq, bit), self.ray)
        return (self.seq, flip(self.ray, bit))

    def value(self, axis, bit):
        return ((self.seq if axis == "seq" else self.ray) // bit) % 2

    def along(self, way):
        return (self.seq, self.ray + (self.n_fast if way == 0 else -self.n_fast))

    def after(self, step):
        return (self.seq, (self.slow + step) % SLOW * self.n_fast + self.fast)

    def mirrored(self, way, chunk):
        return chunk if way == 0 else SLOW - 1 - chunk


def remote(src, dst, send_sem, recv_sem, device):
    return pltpu.make_async_remote_copy(
        src_ref=src,
        dst_ref=dst,
        send_sem=send_sem,
        recv_sem=recv_sem,
        device_id=device,
        device_id_type=MESH,
    )


def greet(place, exchanges):
    barrier = pltpu.get_barrier_semaphore()
    for axis, bit in exchanges:
        pl.semaphore_signal(barrier, inc=1, device_id=place.across(axis, bit), device_id_type=MESH)
    for step in range(1, SLOW):
        pl.semaphore_signal(barrier, inc=1, device_id=place.after(step), device_id_type=MESH)
    pl.semaphore_wait(barrier, len(exchanges) + SLOW - 1)


class Line:
    def __init__(self, place, block, recv, send_sem, recv_sem):
        self.place, self.block, self.recv, self.send_sem, self.recv_sem = place, block, recv, send_sem, recv_sem

    def copy(self, way, t, to):
        chunk = self.place.mirrored(way, SLOW - 1 - (t - self.place.spots[way]))
        return remote(
            self.block(chunk), self.recv(way, t), self.send_sem(way, t), self.recv_sem(way, t), self.place.along(to)
        )

    def landed(self, way, t):
        remote(
            self.recv(way, t), self.recv(way, t), self.send_sem(way, t), self.recv_sem(way, t), self.place.along(1 - way)
        ).wait_recv()
        return self.recv(way, t)[...].astype(f32)

    def step(self, t):
        for way in range(2):
            spot = self.place.spots[way]

            @pl.when((spot <= t) & (spot < SLOW - 1))
            def _(way=way, spot=spot):
                if t > 0:

                    @pl.when(spot > 0)
                    def _():
                        block = self.block(self.place.mirrored(way, SLOW - 1 - (t - spot)))
                        block[...] = (block[...].astype(f32) + self.landed(way, t - 1)).astype(bf16)

                self.copy(way, t, way).start()

    def last(self, total):
        total[...] = self.block(self.place.slow)[...].astype(f32)
        for way in range(2):

            @pl.when(self.place.spots[way] > 0)
            def _(way=way):
                total[...] += self.landed(way, SLOW - 2)

    def drain(self):
        for way in range(2):
            for t in range(SLOW - 1):
                spot = self.place.spots[way]

                @pl.when((spot <= t) & (spot < SLOW - 1))
                def _(way=way, t=t):
                    self.copy(way, t, way).wait_send()


class Spread:
    def __init__(self, place, block, send_sem, recv_sem):
        self.place, self.block, self.send_sem, self.recv_sem = place, block, send_sem, recv_sem

    def copy(self, way, t, to):
        chunk = self.place.mirrored(way, self.place.spots[way] - t)
        block = self.block(chunk)
        return remote(block, block, self.send_sem(way, t), self.recv_sem(way, t), self.place.along(to))

    def step(self, t):
        for way in range(2):
            spot = self.place.spots[way]

            @pl.when(spot >= t)
            def _(way=way, spot=spot):
                if t > 0:
                    block = self.block(self.place.mirrored(way, spot - t))
                    remote(
                        block, block, self.send_sem(way, t - 1), self.recv_sem(way, t - 1), self.place.along(1 - way)
                    ).wait_recv()
                if t < SLOW - 1:

                    @pl.when(spot < SLOW - 1)
                    def _():
                        self.copy(way, t, way).start()

    def drain(self):
        for way in range(2):
            for t in range(SLOW - 1):
                spot = self.place.spots[way]

                @pl.when((spot >= t) & (spot < SLOW - 1))
                def _(way=way, t=t):
                    self.copy(way, t, way).wait_send()


def units_of(rows, n_x, n_fast):
    share = n_x * n_fast * SLOW * 16
    return rows // BLOCK if BLOCK % share == 0 else 1


def sum_kernel(
    n_seq,
    n_ray,
    units,
    lengths,
    wq_ref,
    wk_ref,
    wv_ref,
    shifted_ref,
    rays_ref,
    rows_ref,
    small_ref,
    q_ref,
    g_ref,
    lse_ref,
    dots_ref,
    scene_ref,
    rest_ref,
    gh_hbm,
    early_hbm,
    k_hbm,
    kt_hbm,
    v_hbm,
    all_hbm,
    o_q,
    o_k,
    o_v,
    o_o,
    o_u,
    o_d,
    glat_ref,
    grays_ref,
    small_out,
    k_slot,
    kt_slot,
    v_slot,
    all_slot,
    seg_ref,
    sum_kv,
    grads_kv,
    weights_kv,
    turned_q,
    gq_ref,
    own,
    other,
    full,
    rx,
    z_recv,
    lat,
    lat_recv,
    lz_recv,
    small_now,
    small_recv,
    early_sem,
    slot_sem,
    core_sem,
    halve_sem,
    z_sem,
    zg_sem,
    double_sem,
    back_sem,
    out_sem,
    lat_sem,
    lz_sem,
    small_sem,
):
    place = Place(n_seq, n_ray)
    core_pair = ("seq", 1)
    halvings = place.x_bits + place.fast_bits
    exchanges = [core_pair] + halvings + place.slow_bits
    core = place.core
    rows, width = own.shape
    late_from = early_hbm.shape[1]
    unit_rows = rows // units
    early_units = late_from // unit_rows
    sizes = [unit_rows >> i for i in range(len(halvings) + 1)]
    share = sizes[-1]
    line = share % (16 * SLOW) == 0
    piece = share // SLOW if line else share

    early_load = pltpu.make_async_copy(early_hbm.at[core], own.at[pl.ds(0, late_from)], early_sem.at[0])
    early_load.start()
    gh_load = pltpu.make_async_copy(gh_hbm, grays_ref, early_sem.at[1])
    gh_load.start()
    greet(place, [core_pair] + halvings)

    def base(u, stages):
        start = u * unit_rows
        for i in range(stages):
            start = start + place.value(*halvings[i]) * sizes[i + 1]
        return start

    def unit(u):
        return lane_rows(u * unit_rows, unit_rows)

    def core_parts(u):
        if units == 1:
            rows_of = (pl.ds(0, late_from), pl.ds(0, rows - late_from))
            when = (u == 0, u == 0)
            into = (pl.ds(0, late_from), pl.ds(late_from, rows - late_from))
        else:
            rows_of = (unit(u), lane_rows(u * unit_rows - late_from, unit_rows))
            when = (u < early_units, u >= early_units)
            into = (unit(u), unit(u))
        sources = (early_hbm.at[1 - core, rows_of[0]], other.at[rows_of[1]])
        return [
            (
                when[n],
                remote(
                    sources[n], full.at[into[n]], core_sem.at[0, n, u], core_sem.at[1, n, u], place.across(*core_pair)
                ),
            )
            for n in range(2)
        ]

    def halve_copy(i, u):
        size = sizes[i + 1]
        sent = base(u, i) + (1 - place.value(*halvings[i])) * size
        return remote(
            own.at[lane_rows(sent, size)],
            rx[i].at[lane_rows(u * size, size)],
            halve_sem.at[0, i, u],
            halve_sem.at[1, i, u],
            place.across(*halvings[i]),
        )

    def start_core(u):
        for when, copy in core_parts(u):

            @pl.when(when)
            def _(copy=copy):
                copy.start()

    def join_core(u):
        for when, copy in core_parts(u):

            @pl.when(when)
            def _(copy=copy):
                copy.wait()

        own[unit(u), :] = (own[unit(u), :].astype(f32) + full[unit(u), :].astype(f32)).astype(bf16)
        halve_copy(0, u).start()

    def join_half(i):
        def run(u):
            size = sizes[i + 1]
            halve_copy(i, u).wait()
            kept = lane_rows(base(u, i + 1), size)
            own[kept, :] = (own[kept, :].astype(f32) + rx[i][lane_rows(u * size, size), :].astype(f32)).astype(bf16)
            if i + 1 < len(halvings):
                halve_copy(i + 1, u).start()

        return run

    def z_rows(u, chunk):
        return lane_rows(base(u, len(halvings)) + chunk * piece, piece)

    def z_copy(u, step):
        return remote(
            own.at[z_rows(u, (place.slow + step) % SLOW)],
            z_recv.at[u, step - 1],
            z_sem.at[0, u, step - 1],
            z_sem.at[1, u, step - 1],
            place.after(step),
        )

    def z_back_copy(u, step, chunk):
        block = full.at[z_rows(u, chunk)]
        return remote(block, block, zg_sem.at[0, u, step - 1], zg_sem.at[1, u, step - 1], place.after(step))

    def start_z(u):
        for step in range(1, SLOW):
            z_copy(u, step).start()

    def join_z(u):
        total = own[z_rows(u, place.slow), :].astype(f32)
        for step in range(1, SLOW):
            z_copy(u, step).wait()
            total = total + z_recv[u, step - 1].astype(f32)
        full[z_rows(u, place.slow), :] = total.astype(bf16)
        for step in range(1, SLOW):
            z_back_copy(u, step, place.slow).start()

    def join_z_back(u):
        for step in range(1, SLOW):
            z_back_copy(u, step, place.slow).wait_send()
            z_back_copy(u, step, (place.slow + SLOW - step) % SLOW).wait_recv()

    def whole_copy(i, u):
        return remote(
            own.at[lane_rows(base(u, len(halvings)), share)],
            z_recv.at[u, i],
            z_sem.at[0, u, i],
            z_sem.at[1, u, i],
            place.across(*place.slow_bits[i]),
        )

    def whole_step(i):
        def run(u):
            mine = lane_rows(base(u, len(halvings)), share)
            if i > 0:
                whole_copy(i - 1, u).wait()
                own[mine, :] = (own[mine, :].astype(f32) + z_recv[u, i - 1].astype(f32)).astype(bf16)
            if i < len(place.slow_bits):
                whole_copy(i, u).start()
            else:
                full[mine, :] = own[mine, :]

        return run

    def double_copy(i, u):
        block = full.at[lane_rows(base(u, i + 1), sizes[i + 1])]
        return remote(block, block, double_sem.at[0, i, u], double_sem.at[1, i, u], place.across(*halvings[i]))

    def targets(n, c):
        per = width // BLOCK
        part, at = n // per, n % per
        rows_at = pl.ds(pl.multiple_of(at * BLOCK, BLOCK), BLOCK)
        after = pl.ds(pl.multiple_of((n + per - 1) % per * BLOCK, BLOCK), BLOCK)
        half_at = pl.ds(pl.multiple_of(c * width, 128), width)
        lower = pl.ds(pl.multiple_of(c * width + at * BLOCK, BLOCK), BLOCK)
        last = pl.ds(2 * BLOCK, BLOCK)
        return [
            (part == 0, o_u.at[rows_at, half_at]),
            (part == 1, o_d.at[lower]),
            (n == 2 * per, o_o.at[pl.ds(pl.multiple_of(c * BLOCK, BLOCK), BLOCK)]),
            ((n > 2 * per) & (n <= 3 * per) & (c == 0), o_k.at[after]),
            ((n > 2 * per) & (n <= 3 * per) & (c == 1), o_v.at[after]),
            ((n == 3 * per + 1) & (c == 0), o_o.at[last]),
            ((n == 3 * per + 1) & (c == 1), o_q.at[pl.ds(0, BLOCK)]),
            (n == 3 * per + 2, o_q.at[pl.ds(pl.multiple_of((1 + c) * BLOCK, BLOCK), BLOCK)]),
        ]

    def block_rows(n):
        return lane_rows(n * BLOCK, BLOCK)

    def blocks_of(u):
        return [u] if units > 1 else list(range(rows // BLOCK))

    def send_block(n):
        for when, target in targets(n, core):

            @pl.when(when)
            def _(target=target):
                source = full.at[block_rows(n)]
                remote(source, target, back_sem.at[0, n], back_sem.at[1, n], place.across(*core_pair)).start()
                pltpu.make_async_copy(source, target, out_sem.at[n]).start()

    def end_block(n):
        for when, target in targets(n, core):

            @pl.when(when)
            def _(target=target):
                source = full.at[block_rows(n)]
                remote(source, target, back_sem.at[0, n], back_sem.at[1, n], place.across(*core_pair)).wait_send()
                pltpu.make_async_copy(source, target, out_sem.at[n]).wait()

        for when, target in targets(n, 1 - core):

            @pl.when(when)
            def _(target=target):
                source = full.at[block_rows(n)]
                remote(source, target, back_sem.at[0, n], back_sem.at[1, n], place.across(*core_pair)).wait_recv()

    def start_double(u):
        double_copy(len(halvings) - 1, u).start()

    def join_double(i):
        def run(u):
            double_copy(i, u).wait()
            if i > 0:
                double_copy(i - 1, u).start()
            else:
                for n in blocks_of(u):
                    send_block(n)

        return run

    def finish_unit(u):
        for n in blocks_of(u):
            end_block(n)

    stages = [[start_core], [join_core]] + [[join_half(i)] for i in range(len(halvings))]
    if line:
        stages[-1].append(start_z)
        stages += [[join_z], [join_z_back]]
    else:
        stages[-1].append(whole_step(0))
        stages += [[whole_step(i)] for i in range(1, len(place.slow_bits) + 1)]
    stages[-1].append(start_double)
    stages += [[join_double(i)] for i in reversed(range(len(halvings)))]
    stages += [[finish_unit]]

    n_fast, block = lat.shape[1:3]
    group = n_fast * block
    half_rows = block // 2
    fast_sizes = [n_fast >> i for i in range(len(place.fast_bits) + 1)]

    def chunk_of(k):
        near = jnp.minimum(place.slow, SLOW - 1 - place.slow)
        ahead = SLOW - 1 - near
        chunk = jnp.where(k < ahead, SLOW - 1 - k, jnp.where(k - ahead < near, k - ahead, near))
        return jnp.where(place.slow == near, chunk, SLOW - 1 - chunk)

    def lat_base(stages):
        start = 0
        for i in range(stages):
            start = start + place.value(*place.fast_bits[i]) * fast_sizes[i + 1]
        return start

    def lat_half(m):
        return lane_rows((m % 2) * half_rows, half_rows)

    def lat_copy(i, m):
        size = fast_sizes[i + 1]
        sent = lat_base(i) + (1 - place.value(*place.fast_bits[i])) * size
        return remote(
            lat.at[chunk_of(m // 2), pl.ds(sent, size), lat_half(m)],
            lat_recv[i].at[m],
            lat_sem.at[0, i, m],
            lat_sem.at[1, i, m],
            place.across(*place.fast_bits[i]),
        )

    def start_lat(m):
        lat_copy(0, m).start()

    def lat_line(m):
        half = m % 2
        return Line(
            place,
            lambda chunk: lat.at[chunk, place.fast, lat_half(m)],
            lambda way, t: lz_recv.at[half, way, t],
            lambda way, t: lz_sem.at[0, half, way, t],
            lambda way, t: lz_sem.at[1, half, way, t],
        )

    def join_lat(i):
        def run(m):
            lat_copy(i, m).wait()
            kept = lat.at[chunk_of(m // 2), pl.ds(lat_base(i + 1), fast_sizes[i + 1]), lat_half(m)]
            kept[...] = (kept[...].astype(f32) + lat_recv[i][m].astype(f32)).astype(bf16)
            if i + 1 < len(place.fast_bits):
                lat_copy(i + 1, m).start()
            else:
                for t in range(SLOW - 1):

                    @pl.when(m // 2 == t)
                    def _(t=t):
                        lat_line(m).step(t)

        return run

    def finish_lat(m):
        @pl.when(m // 2 == SLOW - 1)
        def _():
            lat_line(m).last(glat_ref.at[lat_half(m)])
            lat_line(m).drain()

    lat_stages = [start_lat] + [join_lat(i) for i in range(len(place.fast_bits))] + [finish_lat]

    def small_copy(i):
        axis, bit = exchanges[i]
        return remote(
            small_now.at[i], small_recv.at[i], small_sem.at[0, i], small_sem.at[1, i], place.across(axis, bit)
        )

    def start_small():
        small_copy(0).start()

    def join_small(i):
        def run():
            small_copy(i).wait()
            small_now[i + 1] = small_now[i] + small_recv[i]
            if i + 1 < len(exchanges):
                small_copy(i + 1).start()

        return run

    tiles, groups = scene_ref.shape[0], width // WIDE
    pairs, parts = tiles // PAIR, group // STEP
    per_chunk = pairs * parts

    def slot_loads(k):
        chunk = chunk_of(k)
        at, columns = lane_rows(chunk * group, group), pl.ds(pl.multiple_of(chunk * group, 128), group)
        return (
            pltpu.make_async_copy(k_hbm.at[at], k_slot, slot_sem.at[0]),
            pltpu.make_async_copy(kt_hbm.at[:, columns], kt_slot, slot_sem.at[1]),
            pltpu.make_async_copy(v_hbm.at[at], v_slot, slot_sem.at[2]),
        )

    def all_load(k):
        columns = pl.ds(pl.multiple_of(chunk_of(k) * group, 128), group)
        return pltpu.make_async_copy(all_hbm.at[:, columns], all_slot, slot_sem.at[3])

    def open_chunk(k):
        for load in slot_loads(k):
            load.wait()

        all_load(k).start()
        seg_ref[...] = segments(lengths, chunk_of(k) * group, group)
        sum_kv[...] = jnp.zeros_like(sum_kv)

    def tile_rows(t):
        return pl.ds(pl.multiple_of(t * TILE, TILE), TILE)

    def back_step(pair, part):
        at = pl.ds(pl.multiple_of(part * STEP, 128), STEP)
        own_tiles = [pair * PAIR + i for i in range(PAIR)]
        seen = jnp.concatenate([seg_ref[at, :]] * PAIR, axis=1) == jnp.concatenate(
            [scene_ref[pl.ds(t, 1), :] for t in own_tiles], axis=1
        )
        for g in range(groups):
            to = group_at(g)
            q_spread = jnp.concatenate([spread_heads(q_ref[tile_rows(t), to]) for t in own_tiles], axis=0)
            g_spread = jnp.concatenate([spread_heads(g_ref[tile_rows(t), to]) for t in own_tiles], axis=0)
            lse = jnp.concatenate([lse_ref[pl.ds(t, 1), to] for t in own_tiles], axis=1)
            dots = jnp.concatenate([dots_ref[pl.ds(t, 1), to] for t in own_tiles], axis=1)
            s = matmul(k_slot[at, to], q_spread, 1, 1)
            p = jnp.where(seen, jnp.exp(s - lse), 0.0)
            sum_kv[1, at, to] += matmul(p.astype(bf16), g_spread, 1, 0)
            gp = matmul(v_slot[at, to], g_spread, 1, 1)
            gs = (p * (gp - dots)).astype(bf16)
            sum_kv[0, at, to] += matmul(gs, q_spread, 1, 0)
            turned_q[g, pair] += matmul(kt_slot[to, at], gs, 1, 0)

    def close_chunk(k):
        @pl.when(k + 1 < SLOW)
        def _():
            for load in slot_loads(k + 1):
                load.start()

        grads_kv[...] = sum_kv[...].astype(bf16)
        total = matmul(grads_kv[0], wk_ref[...], 1, 1) + matmul(grads_kv[1], wv_ref[...], 1, 1)
        lat[chunk_of(k)] = total.astype(bf16).reshape(n_fast, block, width)
        all_load(k).wait()
        for n in range(2):
            weights_kv[n] += matmul(all_slot[...], grads_kv[n], 1, 0)
        small_now[0, 7:8] += jnp.sum(grads_kv[1].astype(f32), axis=0, keepdims=True)

    def attend(step):
        k, part_of = step // per_chunk, step % per_chunk

        @pl.when(part_of == 0)
        def _():
            open_chunk(k)

        back_step(part_of // parts, part_of % parts)

        @pl.when(part_of == per_chunk - 1)
        def _():
            close_chunk(k)

    def key_terms():
        own[late_from : late_from + width, :] = weights_kv[core].astype(bf16)
        other[:width, :] = weights_kv[1 - core].astype(bf16)

    def query_terms():
        for t in range(tiles):
            for g in range(groups):
                turned = turned_q[g, t // PAIR, :, t % PAIR * WIDE : (t % PAIR + 1) * WIDE]
                gq_ref[t * TILE : (t + 1) * TILE, group_at(g)] = (fold_heads(turned) * HEAD ** (-0.5)).astype(bf16)

    def query_weight_terms():
        terms = matmul(shifted_ref[...], gq_ref[...], 0, 0).astype(bf16)
        first, second, third = [terms[b * BLOCK : (b + 1) * BLOCK] for b in range(width // BLOCK)]
        after = late_from + width

        @pl.when(core == 0)
        def _():
            own[after : after + BLOCK, :] = rest_ref[...]
            own[after + BLOCK :, :] = second
            other[width : width + BLOCK, :] = first
            other[width + BLOCK :, :] = third

        @pl.when(core == 1)
        def _():
            own[after : after + BLOCK, :] = first
            own[after + BLOCK :, :] = third
            other[width : width + BLOCK, :] = rest_ref[...]
            other[width + BLOCK :, :] = second

    def ray_terms():
        inputs = rays_ref[...].astype(f32)
        centred = inputs - jnp.mean(inputs, axis=1, keepdims=True)
        inverse = lax.rsqrt(jnp.mean(centred * centred, axis=1, keepdims=True) + 1e-05)
        normed = centred * inverse
        grad_shifted = matmul(gq_ref[...], wq_ref[...], 1, 1)
        grad_normed = grad_shifted * rows_ref[0:1, :]
        gh_load.wait()
        grays_ref[...] += inverse * (
            grad_normed
            - jnp.mean(grad_normed, axis=1, keepdims=True)
            - normed * jnp.mean(grad_normed * normed, axis=1, keepdims=True)
        )
        small_now[0, 4:5] = jnp.sum(grad_shifted * normed, axis=0, keepdims=True)
        small_now[0, 5:6] = jnp.sum(grad_shifted, axis=0, keepdims=True)
        small_now[0, 6:7] = jnp.sum(gq_ref[...].astype(f32), axis=0, keepdims=True)

    for load in slot_loads(0):
        load.start()
    turned_q[...] = jnp.zeros_like(turned_q)
    weights_kv[...] = jnp.zeros_like(weights_kv)
    small_now[0] = small_ref[...]
    early_load.wait()

    steps = SLOW * per_chunk
    late_start = steps if units > 1 else steps + 3
    finish = [key_terms, query_terms, query_weight_terms, ray_terms, start_small]
    work = {steps + n: [run] for n, run in enumerate(finish)}
    for i in range(len(exchanges)):
        work.setdefault(steps + len(finish) + i, []).append(join_small(i))
    lat_wait = LAT_WAIT
    late_waits = [0, LATE_CORE] + [LATE_X] + [LATE_STEP] * (len(stages) - 5) + [LATE_X, 1]
    late_at = [sum(late_waits[: n + 1]) for n in range(len(stages))]
    lat_span = steps + 2 + lat_wait * (len(lat_stages) - 1)
    beats = max(late_start + units - early_units + late_at[-1], lat_span, max(work) + 1)

    def one_beat(now, carry):
        for beat, runs in work.items():

            @pl.when(now == beat)
            def _(runs=runs):
                for run in runs:
                    run()

        for s in range(len(stages)):
            early = now - EARLY_WAIT * s
            late = now - late_start - late_at[s]
            u = jnp.where(late >= 0, late + early_units, early)

            @pl.when(((late >= 0) & (u < units)) | ((early >= 0) & (early < early_units)))
            def _(u=u, s=s):
                for run in stages[s]:
                    run(u)

        for s in range(len(lat_stages)):
            ahead = now - per_chunk - lat_wait * s
            m = ahead // per_chunk * 2 + ahead % per_chunk

            @pl.when((ahead >= 0) & (ahead % per_chunk < 2) & (m < 2 * SLOW))
            def _(m=m, s=s):
                lat_stages[s](m)

        @pl.when(now < steps)
        def _():
            attend(now)

        return carry

    lax.fori_loop(0, beats, one_beat, 0)
    small_out[...] = small_now[len(exchanges)]


def back_and_sum(
    n_seq,
    n_ray,
    block,
    lengths,
    w_query,
    w_key,
    w_value,
    shifted,
    rays,
    gh,
    rows,
    small,
    queries,
    ga,
    lse,
    dots,
    scene_rows,
    rest,
    early,
    keys,
    keys_t,
    values,
    all_t,
):
    n_fast = n_ray // SLOW
    n_x = n_seq // 2
    n_rays, width = rays.shape
    group = n_fast * block
    groups, pairs = width // WIDE, n_rays // TILE // PAIR
    sum_rows = 4 * width
    late_rows = sum_rows - early.shape[1]
    units = units_of(sum_rows, n_x, n_fast)
    halvings = len(bits_of(n_x)) + len(bits_of(n_fast))
    fast_bits = len(bits_of(n_fast))
    exchanges = 1 + halvings + len(bits_of(SLOW))
    share = sum_rows // units >> halvings
    piece = share // SLOW if share % (16 * SLOW) == 0 else share
    half = block // 2
    vmem = pltpu.VMEM
    sem = pltpu.SemaphoreType.DMA
    struct = jax.ShapeDtypeStruct
    in_vmem = pl.BlockSpec(memory_space=vmem)
    anywhere = pl.BlockSpec(memory_space=pl.ANY)
    return pl.pallas_call(
        functools.partial(sum_kernel, n_seq, n_ray, units),
        out_shape=(
            struct((width, width), bf16),
            struct((width, width), bf16),
            struct((width, width), bf16),
            struct((width, width), bf16),
            struct((width, 2 * width), bf16),
            struct((2 * width, width), bf16),
            struct((block, width), f32),
            struct((n_rays, width), f32),
            struct((8, width), f32),
        ),
        in_specs=[pl.BlockSpec(memory_space=pltpu.SMEM)] + [in_vmem] * 13 + [anywhere] * 6,
        out_specs=(anywhere,) * 6 + (in_vmem,) * 3,
        scratch_shapes=[
            vmem((group, width), bf16),
            vmem((width, group), bf16),
            vmem((group, width), bf16),
            vmem((width, group), bf16),
            vmem((group, WIDE), f32),
            vmem((2, group, width), f32),
            vmem((2, group, width), bf16),
            vmem((2, width, width), f32),
            vmem((groups, pairs, WIDE, PAIR * WIDE), f32),
            vmem((n_rays, width), bf16),
            vmem((sum_rows, width), bf16),
            vmem((late_rows, width), bf16),
            vmem((sum_rows, width), bf16),
            [vmem((sum_rows >> (i + 1), width), bf16) for i in range(halvings)],
            vmem((units, SLOW - 1, piece, width), bf16),
            vmem((SLOW, n_fast, block, width), bf16),
            [vmem((2 * SLOW, n_fast >> (i + 1), half, width), bf16) for i in range(fast_bits)],
            vmem((2, 2, SLOW - 1, half, width), bf16),
            vmem((exchanges + 1, 8, width), f32),
            vmem((exchanges, 8, width), f32),
            sem((2,)),
            sem((4,)),
            sem((2, 2, units)),
            sem((2, halvings, units)),
            sem((2, units, SLOW - 1)),
            sem((2, units, SLOW - 1)),
            sem((2, halvings, units)),
            sem((2, sum_rows // BLOCK)),
            sem((sum_rows // BLOCK,)),
            sem((2, fast_bits, 2 * SLOW)),
            sem((2, 2, 2, SLOW - 1)),
            sem((2, exchanges)),
        ],
        compiler_params=pltpu.CompilerParams(collective_id=1, has_side_effects=True, vmem_limit_bytes=63 << 20),
        name="back_and_sum",
    )(
        lengths,
        w_query,
        w_key,
        w_value,
        shifted,
        rays,
        rows,
        small,
        queries,
        ga,
        lse,
        dots,
        scene_rows,
        rest,
        gh,
        early,
        keys,
        keys_t,
        values,
        all_t,
    )


def gather_kernel(
    n_seq,
    n_ray,
    lengths,
    rays_ref,
    lat_ref,
    scene_ref,
    rows_ref,
    wq_ref,
    wk_ref,
    wv_ref,
    all_ref,
    k_ref,
    kt_ref,
    v_ref,
    q_ref,
    shifted_ref,
    att_ref,
    lse_ref,
    full,
    all_own,
    k_own,
    kt_own,
    v_own,
    vt_own,
    seg_ref,
    tops,
    totals,
    mixed,
    z_sem,
    y_sem,
    out_sem,
):
    place = Place(n_seq, n_ray)
    fast_bits = place.fast_bits[::-1]
    greet(place, place.fast_bits)
    block, width = lat_ref.shape
    half_rows = block // 2
    group = place.n_fast * block
    full[place.slow, place.fast] = lat_ref[...]

    def half_at(half):
        return pl.ds(half * half_rows, half_rows)

    def spread(half):
        return Spread(
            place,
            lambda chunk: full.at[chunk, place.fast, half_at(half)],
            lambda way, t: z_sem.at[0, half, way, t],
            lambda way, t: z_sem.at[1, half, way, t],
        )

    def fast_copy(i, chunk, half):
        axis, bit = fast_bits[i]
        mine = full.at[chunk, pl.ds(place.fast // bit * bit, bit), half_at(half)]
        return remote(mine, mine, y_sem.at[0, i, chunk, half], y_sem.at[1, i, chunk, half], place.across(axis, bit))

    def chunk_of(way, t):
        return place.mirrored(way, place.spots[way] - t)

    for half in range(2):
        fast_copy(0, place.slow, half).start()
        spread(half).step(0)

    inputs = rays_ref[...].astype(f32)
    centred = inputs - jnp.mean(inputs, axis=1, keepdims=True)
    inverse = lax.rsqrt(jnp.mean(centred * centred, axis=1, keepdims=True) + 1e-05)
    shifted = (centred * inverse * rows_ref[0:1, :] + rows_ref[1:2, :]).astype(bf16)
    shifted_ref[...] = shifted
    queries = (matmul(shifted, wq_ref[...], 1, 0) + rows_ref[2:3, :]).astype(bf16)
    q_ref[...] = (queries.astype(f32) * HEAD ** (-0.5)).astype(bf16)
    tiles, groups = scene_ref.shape[0], width // WIDE
    tops[...] = jnp.full_like(tops, masked_score)
    totals[...] = jnp.zeros_like(totals)
    mixed[...] = jnp.zeros_like(mixed)

    def attend(chunk):
        seg_ref[...] = segments(lengths, chunk * group, group)

        def one_tile(t, carry):
            ray_rows = pl.ds(pl.multiple_of(t * TILE, TILE), TILE)
            seen = seg_ref[...] == scene_ref[pl.ds(t, 1), :]
            for g in range(groups):
                s = matmul(k_own[chunk, :, group_at(g)], spread_heads(q_ref[ray_rows, group_at(g)]), 1, 1)
                s = jnp.where(seen, s, masked_score)
                old = tops[g, t]
                new = jnp.maximum(old, jnp.max(fold_rows(s, jnp.max), axis=0, keepdims=True))
                e = jnp.exp(s - new[0:1])
                fix = jnp.exp(old - new)
                tops[g, t] = new
                totals[g, t] = totals[g, t] * fix + fold_rows(e, jnp.sum)
                mixed[g, t] = mixed[g, t] * fix[0:1] + matmul(vt_own[chunk, group_at(g), :], e.astype(bf16), 1, 0)
            return carry

        lax.fori_loop(0, tiles, one_tile, 0)

    def results(chunk):
        rows = pl.ds(pl.multiple_of(chunk * group, 16), group)
        columns = pl.ds(pl.multiple_of(chunk * group, 128), group)
        return [
            (k_own.at[chunk], k_ref.at[rows]),
            (kt_own.at[chunk], kt_ref.at[:, columns]),
            (v_own.at[chunk], v_ref.at[rows]),
            (all_own.at[chunk], all_ref.at[:, columns]),
        ]

    def project(chunk):
        for half in range(2):
            for i in range(len(fast_bits)):
                fast_copy(i, chunk, half).wait()
                if i + 1 < len(fast_bits):
                    fast_copy(i + 1, chunk, half).start()
        latents = full[chunk].reshape(group, width)
        keys = matmul(latents, wk_ref[...], 1, 0).astype(bf16)
        k_own[chunk] = keys
        all_own[chunk] = latents.T
        kt_own[chunk] = keys.T
        values = (matmul(latents, wv_ref[...], 1, 0) + rows_ref[3:4, :]).astype(bf16)
        v_own[chunk] = values
        vt_own[chunk] = values.T
        for n, (source, target) in enumerate(results(chunk)):
            pltpu.make_async_copy(source, target, out_sem.at[n, chunk]).start()
        attend(chunk)

    def visit(index, carry):
        t, way = index // 2, index % 2
        for later in range(1, SLOW):

            @pl.when(index == 2 * (later - 1))
            def _(later=later):
                for half in range(2):
                    spread(half).step(later)
                    for to in range(2):

                        @pl.when(place.spots[to] >= later)
                        def _(half=half, to=to):
                            fast_copy(0, chunk_of(to, later), half).start()

        spot = jnp.where(way == 0, place.slow, SLOW - 1 - place.slow)
        chunk = jnp.where(way == 0, spot - t, SLOW - 1 - spot + t)

        @pl.when((spot >= t) & (index != 1))
        def _():
            project(chunk)

        return carry

    lax.fori_loop(0, 2 * SLOW, visit, 0)

    for t in range(tiles):
        for g in range(groups):
            total = jnp.sum(totals[g, t], axis=0, keepdims=True)
            att_ref[t * TILE : (t + 1) * TILE, group_at(g)] = fold_heads(mixed[g, t] * (1.0 / total))
            lse_ref[t : t + 1, group_at(g)] = tops[g, t][0:1] + jnp.log(total)

    def end(chunk, carry):
        for n, (source, target) in enumerate(results(chunk)):
            pltpu.make_async_copy(source, target, out_sem.at[n, chunk]).wait()
        return carry

    lax.fori_loop(0, SLOW, end, 0)
    for half in range(2):
        spread(half).drain()


def gather_and_attend(n_seq, n_ray, rays, latents, lengths, scene_rows, rows, w_query, w_key, w_value):
    block, width = latents.shape
    n_rays = rays.shape[0]
    n_fast = n_ray // SLOW
    group = n_fast * block
    total = n_ray * block
    tiles, groups = n_rays // TILE, width // WIDE
    fast_bits = len(bits_of(n_fast))
    vmem = pltpu.VMEM
    sem = pltpu.SemaphoreType.DMA
    in_vmem = pl.BlockSpec(memory_space=vmem)
    anywhere = pl.BlockSpec(memory_space=pl.ANY)
    struct = jax.ShapeDtypeStruct
    tall, wide = struct((total, width), bf16), struct((width, total), bf16)
    return pl.pallas_call(
        functools.partial(gather_kernel, n_seq, n_ray),
        out_shape=(
            wide,
            tall,
            wide,
            tall,
            struct((n_rays, width), bf16),
            struct((n_rays, width), bf16),
            struct((n_rays, width), f32),
            struct((tiles, width), f32),
        ),
        in_specs=[pl.BlockSpec(memory_space=pltpu.SMEM)] + [in_vmem] * 7,
        out_specs=(anywhere,) * 4 + (in_vmem,) * 4,
        scratch_shapes=[
            vmem((SLOW, n_fast, block, width), bf16),
            vmem((SLOW, width, group), bf16),
            vmem((SLOW, group, width), bf16),
            vmem((SLOW, width, group), bf16),
            vmem((SLOW, group, width), bf16),
            vmem((SLOW, width, group), bf16),
            vmem((group, WIDE), f32),
            vmem((groups, tiles, 8, WIDE), f32),
            vmem((groups, tiles, 8, WIDE), f32),
            vmem((groups, tiles, WIDE, WIDE), f32),
            sem((2, 2, 2, SLOW - 1)),
            sem((2, fast_bits, SLOW, 2)),
            sem((4, SLOW)),
        ],
        compiler_params=pltpu.CompilerParams(collective_id=0, has_side_effects=True, vmem_limit_bytes=58 << 20),
        name="gather_and_attend",
    )(lengths, rays, latents, scene_rows, rows, w_query, w_key, w_value)


def local(
    rays,
    latents,
    lengths,
    scenes,
    ln_gain,
    ln_bias,
    w_query,
    b_query,
    w_key,
    w_value,
    b_value,
    w_out,
    b_out,
    w_up,
    b_up,
    w_down,
    b_down,
    cotangent,
):
    width = rays.shape[1]
    n_seq, n_ray = lax.axis_size("seq"), lax.axis_size("ray")
    tiles = rays.shape[0] // TILE
    names = (ln_gain, ln_bias, b_query, b_value, b_out, b_up, b_down)
    rows = jnp.concatenate([v.reshape(-1, width) for v in names]).astype(f32)
    scene_rows = jnp.broadcast_to(scenes.reshape(tiles, 1, TILE), (tiles, PACK, TILE)).reshape(tiles, WIDE).astype(f32)
    all_t, keys, keys_t, values, queries, shifted, attended, lse = gather_and_attend(
        n_seq, n_ray, rays, latents, lengths, scene_rows, rows, w_query, w_key, w_value
    )
    result, grad_hidden, grad_attended, dots, small, early, rest = mlp(attended, rays, cotangent, rows, w_out, w_up, w_down)
    sum_q, sum_k, sum_v, sum_o, sum_u, sum_d, grad_latents, grad_rays, vectors = back_and_sum(
        n_seq,
        n_ray,
        latents.shape[0],
        lengths,
        w_query,
        w_key,
        w_value,
        shifted,
        rays,
        grad_hidden,
        rows,
        small,
        queries,
        grad_attended,
        lse,
        dots,
        scene_rows,
        rest,
        early,
        keys,
        keys_t,
        values,
        all_t,
    )
    return (
        result,
        grad_rays,
        grad_latents,
        vectors[4],
        vectors[5],
        sum_q.astype(f32),
        vectors[6],
        sum_k.astype(f32),
        sum_v.astype(f32),
        vectors[7],
        sum_o.astype(f32),
        vectors[0],
        sum_u.astype(f32),
        vectors[1:3].reshape(-1),
        sum_d.astype(f32),
        vectors[3],
    )


def solution(mesh):
    whole = P(("seq", "ray"), None)
    in_specs = (whole, whole, P("seq", None), P(("seq", "ray"))) + (P(),) * 13 + (whole,)
    out_specs = (whole,) * 3 + (P(),) * 13
    return jax.shard_map(local, mesh=mesh, in_specs=in_specs, out_specs=out_specs, check_vma=False)
```

time: 328 us -> 300 us (0.915)
  Pallas kernels: 292 us -> 263 us
    pallas_call x3, Pallas kernels: 292 us -> 263 us  [the longest x1 169 us: back_and_sum(): pl.pallas_call(functools.partial(sum_kernel, n_seq, n_ray, units), out_sh...]
    unnamed x34 -> x40, local copies, waits for them, and re-layouts: 11.5 us -> 12.8 us
where the time goes in v5:
time: 300 us; the launch traced here: 299 us
  Pallas kernels  263 us (88%)
  local copies, waits for them, and re-layouts  21.4 us (7%)
  other arithmetic  14.2 us (5%)
    pallas_call x1, Pallas kernels, back_and_sum(): pl.pallas_call(functools.partial(sum_kernel, n_seq, n_ray, units), out_sh...  169 us
    pallas_call x1, Pallas kernels, gather_and_attend(): pl.pallas_call(functools.partial(gather_kernel, n_seq, n_ray), out_shape=...  78.8 us
    pallas_call x1, Pallas kernels, mlp(): pl.pallas_call(mlp_kernel, out_shape=(struct((n_rays, width), bf16), stru...  14.4 us
    unnamed x40, local copies, waits for them, and re-layouts  12.8 us

profile of v5, /device:TPU:0, one launch (start us, length us, event | category | flops | bytes accessed | tf_op | source)
XLA Modules:
  0.0 299.0 jit_solution(2016322467426816847)
XLA Ops:
  0.6 0.7 convert_element_type.28
  1.3 0.1 convert_element_type.29
  1.4 0.7 convert_element_type.30.scene_ref
  2.1 0.7 reshape.61
  2.8 0.7 reshape.62
  3.5 0.7 reshape.63
  4.2 0.7 reshape.64
  4.8 0.7 reshape.65
  5.5 0.7 reshape.66
  6.2 0.7 reshape.67
  7.0 0.6 convert_element_type.31.rows_ref
  7.6 0.0 copy-start
  7.6 0.0 copy-start.1
  7.6 0.0 copy-start.9
  7.6 78.8 %gather_and_attend.1 = (bf16[768,3072]{1,0:T(8,128)(2,1)}, bf16[3072,768]{1,0:T(8,128)(2,1)}, bf16[768,3072]{1,0:T(8,128)(2,1)}, bf16[3072,768]{1,0:T(8,128)(2,1...) custom-call(s32[1,3]{1,0:T(1,128)} %lengths.3, ...), custom_call_target="tpu_custom_call" | custom-call | tf_op jit(solution)/shard_map/gather_and_attend/pallas_call | solution.py:1218
  86.3 0.0 copy-done
  86.4 0.0 copy-done.1
  86.4 0.0 copy-done.9
  86.4 0.0 copy-start.2
  86.4 1.7 copy-done.2
  88.0 0.0 copy-start.3
  88.0 1.3 copy-done.3
  89.3 0.0 copy-start.5
  89.3 1.3 copy-done.5
  90.6 0.0 copy-start.6
  90.6 1.1 copy-done.6
  91.7 14.4 %mlp.1 = (bf16[384,768]{1,0:T(8,128)(2,1)}, f32[384,768]{1,0:T(8,128)S(1)}, bf16[384,768]{1,0:T(8,128)(2,1)S(1)}, f32[6,768]{1,0:T(8,128)S(1)}, f32[8,768]{1,0:T...) custom-call(f32[384,768]{1,0:T(8,128)S(1)} %copy-done.5, bf16[384,768]{1,0:T(8,128)(2,1)S(1)} %copy-done, ...), custom_call_target="tpu_custom_call" | custom-call | tf_op jit(solution)/shard_map/mlp/pallas_call | solution.py:176
  106.1 0.0 copy-start.4
  106.1 1.0 copy-done.4
  107.1 0.0 copy-start.7
  107.1 0.8 copy-done.7
  107.9 0.0 copy-start.8
  107.9 0.7 copy-done.8
  108.6 0.0 copy-start.10
  108.6 0.6 copy-done.10
  109.2 0.0 copy-start.11
  109.2 0.6 copy-done.11
  109.8 169.4 %back_and_sum.1 = (bf16[768,768]{1,0:T(8,128)(2,1)}, bf16[768,768]{1,0:T(8,128)(2,1)}, bf16[768,768]{1,0:T(8,128)(2,1)}, bf16[768,768]{1,0:T(8,128)(2,1)}, bf16[...) custom-call(s32[1,3]{1,0:T(1,128)} %lengths.3, ...), custom_call_target="tpu_custom_call" | custom-call | tf_op jit(solution)/shard_map/back_and_sum/pallas_call | solution.py:964
  279.3 0.0 copy-start.16
  279.3 1.6 slice_reduce_fusion
  280.9 2.8 convert_element_type.32
  283.8 0.0 copy-start.15
  283.8 0.0 copy-done.16
  283.8 1.6 convert_element_type.33
  285.4 0.0 copy-start.14
  285.4 0.1 copy-done.15
  285.4 1.6 convert_element_type.34
  287.0 0.0 copy-start.13
  287.0 0.0 copy-done.14
  287.0 1.6 convert_element_type.35
  288.6 0.9 copy-done.13
  289.5 0.0 copy-start.12
  289.5 2.8 convert_element_type.36
  292.4 0.7 slice.26
  293.1 0.6 reshape.68
  293.7 0.0 copy-done.12
  293.7 0.0 copy-start.18
  293.7 2.5 convert_element_type.37
  296.3 0.0 copy-start.17
  296.3 0.0 copy-done.18
  296.3 1.0 copy.36
  297.3 0.7 copy-done.17
  298.0 1.0 copy.37
  (2 shorter events, 0.1 us)
Async XLA Ops:
  7.6 78.8 %copy-start = (bf16[384,768]{1,0:T(8,128)(2,1)S(1)}, bf16[384,768]{1,0:T(8,128)(2,1)}, u32[]{:S(2)}) copy-start(bf16[384,768]{1,0:T(8,128)(2,1)} %rays_ref.5) | copy-start | bytes 1769476
  7.6 78.8 %copy-start.1 = (bf16[768,1536]{1,0:T(8,128)(2,1)S(1)}, bf16[768,1536]{1,0:T(8,128)(2,1)}, u32[]{:S(2)}) copy-start(bf16[768,1536]{1,0:T(8,128)(2,1)} %wu_ref.1) | copy-start | bytes 7077892
  7.6 78.8 %copy-start.9 = (f32[8,768]{1,0:T(8,128)S(1)}, f32[8,768]{1,0:T(8,128)}, u32[]{:S(2)}) copy-start(f32[8,768]{1,0:T(8,128)} %convert_element_type.31.rows_ref) | copy-start | bytes 73732
  86.4 1.7 copy-start.2
  88.0 1.3 copy-start.3
  89.3 1.3 copy-start.5
  90.6 1.1 copy-start.6
  106.1 1.0 copy-start.4
  107.1 0.8 copy-start.7
  107.9 0.7 copy-start.8
  108.6 0.6 copy-start.10
  109.2 0.6 copy-start.11
  279.3 4.5 %copy-start.16 = (bf16[768,768]{1,0:T(8,128)(2,1)S(1)}, bf16[768,768]{1,0:T(8,128)(2,1)}, u32[]{:S(2)}) copy-start(bf16[768,768]{1,0:T(8,128)(2,1)} %get-tuple-element.59) | copy-start | bytes 3538948
  283.8 1.7 copy-start.15
  285.4 1.7 copy-start.14
  287.0 2.5 copy-start.13
  289.5 4.2 %copy-start.12 = (bf16[1536,768]{1,0:T(8,128)(2,1)S(1)}, bf16[1536,768]{1,0:T(8,128)(2,1)}, u32[]{:S(2)}) copy-start(bf16[1536,768]{1,0:T(8,128)(2,1)} %get-tuple-element.63) | copy-start | bytes 7077892
  293.7 2.6 copy-start.18
  296.3 1.7 copy-start.17

commit v6 on v5

--- a/solution.py
+++ b/solution.py
@@ -16,8 +16,9 @@
 EARLY_WAIT = 2
 LATE_CORE, LATE_X, LATE_STEP = 1, 2, 1
 LAT_WAIT = 3
-PAIR = 2
-STEP = 384
+FORWARD = 2
+PAIR = 3
+STEP = 256
 
 masked_score = -1e30
 f32 = jnp.float32
@@ -69,135 +70,6 @@
 def gelu_both(pre):
     half = 0.5 * (1.0 + lax.erf(pre * math.sqrt(0.5)))
     return pre * half, half + pre * jnp.exp(-0.5 * pre * pre) * (1.0 / math.sqrt(2.0 * math.pi))
-
-
-def mlp_kernel(
-    att_ref,
-    rays_ref,
-    cot_ref,
-    rows_ref,
-    wo_ref,
-    wu_ref,
-    wd_ref,
-    result_ref,
-    gh_ref,
-    ga_ref,
-    dots_ref,
-    small_ref,
-    early_hbm,
-    rest_ref,
-    active_ref,
-    gpre_ref,
-    gu_slot,
-    gd_slot,
-    go_slot,
-    early_sem,
-    go_sem,
-):
-    attended = att_ref[...].astype(bf16)
-    hidden = rays_ref[...].astype(f32) + matmul(attended, wo_ref[...], 1, 0) + rows_ref[4:5, :]
-    hidden_low = hidden.astype(bf16)
-    hidden_turned = hidden_low.T
-    cot = cot_ref[...]
-    width, inner = wu_ref.shape
-    blocks = inner // WIDE
-    per_half = blocks // 2
-
-    def early_copies(n):
-        half, part = n // per_half, n % per_half
-        slot = n % 2
-        return (
-            pltpu.make_async_copy(
-                gu_slot.at[slot], early_hbm.at[half, pl.ds(0, width), pl.ds(part * WIDE, WIDE)], early_sem.at[0, slot]
-            ),
-            pltpu.make_async_copy(
-                gd_slot.at[slot], early_hbm.at[half, pl.ds(width + part * WIDE, WIDE)], early_sem.at[1, slot]
-            ),
-        )
-
-    for n in range(blocks):
-        at = slice(n * WIDE, (n + 1) * WIDE)
-        bias_row, bias_at = 5 + n * WIDE // width, slice(n * WIDE % width, n * WIDE % width + WIDE)
-        pre = matmul(hidden_low, wu_ref[:, at], 1, 0) + rows_ref[bias_row : bias_row + 1, bias_at]
-        active, slope = gelu_both(pre)
-        active = active.astype(bf16)
-        active_ref[:, at] = active
-        grad_pre = (matmul(cot, wd_ref[at, :], 1, 1) * slope).astype(bf16)
-        gpre_ref[:, at] = grad_pre
-        small_ref[bias_row - 4 : bias_row - 3, bias_at] = jnp.sum(grad_pre.astype(f32), axis=0, keepdims=True)
-        if n >= 2:
-            for copy in early_copies(n - 2):
-                copy.wait()
-        gu_slot[n % 2] = matmul(hidden_turned, grad_pre, 1, 0).astype(bf16)
-        gd_slot[n % 2] = matmul(active, cot, 0, 0).astype(bf16)
-        for copy in early_copies(n):
-            copy.start()
-    result_ref[...] = (hidden + matmul(active_ref[...], wd_ref[...], 1, 0) + rows_ref[7:8, :]).astype(bf16)
-    grad_top = cot.astype(f32)
-    small_ref[3:4, :] = jnp.sum(grad_top, axis=0, keepdims=True)
-    grad_hidden = grad_top + matmul(gpre_ref[...], wu_ref[...], 1, 1)
-    gh_ref[...] = grad_hidden
-    grad_branch = grad_hidden.astype(bf16)
-    small_ref[0:1, :] = jnp.sum(grad_branch.astype(f32), axis=0, keepdims=True)
-    small_ref[4:8, :] = jnp.zeros((4, width), f32)
-    grad_out = matmul(attended, grad_branch, 0, 0).astype(bf16)
-    go_slot[...] = grad_out[: 2 * BLOCK]
-    go_copies = [
-        pltpu.make_async_copy(
-            go_slot.at[pl.ds(c * BLOCK, BLOCK)], early_hbm.at[c, pl.ds(2 * width, BLOCK)], go_sem.at[c]
-        )
-        for c in range(2)
-    ]
-    for copy in go_copies:
-        copy.start()
-    rest_ref[...] = grad_out[2 * BLOCK :]
-    grad_attended = matmul(grad_branch, wo_ref[...], 1, 1).astype(bf16)
-    ga_ref[...] = grad_attended
-    product = grad_attended.astype(f32) * att_ref[...]
-    for t in range(dots_ref.shape[0]):
-        for g in range(width // WIDE):
-            dots_ref[t : t + 1, group_at(g)] = lax.dot_general(
-                jnp.ones((8, WIDE), f32),
-                spread_heads(product[t * TILE : (t + 1) * TILE, group_at(g)]),
-                (((1,), (1,)), ((), ())),
-                precision=lax.Precision.HIGHEST,
-                preferred_element_type=f32,
-            )[0:1, :]
-    for copy in early_copies(blocks - 2) + early_copies(blocks - 1) + tuple(go_copies):
-        copy.wait()
-
-
-def mlp(attended, rays, cotangent, rows, w_out, w_up, w_down):
-    n_rays, width = rays.shape
-    inner = w_up.shape[1]
-    vmem = pltpu.VMEM
-    in_vmem = pl.BlockSpec(memory_space=vmem)
-    struct = jax.ShapeDtypeStruct
-    return pl.pallas_call(
-        mlp_kernel,
-        out_shape=(
-            struct((n_rays, width), bf16),
-            struct((n_rays, width), f32),
-            struct((n_rays, width), bf16),
-            struct((n_rays // TILE, width), f32),
-            struct((8, width), f32),
-            struct((2, 2 * width + BLOCK, width), bf16),
-            struct((width - 2 * BLOCK, width), bf16),
-        ),
-        in_specs=[in_vmem] * 7,
-        out_specs=(in_vmem,) * 5 + (pl.BlockSpec(memory_space=pl.ANY), in_vmem),
-        scratch_shapes=[
-            vmem((n_rays, inner), bf16),
-            vmem((n_rays, inner), bf16),
-            vmem((2, width, WIDE), bf16),
-            vmem((2, WIDE, width), bf16),
-            vmem((2 * BLOCK, width), bf16),
-            pltpu.SemaphoreType.DMA((2, 2)),
-            pltpu.SemaphoreType.DMA((2,)),
-        ],
-        compiler_params=pltpu.CompilerParams(vmem_limit_bytes=40 << 20),
-        name="mlp",
-    )(attended, rays, cotangent, rows, w_out, w_up, w_down)
 
 
 MESH = pl.DeviceIdType.MESH
@@ -1043,18 +915,35 @@
     rays_ref,
     lat_ref,
     scene_ref,
-    rows_ref,
+    up_bias_ref,
+    gain_ref,
+    bias_ref,
+    q_bias_ref,
+    v_bias_ref,
+    out_bias_ref,
+    down_bias_ref,
     wq_ref,
     wk_ref,
     wv_ref,
+    cot_hbm,
+    wo_hbm,
+    wu_hbm,
+    wd_hbm,
     all_ref,
     k_ref,
     kt_ref,
     v_ref,
     q_ref,
     shifted_ref,
-    att_ref,
     lse_ref,
+    rows_ref,
+    result_ref,
+    gh_ref,
+    ga_ref,
+    dots_ref,
+    small_ref,
+    early_hbm,
+    rest_ref,
     full,
     all_own,
     k_own,
@@ -1065,9 +954,22 @@
     tops,
     totals,
     mixed,
+    att_ref,
+    cot_ref,
+    wo_ref,
+    wu_ref,
+    wd_ref,
+    active_ref,
+    gpre_ref,
+    gu_slot,
+    gd_slot,
+    go_slot,
     z_sem,
     y_sem,
     out_sem,
+    weight_sem,
+    early_sem,
+    go_sem,
 ):
     place = Place(n_seq, n_ray)
     fast_bits = place.fast_bits[::-1]
@@ -1099,6 +1001,19 @@
     for half in range(2):
         fast_copy(0, place.slow, half).start()
         spread(half).step(0)
+
+    weight_loads = [
+        pltpu.make_async_copy(source, target, weight_sem.at[n])
+        for n, (source, target) in enumerate(
+            ((wo_hbm, wo_ref), (wu_hbm, wu_ref), (wd_hbm, wd_ref), (cot_hbm, cot_ref))
+        )
+    ]
+    for load in weight_loads:
+        load.start()
+    for n, vector in enumerate((gain_ref, bias_ref, q_bias_ref, v_bias_ref, out_bias_ref)):
+        rows_ref[n : n + 1, :] = vector[...].astype(f32).reshape(1, width)
+    rows_ref[5:7, :] = up_bias_ref[...].astype(f32)
+    rows_ref[7:8, :] = down_bias_ref[...].astype(f32).reshape(1, width)
 
     inputs = rays_ref[...].astype(f32)
     centred = inputs - jnp.mean(inputs, axis=1, keepdims=True)
@@ -1115,31 +1030,41 @@
     def attend(chunk):
         seg_ref[...] = segments(lengths, chunk * group, group)
 
-        def one_tile(t, carry):
-            ray_rows = pl.ds(pl.multiple_of(t * TILE, TILE), TILE)
-            seen = seg_ref[...] == scene_ref[pl.ds(t, 1), :]
+        def some_tiles(n, carry):
+            own_tiles = [n * FORWARD + i for i in range(FORWARD)]
+            scenes = jnp.concatenate([scene_ref[pl.ds(t, 1), :] for t in own_tiles], axis=1)
+            seen = jnp.concatenate([seg_ref[...]] * FORWARD, axis=1) == scenes
+            scores, old, new = [], [], []
             for g in range(groups):
-                s = matmul(k_own[chunk, :, group_at(g)], spread_heads(q_ref[ray_rows, group_at(g)]), 1, 1)
-                s = jnp.where(seen, s, masked_score)
-                old = tops[g, t]
-                new = jnp.maximum(old, jnp.max(fold_rows(s, jnp.max), axis=0, keepdims=True))
-                e = jnp.exp(s - new[0:1])
-                fix = jnp.exp(old - new)
-                tops[g, t] = new
-                totals[g, t] = totals[g, t] * fix + fold_rows(e, jnp.sum)
-                mixed[g, t] = mixed[g, t] * fix[0:1] + matmul(vt_own[chunk, group_at(g), :], e.astype(bf16), 1, 0)
+                spread_q = [
+                    spread_heads(q_ref[pl.ds(pl.multiple_of(t * TILE, TILE), TILE), group_at(g)]) for t in own_tiles
+                ]
+                s = matmul(k_own[:, group_at(g)], jnp.concatenate(spread_q, axis=0), 1, 1)
+                scores.append(jnp.where(seen, s, masked_score))
+                old.append(jnp.concatenate([tops[g, t] for t in own_tiles], axis=1))
+                new.append(jnp.maximum(old[g], jnp.max(fold_rows(scores[g], jnp.max), axis=0, keepdims=True)))
+            for g in range(groups):
+                fix = jnp.exp(old[g] - new[g])
+                e = jnp.exp(scores[g] - new[g][0:1])
+                total = fold_rows(e, jnp.sum)
+                mix = matmul(vt_own[group_at(g), :], e.astype(bf16), 1, 0)
+                for i, t in enumerate(own_tiles):
+                    cut = group_at(i)
+                    tops[g, t] = new[g][:, cut]
+                    totals[g, t] = totals[g, t] * fix[:, cut] + total[:, cut]
+                    mixed[g, t] = mixed[g, t] * fix[0:1, cut] + mix[:, cut]
             return carry
 
-        lax.fori_loop(0, tiles, one_tile, 0)
+        lax.fori_loop(0, tiles // FORWARD, some_tiles, 0)
 
     def results(chunk):
         rows = pl.ds(pl.multiple_of(chunk * group, 16), group)
         columns = pl.ds(pl.multiple_of(chunk * group, 128), group)
         return [
-            (k_own.at[chunk], k_ref.at[rows]),
-            (kt_own.at[chunk], kt_ref.at[:, columns]),
-            (v_own.at[chunk], v_ref.at[rows]),
-            (all_own.at[chunk], all_ref.at[:, columns]),
+            (k_own, k_ref.at[rows]),
+            (kt_own, kt_ref.at[:, columns]),
+            (v_own, v_ref.at[rows]),
+            (all_own, all_ref.at[:, columns]),
         ]
 
     def project(chunk):
@@ -1150,15 +1075,17 @@
                     fast_copy(i + 1, chunk, half).start()
         latents = full[chunk].reshape(group, width)
         keys = matmul(latents, wk_ref[...], 1, 0).astype(bf16)
-        k_own[chunk] = keys
-        all_own[chunk] = latents.T
-        kt_own[chunk] = keys.T
+        k_own[...] = keys
+        all_own[...] = latents.T
+        kt_own[...] = keys.T
         values = (matmul(latents, wv_ref[...], 1, 0) + rows_ref[3:4, :]).astype(bf16)
-        v_own[chunk] = values
-        vt_own[chunk] = values.T
+        v_own[...] = values
+        vt_own[...] = values.T
         for n, (source, target) in enumerate(results(chunk)):
-            pltpu.make_async_copy(source, target, out_sem.at[n, chunk]).start()
+            pltpu.make_async_copy(source, target, out_sem.at[n]).start()
         attend(chunk)
+        for n, (source, target) in enumerate(results(chunk)):
+            pltpu.make_async_copy(source, target, out_sem.at[n]).wait()
 
     def visit(index, carry):
         t, way = index // 2, index % 2
@@ -1191,17 +1118,91 @@
             att_ref[t * TILE : (t + 1) * TILE, group_at(g)] = fold_heads(mixed[g, t] * (1.0 / total))
             lse_ref[t : t + 1, group_at(g)] = tops[g, t][0:1] + jnp.log(total)
 
-    def end(chunk, carry):
-        for n, (source, target) in enumerate(results(chunk)):
-            pltpu.make_async_copy(source, target, out_sem.at[n, chunk]).wait()
-        return carry
-
-    lax.fori_loop(0, SLOW, end, 0)
+    attended = att_ref[...].astype(bf16)
+    weight_loads[0].wait()
+    hidden = rays_ref[...].astype(f32) + matmul(attended, wo_ref[...], 1, 0) + rows_ref[4:5, :]
+    hidden_low = hidden.astype(bf16)
+    hidden_turned = hidden_low.T
+    weight_loads[3].wait()
+    cot = cot_ref[...]
+    inner = wu_ref.shape[1]
+    blocks = inner // WIDE
+    weight_loads[1].wait()
+    weight_loads[2].wait()
+    per_half = blocks // 2
+
+    def early_copies(n):
+        half, part = n // per_half, n % per_half
+        slot = n % 2
+        return (
+            pltpu.make_async_copy(
+                gu_slot.at[slot], early_hbm.at[half, pl.ds(0, width), pl.ds(part * WIDE, WIDE)], early_sem.at[0, slot]
+            ),
+            pltpu.make_async_copy(
+                gd_slot.at[slot], early_hbm.at[half, pl.ds(width + part * WIDE, WIDE)], early_sem.at[1, slot]
+            ),
+        )
+
+    for n in range(blocks):
+        at = slice(n * WIDE, (n + 1) * WIDE)
+        bias_row, bias_at = 5 + n * WIDE // width, slice(n * WIDE % width, n * WIDE % width + WIDE)
+        pre = matmul(hidden_low, wu_ref[:, at], 1, 0) + rows_ref[bias_row : bias_row + 1, bias_at]
+        active, slope = gelu_both(pre)
+        active = active.astype(bf16)
+        active_ref[:, at] = active
+        grad_pre = (matmul(cot, wd_ref[at, :], 1, 1) * slope).astype(bf16)
+        gpre_ref[:, at] = grad_pre
+        small_ref[bias_row - 4 : bias_row - 3, bias_at] = jnp.sum(grad_pre.astype(f32), axis=0, keepdims=True)
+        if n >= 2:
+            for copy in early_copies(n - 2):
+                copy.wait()
+        gu_slot[n % 2] = matmul(hidden_turned, grad_pre, 1, 0).astype(bf16)
+        gd_slot[n % 2] = matmul(active, cot, 0, 0).astype(bf16)
+        for copy in early_copies(n):
+            copy.start()
+    result_ref[...] = (hidden + matmul(active_ref[...], wd_ref[...], 1, 0) + rows_ref[7:8, :]).astype(bf16)
+    grad_top = cot.astype(f32)
+    small_ref[3:4, :] = jnp.sum(grad_top, axis=0, keepdims=True)
+    grad_hidden = grad_top + matmul(gpre_ref[...], wu_ref[...], 1, 1)
+    gh_ref[...] = grad_hidden
+    grad_branch = grad_hidden.astype(bf16)
+    small_ref[0:1, :] = jnp.sum(grad_branch.astype(f32), axis=0, keepdims=True)
+    small_ref[4:8, :] = jnp.zeros((4, width), f32)
+    grad_out = matmul(attended, grad_branch, 0, 0).astype(bf16)
+    go_slot[...] = grad_out[: 2 * BLOCK]
+    go_copies = [
+        pltpu.make_async_copy(
+            go_slot.at[pl.ds(c * BLOCK, BLOCK)], early_hbm.at[c, pl.ds(2 * width, BLOCK)], go_sem.at[c]
+        )
+        for c in range(2)
+    ]
+    for copy in go_copies:
+        copy.start()
+    rest_ref[...] = grad_out[2 * BLOCK :]
+    grad_attended = matmul(grad_branch, wo_ref[...], 1, 1).astype(bf16)
+    ga_ref[...] = grad_attended
+    product = grad_attended.astype(f32) * att_ref[...]
+    for t in range(dots_ref.shape[0]):
+        for g in range(width // WIDE):
+            dots_ref[t : t + 1, group_at(g)] = lax.dot_general(
+                jnp.ones((8, WIDE), f32),
+                spread_heads(product[t * TILE : (t + 1) * TILE, group_at(g)]),
+                (((1,), (1,)), ((), ())),
+                precision=lax.Precision.HIGHEST,
+                preferred_element_type=f32,
+            )[0:1, :]
+    for copy in early_copies(blocks - 2) + early_copies(blocks - 1) + tuple(go_copies):
+        copy.wait()
+
+
     for half in range(2):
         spread(half).drain()
 
 
-def gather_and_attend(n_seq, n_ray, rays, latents, lengths, scene_rows, rows, w_query, w_key, w_value):
+def gather_and_attend(
+    n_seq, n_ray, rays, latents, lengths, scene_rows, vectors, w_query, w_key, w_value, cotangent, w_out, w_up, w_down
+):
+    inner = w_up.shape[1]
     block, width = latents.shape
     n_rays = rays.shape[0]
     n_fast = n_ray // SLOW
@@ -1224,29 +1225,73 @@
             tall,
             struct((n_rays, width), bf16),
             struct((n_rays, width), bf16),
+            struct((tiles, width), f32),
+            struct((8, width), f32),
+            struct((n_rays, width), bf16),
             struct((n_rays, width), f32),
+            struct((n_rays, width), bf16),
             struct((tiles, width), f32),
+            struct((8, width), f32),
+            struct((2, 2 * width + BLOCK, width), bf16),
+            struct((width - 2 * BLOCK, width), bf16),
         ),
-        in_specs=[pl.BlockSpec(memory_space=pltpu.SMEM)] + [in_vmem] * 7,
-        out_specs=(anywhere,) * 4 + (in_vmem,) * 4,
+        in_specs=[pl.BlockSpec(memory_space=pltpu.SMEM)] + [in_vmem] * 13 + [anywhere] * 4,
+        out_specs=(anywhere,) * 4 + (in_vmem,) * 9 + (anywhere, in_vmem),
         scratch_shapes=[
             vmem((SLOW, n_fast, block, width), bf16),
-            vmem((SLOW, width, group), bf16),
-            vmem((SLOW, group, width), bf16),
-            vmem((SLOW, width, group), bf16),
-            vmem((SLOW, group, width), bf16),
-            vmem((SLOW, width, group), bf16),
+            vmem((width, group), bf16),
+            vmem((group, width), bf16),
+            vmem((width, group), bf16),
+            vmem((group, width), bf16),
+            vmem((width, group), bf16),
             vmem((group, WIDE), f32),
             vmem((groups, tiles, 8, WIDE), f32),
             vmem((groups, tiles, 8, WIDE), f32),
             vmem((groups, tiles, WIDE, WIDE), f32),
+            vmem((n_rays, width), f32),
+            vmem((n_rays, width), bf16),
+            vmem((width, width), bf16),
+            vmem((width, inner), bf16),
+            vmem((inner, width), bf16),
+            vmem((n_rays, inner), bf16),
+            vmem((n_rays, inner), bf16),
+            vmem((2, width, WIDE), bf16),
+            vmem((2, WIDE, width), bf16),
+            vmem((2 * BLOCK, width), bf16),
             sem((2, 2, 2, SLOW - 1)),
             sem((2, fast_bits, SLOW, 2)),
-            sem((4, SLOW)),
+            sem((4,)),
+            sem((4,)),
+            sem((2, 2)),
+            sem((2,)),
         ],
-        compiler_params=pltpu.CompilerParams(collective_id=0, has_side_effects=True, vmem_limit_bytes=58 << 20),
+        compiler_params=pltpu.CompilerParams(collective_id=0, has_side_effects=True, vmem_limit_bytes=62 << 20),
         name="gather_and_attend",
-    )(lengths, rays, latents, scene_rows, rows, w_query, w_key, w_value)
+    )(lengths, rays, latents, scene_rows, *vectors, w_query, w_key, w_value, cotangent, w_out, w_up, w_down)
+
+
+def widen_kernel(*refs):
+    sums, vectors, wide, lines = refs[:6], refs[6], refs[7:13], refs[13:]
+    for source, target in zip(sums, wide):
+        target[...] = source[...].astype(f32)
+    for n, line in enumerate(lines):
+        line[...] = vectors[n, :]
+
+
+def widen(sums, vectors):
+    steps = 6
+    width = vectors.shape[1]
+    struct = jax.ShapeDtypeStruct
+    blocks = [pl.BlockSpec((a.shape[0] // steps, a.shape[1]), lambda i: (i, 0)) for a in sums]
+    return pl.pallas_call(
+        widen_kernel,
+        grid=(steps,),
+        out_shape=tuple(struct(a.shape, f32) for a in sums) + (struct((width,), f32),) * vectors.shape[0],
+        in_specs=blocks + [pl.BlockSpec(vectors.shape, lambda i: (0, 0))],
+        out_specs=tuple(blocks) + (pl.BlockSpec((width,), lambda i: (0,)),) * vectors.shape[0],
+        compiler_params=pltpu.CompilerParams(vmem_limit_bytes=62 << 20),
+        name="widen",
+    )(*sums, vectors)
 
 
 def local(
@@ -1272,14 +1317,41 @@
     width = rays.shape[1]
     n_seq, n_ray = lax.axis_size("seq"), lax.axis_size("ray")
     tiles = rays.shape[0] // TILE
-    names = (ln_gain, ln_bias, b_query, b_value, b_out, b_up, b_down)
-    rows = jnp.concatenate([v.reshape(-1, width) for v in names]).astype(f32)
+    vectors = (b_up.reshape(-1, width), ln_gain, ln_bias, b_query, b_value, b_out, b_down)
     scene_rows = jnp.broadcast_to(scenes.reshape(tiles, 1, TILE), (tiles, PACK, TILE)).reshape(tiles, WIDE).astype(f32)
-    all_t, keys, keys_t, values, queries, shifted, attended, lse = gather_and_attend(
-        n_seq, n_ray, rays, latents, lengths, scene_rows, rows, w_query, w_key, w_value
+    (
+        all_t,
+        keys,
+        keys_t,
+        values,
+        queries,
+        shifted,
+        lse,
+        rows,
+        result,
+        grad_hidden,
+        grad_attended,
+        dots,
+        small,
+        early,
+        rest,
+    ) = gather_and_attend(
+        n_seq,
+        n_ray,
+        rays,
+        latents,
+        lengths,
+        scene_rows,
+        vectors,
+        w_query,
+        w_key,
+        w_value,
+        cotangent,
+        w_out,
+        w_up,
+        w_down,
     )
-    result, grad_hidden, grad_attended, dots, small, early, rest = mlp(attended, rays, cotangent, rows, w_out, w_up, w_down)
-    sum_q, sum_k, sum_v, sum_o, sum_u, sum_d, grad_latents, grad_rays, vectors = back_and_sum(
+    sum_q, sum_k, sum_v, sum_o, sum_u, sum_d, grad_latents, grad_rays, small_sums = back_and_sum(
         n_seq,
         n_ray,
         latents.shape[0],
@@ -1304,23 +1376,25 @@
         values,
         all_t,
     )
+    wide = widen((sum_q, sum_k, sum_v, sum_o, sum_u, sum_d), small_sums)
+    lines = wide[6:]
     return (
         result,
         grad_rays,
         grad_latents,
-        vectors[4],
-        vectors[5],
-        sum_q.astype(f32),
-        vectors[6],
-        sum_k.astype(f32),
-        sum_v.astype(f32),
-        vectors[7],
-        sum_o.astype(f32),
-        vectors[0],
-        sum_u.astype(f32),
-        vectors[1:3].reshape(-1),
-        sum_d.astype(f32),
-        vectors[3],
+        lines[4],
+        lines[5],
+        wide[0],
+        lines[6],
+        wide[1],
+        wide[2],
+        lines[7],
+        wide[3],
+        lines[0],
+        wide[4],
+        jnp.concatenate(lines[1:3]),
+        wide[5],
+        lines[3],
     )
 
 

time: 300 us -> 271 us (0.903)
  local copies, waits for them, and re-layouts: 21.4 us -> 4.89 us
  other arithmetic: 14.2 us -> 2.09 us
    convert_element_type x7 -> x0, other arithmetic: 13.6 us -> none  [the longest x1 2.85 us: local(): sum_q.astype(f32)]
    unnamed x40 -> x9, local copies, waits for them, and re-layouts: 12.8 us -> 2.85 us
    pallas_call x1, Pallas kernels: 78.8 us -> 86.1 us  [gather_and_attend(): pl.pallas_call(functools.partial(gather_kernel, n_seq, n_ray), out_shape=...]
    reshape x8 -> x1, local copies, waits for them, and re-layouts: 5.42 us -> 1.28 us  [local(): b_up.reshape(-1, width)]
    pallas_call x1, Pallas kernels: 169 us -> 166 us  [back_and_sum(): pl.pallas_call(functools.partial(sum_kernel, n_seq, n_ray, units), out_sh...]
    pallas_call x1, Pallas kernels: 14.4 us -> 11.1 us  [widen(): pl.pallas_call(widen_kernel, grid=(steps,), out_shape=tuple((struct(a.sha...]
where the time goes in v6:
time: 271 us; the launch traced here: 270 us
  Pallas kernels  263 us (97%)
  local copies, waits for them, and re-layouts  4.89 us (2%)
    pallas_call x1, Pallas kernels, back_and_sum(): pl.pallas_call(functools.partial(sum_kernel, n_seq, n_ray, units), out_sh...  166 us
    pallas_call x1, Pallas kernels, gather_and_attend(): pl.pallas_call(functools.partial(gather_kernel, n_seq, n_ray), out_shape=...  86.1 us
    pallas_call x1, Pallas kernels, widen(): pl.pallas_call(widen_kernel, grid=(steps,), out_shape=tuple((struct(a.sha...  11.1 us

profile of v6, /device:TPU:0, one launch (start us, length us, event | category | flops | bytes accessed | tf_op | source)
XLA Modules:
  0.0 270.4 jit_solution(12624151587967427738)
XLA Ops:
  0.6 0.7 convert_element_type.7
  1.3 0.1 convert_element_type.8
  1.4 1.3 reshape.40.up_bias_ref
  2.7 0.7 convert_element_type.9.scene_ref
  3.4 86.1 %gather_and_attend.1 = (bf16[768,3072]{1,0:T(8,128)(2,1)}, bf16[3072,768]{1,0:T(8,128)(2,1)}, bf16[768,3072]{1,0:T(8,128)(2,1)}, bf16[3072,768]{1,0:T(8,128)(2,1...) custom-call(s32[1,3]{1,0:T(1,128)} %lengths.3, ...), custom_call_target="tpu_custom_call" | custom-call | tf_op jit(solution)/shard_map/gather_and_attend/pallas_call | solution.py:1219
  89.5 165.6 %back_and_sum.1 = (bf16[768,768]{1,0:T(8,128)(2,1)}, bf16[768,768]{1,0:T(8,128)(2,1)}, bf16[768,768]{1,0:T(8,128)(2,1)}, bf16[768,768]{1,0:T(8,128)(2,1)}, bf16[...) custom-call(s32[1,3]{1,0:T(1,128)} %lengths.3, ...), custom_call_target="tpu_custom_call" | custom-call | tf_op jit(solution)/shard_map/back_and_sum/pallas_call | solution.py:836
  255.0 0.0 copy-start.2
  255.0 0.0 copy-start.1
  255.1 11.1 %widen.1 = (f32[768,768]{1,0:T(8,128)}, f32[768,768]{1,0:T(8,128)}, f32[768,768]{1,0:T(8,128)}, f32[768,768]{1,0:T(8,128)}, f32[768,1536]{1,0:T(8,128)}, /*index...) custom-call(bf16[768,768]{1,0:T(8,128)(2,1)} %get-tuple-element.71.r, ...), custom_call_target="tpu_custom_call" | custom-call | tf_op jit(solution)/shard_map/widen/pallas_call | solution.py:1286
  266.2 0.0 copy-start
  266.2 1.4 pad_maximum_fusion
  267.6 0.0 copy-done.2
  267.6 0.8 copy.37
  268.4 0.0 copy-done.1
  268.4 1.0 copy.38
  269.4 0.0 copy-done
  269.4 1.0 copy.39
  (1 shorter events, 0.0 us)
Async XLA Ops:
  255.0 12.6 %copy-start.2 = (bf16[384,768]{1,0:T(8,128)(2,1)S(1)}, bf16[384,768]{1,0:T(8,128)(2,1)}, u32[]{:S(2)}) copy-start(bf16[384,768]{1,0:T(8,128)(2,1)} %get-tuple-element.108) | copy-start | bytes 1769476
  255.0 13.4 %copy-start.1 = (f32[384,768]{1,0:T(8,128)S(1)}, f32[384,768]{1,0:T(8,128)}, u32[]{:S(2)}) copy-start(f32[384,768]{1,0:T(8,128)} %get-tuple-element.109) | copy-start | bytes 3538948
  266.2 3.3 %copy-start = (f32[384,768]{1,0:T(8,128)S(1)}, f32[384,768]{1,0:T(8,128)}, u32[]{:S(2)}) copy-start(f32[384,768]{1,0:T(8,128)} %get-tuple-element.110) | copy-start | bytes 3538948

commit v7 on v6

--- a/solution.py
+++ b/solution.py
@@ -239,11 +239,6 @@
     n_ray,
     units,
     lengths,
-    wq_ref,
-    wk_ref,
-    wv_ref,
-    shifted_ref,
-    rays_ref,
     rows_ref,
     small_ref,
     q_ref,
@@ -252,6 +247,11 @@
     dots_ref,
     scene_ref,
     rest_ref,
+    wq_hbm,
+    wk_hbm,
+    wv_hbm,
+    shifted_hbm,
+    rays_hbm,
     gh_hbm,
     early_hbm,
     k_hbm,
@@ -267,6 +267,11 @@
     glat_ref,
     grays_ref,
     small_out,
+    wq_ref,
+    wk_ref,
+    wv_ref,
+    shifted_ref,
+    rays_ref,
     k_slot,
     kt_slot,
     v_slot,
@@ -318,6 +323,18 @@
     early_load.start()
     gh_load = pltpu.make_async_copy(gh_hbm, grays_ref, early_sem.at[1])
     gh_load.start()
+    late_loads = [
+        pltpu.make_async_copy(source, target, early_sem.at[2 + n])
+        for n, (source, target) in enumerate(
+            (
+                (wq_hbm, wq_ref),
+                (wk_hbm, wk_ref),
+                (wv_hbm, wv_ref),
+                (shifted_hbm, shifted_ref),
+                (rays_hbm, rays_ref),
+            )
+        )
+    ]
     greet(place, [core_pair] + halvings)
 
     def base(u, stages):
@@ -667,6 +684,11 @@
             for load in slot_loads(k + 1):
                 load.start()
 
+        @pl.when(k == 0)
+        def _():
+            for load in late_loads:
+                load.wait()
+
         grads_kv[...] = sum_kv[...].astype(bf16)
         total = matmul(grads_kv[0], wk_ref[...], 1, 1) + matmul(grads_kv[1], wv_ref[...], 1, 1)
         lat[chunk_of(k)] = total.astype(bf16).reshape(n_fast, block, width)
@@ -734,7 +756,7 @@
         small_now[0, 5:6] = jnp.sum(grad_shifted, axis=0, keepdims=True)
         small_now[0, 6:7] = jnp.sum(gq_ref[...].astype(f32), axis=0, keepdims=True)
 
-    for load in slot_loads(0):
+    for load in slot_loads(0) + tuple(late_loads):
         load.start()
     turned_q[...] = jnp.zeros_like(turned_q)
     weights_kv[...] = jnp.zeros_like(weights_kv)
@@ -743,10 +765,11 @@
 
     steps = SLOW * per_chunk
     late_start = steps if units > 1 else steps + 3
-    finish = [key_terms, query_terms, query_weight_terms, ray_terms, start_small]
-    work = {steps + n: [run] for n, run in enumerate(finish)}
+    finish = [key_terms, query_terms, query_weight_terms, ray_terms]
+    work = {steps - 1 + n: [run] for n, run in enumerate(finish)}
     for i in range(len(exchanges)):
         work.setdefault(steps + len(finish) + i, []).append(join_small(i))
+    work[steps + len(finish) - 2].append(start_small)
     lat_wait = LAT_WAIT
     late_waits = [0, LATE_CORE] + [LATE_X] + [LATE_STEP] * (len(stages) - 5) + [LATE_X, 1]
     late_at = [sum(late_waits[: n + 1]) for n in range(len(stages))]
@@ -754,34 +777,34 @@
     beats = max(late_start + units - early_units + late_at[-1], lat_span, max(work) + 1)
 
     def one_beat(now, carry):
+        for s in range(len(stages)):
+            early = now - EARLY_WAIT * s
+            late = now - late_start - late_at[s]
+            u = jnp.where(late >= 0, late + early_units, early)
+
+            @pl.when(((late >= 0) & (u < units)) | ((early >= 0) & (early < early_units)))
+            def _(u=u, s=s):
+                for run in stages[s]:
+                    run(u)
+
+        for s in range(len(lat_stages)):
+            ahead = now - per_chunk - lat_wait * s
+            m = ahead // per_chunk * 2 + ahead % per_chunk
+
+            @pl.when((ahead >= 0) & (ahead % per_chunk < 2) & (m < 2 * SLOW))
+            def _(m=m, s=s):
+                lat_stages[s](m)
+
+        @pl.when(now < steps)
+        def _():
+            attend(now)
+
         for beat, runs in work.items():
 
             @pl.when(now == beat)
             def _(runs=runs):
                 for run in runs:
                     run()
-
-        for s in range(len(stages)):
-            early = now - EARLY_WAIT * s
-            late = now - late_start - late_at[s]
-            u = jnp.where(late >= 0, late + early_units, early)
-
-            @pl.when(((late >= 0) & (u < units)) | ((early >= 0) & (early < early_units)))
-            def _(u=u, s=s):
-                for run in stages[s]:
-                    run(u)
-
-        for s in range(len(lat_stages)):
-            ahead = now - per_chunk - lat_wait * s
-            m = ahead // per_chunk * 2 + ahead % per_chunk
-
-            @pl.when((ahead >= 0) & (ahead % per_chunk < 2) & (m < 2 * SLOW))
-            def _(m=m, s=s):
-                lat_stages[s](m)
-
-        @pl.when(now < steps)
-        def _():
-            attend(now)
 
         return carry
 
@@ -846,9 +869,14 @@
             struct((n_rays, width), f32),
             struct((8, width), f32),
         ),
-        in_specs=[pl.BlockSpec(memory_space=pltpu.SMEM)] + [in_vmem] * 13 + [anywhere] * 6,
+        in_specs=[pl.BlockSpec(memory_space=pltpu.SMEM)] + [in_vmem] * 8 + [anywhere] * 11,
         out_specs=(anywhere,) * 6 + (in_vmem,) * 3,
         scratch_shapes=[
+            vmem((width, width), bf16),
+            vmem((width, width), bf16),
+            vmem((width, width), bf16),
+            vmem((n_rays, width), bf16),
+            vmem((n_rays, width), bf16),
             vmem((group, width), bf16),
             vmem((width, group), bf16),
             vmem((group, width), bf16),
@@ -869,7 +897,7 @@
             vmem((2, 2, SLOW - 1, half, width), bf16),
             vmem((exchanges + 1, 8, width), f32),
             vmem((exchanges, 8, width), f32),
-            sem((2,)),
+            sem((7,)),
             sem((4,)),
             sem((2, 2, units)),
             sem((2, halvings, units)),
@@ -886,11 +914,6 @@
         name="back_and_sum",
     )(
         lengths,
-        w_query,
-        w_key,
-        w_value,
-        shifted,
-        rays,
         rows,
         small,
         queries,
@@ -899,6 +922,11 @@
         dots,
         scene_rows,
         rest,
+        w_query,
+        w_key,
+        w_value,
+        shifted,
+        rays,
         gh,
         early,
         keys,
@@ -912,9 +940,8 @@
     n_seq,
     n_ray,
     lengths,
-    rays_ref,
     lat_ref,
-    scene_ref,
+    scenes_ref,
     up_bias_ref,
     gain_ref,
     bias_ref,
@@ -922,9 +949,10 @@
     v_bias_ref,
     out_bias_ref,
     down_bias_ref,
-    wq_ref,
-    wk_ref,
-    wv_ref,
+    rays_hbm,
+    wq_hbm,
+    wk_hbm,
+    wv_hbm,
     cot_hbm,
     wo_hbm,
     wu_hbm,
@@ -936,6 +964,7 @@
     q_ref,
     shifted_ref,
     lse_ref,
+    scene_ref,
     rows_ref,
     result_ref,
     gh_ref,
@@ -955,6 +984,10 @@
     totals,
     mixed,
     att_ref,
+    rays_ref,
+    wq_ref,
+    wk_ref,
+    wv_ref,
     cot_ref,
     wo_ref,
     wu_ref,
@@ -973,11 +1006,30 @@
 ):
     place = Place(n_seq, n_ray)
     fast_bits = place.fast_bits[::-1]
+    weight_loads = [
+        pltpu.make_async_copy(source, target, weight_sem.at[n])
+        for n, (source, target) in enumerate(
+            (
+                (wo_hbm, wo_ref),
+                (wu_hbm, wu_ref),
+                (wd_hbm, wd_ref),
+                (cot_hbm, cot_ref),
+                (rays_hbm, rays_ref),
+                (wq_hbm, wq_ref),
+                (wk_hbm, wk_ref),
+                (wv_hbm, wv_ref),
+            )
+        )
+    ]
+    for load in weight_loads[4:] + weight_loads[:4]:
+        load.start()
     greet(place, place.fast_bits)
     block, width = lat_ref.shape
     half_rows = block // 2
     group = place.n_fast * block
     full[place.slow, place.fast] = lat_ref[...]
+    step = k_own.shape[0]
+    by_block = step == block
 
     def half_at(half):
         return pl.ds(half * half_rows, half_rows)
@@ -1002,19 +1054,19 @@
         fast_copy(0, place.slow, half).start()
         spread(half).step(0)
 
-    weight_loads = [
-        pltpu.make_async_copy(source, target, weight_sem.at[n])
-        for n, (source, target) in enumerate(
-            ((wo_hbm, wo_ref), (wu_hbm, wu_ref), (wd_hbm, wd_ref), (cot_hbm, cot_ref))
-        )
-    ]
-    for load in weight_loads:
-        load.start()
     for n, vector in enumerate((gain_ref, bias_ref, q_bias_ref, v_bias_ref, out_bias_ref)):
         rows_ref[n : n + 1, :] = vector[...].astype(f32).reshape(1, width)
-    rows_ref[5:7, :] = up_bias_ref[...].astype(f32)
+    up_bias = up_bias_ref[...].astype(f32).reshape(1, -1)
+    for n in range(2):
+        rows_ref[5 + n : 6 + n, :] = up_bias[:, n * width : (n + 1) * width]
     rows_ref[7:8, :] = down_bias_ref[...].astype(f32).reshape(1, width)
 
+    scenes = scenes_ref[...].astype(f32).reshape(1, -1)
+    for t in range(scene_ref.shape[0]):
+        scene_ref[t : t + 1, :] = jnp.concatenate([scenes[:, t * TILE : (t + 1) * TILE]] * PACK, axis=1)
+
+    for load in weight_loads[4:]:
+        load.wait()
     inputs = rays_ref[...].astype(f32)
     centred = inputs - jnp.mean(inputs, axis=1, keepdims=True)
     inverse = lax.rsqrt(jnp.mean(centred * centred, axis=1, keepdims=True) + 1e-05)
@@ -1027,8 +1079,8 @@
     totals[...] = jnp.zeros_like(totals)
     mixed[...] = jnp.zeros_like(mixed)
 
-    def attend(chunk):
-        seg_ref[...] = segments(lengths, chunk * group, group)
+    def attend(first):
+        seg_ref[...] = segments(lengths, first, step)
 
         def some_tiles(n, carry):
             own_tiles = [n * FORWARD + i for i in range(FORWARD)]
@@ -1057,9 +1109,9 @@
 
         lax.fori_loop(0, tiles // FORWARD, some_tiles, 0)
 
-    def results(chunk):
-        rows = pl.ds(pl.multiple_of(chunk * group, 16), group)
-        columns = pl.ds(pl.multiple_of(chunk * group, 128), group)
+    def results(first):
+        rows = pl.ds(pl.multiple_of(first, 16), step)
+        columns = pl.ds(pl.multiple_of(first, 128), step)
         return [
             (k_own, k_ref.at[rows]),
             (kt_own, kt_ref.at[:, columns]),
@@ -1067,13 +1119,18 @@
             (all_own, all_ref.at[:, columns]),
         ]
 
-    def project(chunk):
+    def await_fast(chunk):
         for half in range(2):
             for i in range(len(fast_bits)):
                 fast_copy(i, chunk, half).wait()
                 if i + 1 < len(fast_bits):
                     fast_copy(i + 1, chunk, half).start()
-        latents = full[chunk].reshape(group, width)
+
+    def project(chunk, fast):
+        if by_block:
+            first, latents = chunk * group + fast * block, full[chunk, fast]
+        else:
+            first, latents = chunk * group, full[chunk].reshape(group, width)
         keys = matmul(latents, wk_ref[...], 1, 0).astype(bf16)
         k_own[...] = keys
         all_own[...] = latents.T
@@ -1081,17 +1138,17 @@
         values = (matmul(latents, wv_ref[...], 1, 0) + rows_ref[3:4, :]).astype(bf16)
         v_own[...] = values
         vt_own[...] = values.T
-        for n, (source, target) in enumerate(results(chunk)):
+        for n, (source, target) in enumerate(results(first)):
             pltpu.make_async_copy(source, target, out_sem.at[n]).start()
-        attend(chunk)
-        for n, (source, target) in enumerate(results(chunk)):
+        attend(first)
+        for n, (source, target) in enumerate(results(first)):
             pltpu.make_async_copy(source, target, out_sem.at[n]).wait()
 
     def visit(index, carry):
-        t, way = index // 2, index % 2
+        t, across, way = index // 4, index % 4 // 2, index % 2
         for later in range(1, SLOW):
 
-            @pl.when(index == 2 * (later - 1))
+            @pl.when(index == 4 * later)
             def _(later=later):
                 for half in range(2):
                     spread(half).step(later)
@@ -1101,17 +1158,22 @@
                         def _(half=half, to=to):
                             fast_copy(0, chunk_of(to, later), half).start()
 
+        far = t - across
         spot = jnp.where(way == 0, place.slow, SLOW - 1 - place.slow)
-        chunk = jnp.where(way == 0, spot - t, SLOW - 1 - spot + t)
-
-        @pl.when((spot >= t) & (index != 1))
+        chunk = jnp.where(way == 0, spot - far, SLOW - 1 - spot + far)
+        due = (far >= 0) & (far < SLOW) & (spot >= far) & ((far > 0) | (way == 0))
+
+        @pl.when(due & (across == 1))
         def _():
-            project(chunk)
+            await_fast(chunk)
+
+        @pl.when(due & ((across == 1) | by_block))
+        def _():
+            project(chunk, jnp.where(across == 1, flip(place.fast, 1), place.fast))
 
         return carry
 
-    lax.fori_loop(0, 2 * SLOW, visit, 0)
-
+    lax.fori_loop(0, 4 * (SLOW + 1), visit, 0)
     for t in range(tiles):
         for g in range(groups):
             total = jnp.sum(totals[g, t], axis=0, keepdims=True)
@@ -1200,13 +1262,14 @@
 
 
 def gather_and_attend(
-    n_seq, n_ray, rays, latents, lengths, scene_rows, vectors, w_query, w_key, w_value, cotangent, w_out, w_up, w_down
+    n_seq, n_ray, rays, latents, lengths, scenes, vectors, w_query, w_key, w_value, cotangent, w_out, w_up, w_down
 ):
     inner = w_up.shape[1]
     block, width = latents.shape
     n_rays = rays.shape[0]
     n_fast = n_ray // SLOW
     group = n_fast * block
+    step = block if block % 128 == 0 and n_fast == 2 else group
     total = n_ray * block
     tiles, groups = n_rays // TILE, width // WIDE
     fast_bits = len(bits_of(n_fast))
@@ -1226,6 +1289,7 @@
             struct((n_rays, width), bf16),
             struct((n_rays, width), bf16),
             struct((tiles, width), f32),
+            struct((tiles, WIDE), f32),
             struct((8, width), f32),
             struct((n_rays, width), bf16),
             struct((n_rays, width), f32),
@@ -1235,20 +1299,24 @@
             struct((2, 2 * width + BLOCK, width), bf16),
             struct((width - 2 * BLOCK, width), bf16),
         ),
-        in_specs=[pl.BlockSpec(memory_space=pltpu.SMEM)] + [in_vmem] * 13 + [anywhere] * 4,
-        out_specs=(anywhere,) * 4 + (in_vmem,) * 9 + (anywhere, in_vmem),
+        in_specs=[pl.BlockSpec(memory_space=pltpu.SMEM)] + [in_vmem] * 9 + [anywhere] * 8,
+        out_specs=(anywhere,) * 4 + (in_vmem,) * 10 + (anywhere, in_vmem),
         scratch_shapes=[
             vmem((SLOW, n_fast, block, width), bf16),
-            vmem((width, group), bf16),
-            vmem((group, width), bf16),
-            vmem((width, group), bf16),
-            vmem((group, width), bf16),
-            vmem((width, group), bf16),
-            vmem((group, WIDE), f32),
+            vmem((width, step), bf16),
+            vmem((step, width), bf16),
+            vmem((width, step), bf16),
+            vmem((step, width), bf16),
+            vmem((width, step), bf16),
+            vmem((step, WIDE), f32),
             vmem((groups, tiles, 8, WIDE), f32),
             vmem((groups, tiles, 8, WIDE), f32),
             vmem((groups, tiles, WIDE, WIDE), f32),
             vmem((n_rays, width), f32),
+            vmem((n_rays, width), bf16),
+            vmem((width, width), bf16),
+            vmem((width, width), bf16),
+            vmem((width, width), bf16),
             vmem((n_rays, width), bf16),
             vmem((width, width), bf16),
             vmem((width, inner), bf16),
@@ -1261,13 +1329,13 @@
             sem((2, 2, 2, SLOW - 1)),
             sem((2, fast_bits, SLOW, 2)),
             sem((4,)),
-            sem((4,)),
+            sem((8,)),
             sem((2, 2)),
             sem((2,)),
         ],
         compiler_params=pltpu.CompilerParams(collective_id=0, has_side_effects=True, vmem_limit_bytes=62 << 20),
         name="gather_and_attend",
-    )(lengths, rays, latents, scene_rows, *vectors, w_query, w_key, w_value, cotangent, w_out, w_up, w_down)
+    )(lengths, latents, scenes, *vectors, rays, w_query, w_key, w_value, cotangent, w_out, w_up, w_down)
 
 
 def widen_kernel(*refs):
@@ -1279,7 +1347,7 @@
 
 
 def widen(sums, vectors):
-    steps = 6
+    steps = 4
     width = vectors.shape[1]
     struct = jax.ShapeDtypeStruct
     blocks = [pl.BlockSpec((a.shape[0] // steps, a.shape[1]), lambda i: (i, 0)) for a in sums]
@@ -1316,9 +1384,7 @@
 ):
     width = rays.shape[1]
     n_seq, n_ray = lax.axis_size("seq"), lax.axis_size("ray")
-    tiles = rays.shape[0] // TILE
-    vectors = (b_up.reshape(-1, width), ln_gain, ln_bias, b_query, b_value, b_out, b_down)
-    scene_rows = jnp.broadcast_to(scenes.reshape(tiles, 1, TILE), (tiles, PACK, TILE)).reshape(tiles, WIDE).astype(f32)
+    vectors = (b_up, ln_gain, ln_bias, b_query, b_value, b_out, b_down)
     (
         all_t,
         keys,
@@ -1327,6 +1393,7 @@
         queries,
         shifted,
         lse,
+        scene_rows,
         rows,
         result,
         grad_hidden,
@@ -1341,7 +1408,7 @@
         rays,
         latents,
         lengths,
-        scene_rows,
+        scenes,
         vectors,
         w_query,
         w_key,

time: 271 us -> 267 us (0.985)
  no operation moved by 1% of the time
where the time goes in v7:
time: 267 us
  Pallas kernels  262 us (98%)
  local copies, waits for them, and re-layouts  2.85 us (1%)
    pallas_call x1, Pallas kernels, back_and_sum(): pl.pallas_call(functools.partial(sum_kernel, n_seq, n_ray, units), out_sh...  167 us
    pallas_call x1, Pallas kernels, gather_and_attend(): pl.pallas_call(functools.partial(gather_kernel, n_seq, n_ray), out_shape=...  84.9 us
    pallas_call x1, Pallas kernels, widen(): pl.pallas_call(widen_kernel, grid=(steps,), out_shape=tuple((struct(a.sha...  10.3 us

profile of v7, /device:TPU:0, one launch (start us, length us, event | category | flops | bytes accessed | tf_op | source)
XLA Modules:
  0.0 266.7 jit_solution(16660178693098603052)
XLA Ops:
  0.7 84.9 %gather_and_attend.1 = (bf16[768,3072]{1,0:T(8,128)(2,1)}, bf16[3072,768]{1,0:T(8,128)(2,1)}, bf16[768,3072]{1,0:T(8,128)(2,1)}, bf16[3072,768]{1,0:T(8,128)(2,1...) custom-call(s32[1,3]{1,0:T(1,128)} %lengths.3, ...), custom_call_target="tpu_custom_call" | custom-call | tf_op jit(solution)/shard_map/gather_and_attend/pallas_call | solution.py:1282
  85.5 166.6 %back_and_sum.1 = (bf16[768,768]{1,0:T(8,128)(2,1)}, bf16[768,768]{1,0:T(8,128)(2,1)}, bf16[768,768]{1,0:T(8,128)(2,1)}, bf16[768,768]{1,0:T(8,128)(2,1)}, bf16[...) custom-call(s32[1,3]{1,0:T(1,128)} %lengths.3, ...), custom_call_target="tpu_custom_call" | custom-call | tf_op jit(solution)/shard_map/back_and_sum/pallas_call | solution.py:859
  252.1 0.0 copy-start.2
  252.1 0.0 copy-start.1
  252.1 10.3 %widen.1 = (f32[768,768]{1,0:T(8,128)}, f32[768,768]{1,0:T(8,128)}, f32[768,768]{1,0:T(8,128)}, f32[768,768]{1,0:T(8,128)}, f32[768,1536]{1,0:T(8,128)}, /*index...) custom-call(bf16[768,768]{1,0:T(8,128)(2,1)} %get-tuple-element.73.r, ...), custom_call_target="tpu_custom_call" | custom-call | tf_op jit(solution)/shard_map/widen/pallas_call | solution.py:1354
  262.4 0.0 copy-start
  262.4 1.4 pad_maximum_fusion
  263.8 0.0 copy-done.2
  263.8 0.8 copy.37
  264.6 0.0 copy-done.1
  264.6 1.0 copy.38
  265.7 0.0 copy-done
  265.7 1.0 copy.39
Async XLA Ops:
  252.1 11.7 %copy-start.2 = (bf16[384,768]{1,0:T(8,128)(2,1)S(1)}, bf16[384,768]{1,0:T(8,128)(2,1)}, u32[]{:S(2)}) copy-start(bf16[384,768]{1,0:T(8,128)(2,1)} %get-tuple-element.110) | copy-start | bytes 1769476
  252.1 12.5 %copy-start.1 = (f32[384,768]{1,0:T(8,128)S(1)}, f32[384,768]{1,0:T(8,128)}, u32[]{:S(2)}) copy-start(f32[384,768]{1,0:T(8,128)} %get-tuple-element.111) | copy-start | bytes 3538948
  262.4 3.3 %copy-start = (f32[384,768]{1,0:T(8,128)S(1)}, f32[384,768]{1,0:T(8,128)}, u32[]{:S(2)}) copy-start(f32[384,768]{1,0:T(8,128)} %get-tuple-element.112) | copy-start | bytes 3538948

commit v8 on v7

--- a/solution.py
+++ b/solution.py
@@ -766,10 +766,10 @@
     steps = SLOW * per_chunk
     late_start = steps if units > 1 else steps + 3
     finish = [key_terms, query_terms, query_weight_terms, ray_terms]
-    work = {steps - 1 + n: [run] for n, run in enumerate(finish)}
+    work = {steps - 1 + n + (n > 0): [run] for n, run in enumerate(finish)}
     for i in range(len(exchanges)):
-        work.setdefault(steps + len(finish) + i, []).append(join_small(i))
-    work[steps + len(finish) - 2].append(start_small)
+        work.setdefault(steps + len(finish) + 1 + i, []).append(join_small(i))
+    work[steps + len(finish) - 1].append(start_small)
     lat_wait = LAT_WAIT
     late_waits = [0, LATE_CORE] + [LATE_X] + [LATE_STEP] * (len(stages) - 5) + [LATE_X, 1]
     late_at = [sum(late_waits[: n + 1]) for n in range(len(stages))]
@@ -1339,27 +1339,29 @@
 
 
 def widen_kernel(*refs):
-    sums, vectors, wide, lines = refs[:6], refs[6], refs[7:13], refs[13:]
+    sums, vectors, wide, lines = refs[:9], refs[9], refs[10:19], refs[19:]
     for source, target in zip(sums, wide):
-        target[...] = source[...].astype(f32)
+        target[...] = source[...].astype(target.dtype)
     for n, line in enumerate(lines):
         line[...] = vectors[n, :]
 
 
-def widen(sums, vectors):
+def widen(sums, whole, vectors):
     steps = 4
     width = vectors.shape[1]
     struct = jax.ShapeDtypeStruct
-    blocks = [pl.BlockSpec((a.shape[0] // steps, a.shape[1]), lambda i: (i, 0)) for a in sums]
+    blocks = [pl.BlockSpec((a.shape[0] // steps, a.shape[1]), lambda i: (i, 0)) for a in sums + whole]
     return pl.pallas_call(
         widen_kernel,
         grid=(steps,),
-        out_shape=tuple(struct(a.shape, f32) for a in sums) + (struct((width,), f32),) * vectors.shape[0],
+        out_shape=tuple(struct(a.shape, f32) for a in sums)
+        + tuple(struct(a.shape, a.dtype) for a in whole)
+        + (struct((width,), f32),) * vectors.shape[0],
         in_specs=blocks + [pl.BlockSpec(vectors.shape, lambda i: (0, 0))],
         out_specs=tuple(blocks) + (pl.BlockSpec((width,), lambda i: (0,)),) * vectors.shape[0],
         compiler_params=pltpu.CompilerParams(vmem_limit_bytes=62 << 20),
         name="widen",
-    )(*sums, vectors)
+    )(*sums, *whole, vectors)
 
 
 def local(
@@ -1443,12 +1445,14 @@
         values,
         all_t,
     )
-    wide = widen((sum_q, sum_k, sum_v, sum_o, sum_u, sum_d), small_sums)
-    lines = wide[6:]
+    wide = widen(
+        (sum_q, sum_k, sum_v, sum_o, sum_u, sum_d), (result, grad_rays, grad_latents), small_sums
+    )
+    lines = wide[9:]
     return (
-        result,
-        grad_rays,
-        grad_latents,
+        wide[6],
+        wide[7],
+        wide[8],
         lines[4],
         lines[5],
         wide[0],

time: 267 us -> 264 us (0.989)
  local copies, waits for them, and re-layouts: 2.85 us -> 0 us
    unnamed x9 -> x0, local copies, waits for them, and re-layouts: 2.85 us -> none
where the time goes in v8:
time: 264 us
  Pallas kernels  262 us (99%)
    pallas_call x1, Pallas kernels, back_and_sum(): pl.pallas_call(functools.partial(sum_kernel, n_seq, n_ray, units), out_sh...  165 us
    pallas_call x1, Pallas kernels, gather_and_attend(): pl.pallas_call(functools.partial(gather_kernel, n_seq, n_ray), out_shape=...  84.9 us
    pallas_call x1, Pallas kernels, widen(): pl.pallas_call(widen_kernel, grid=(steps,), out_shape=tuple((struct(a.sha...  12.6 us

profile of v8, /device:TPU:0, one launch (start us, length us, event | category | flops | bytes accessed | tf_op | source)
XLA Modules:
  0.0 264.1 jit_solution(6879305554381267502)
XLA Ops:
  0.7 84.9 %gather_and_attend.1 = (bf16[768,3072]{1,0:T(8,128)(2,1)}, bf16[3072,768]{1,0:T(8,128)(2,1)}, bf16[768,3072]{1,0:T(8,128)(2,1)}, bf16[3072,768]{1,0:T(8,128)(2,1...) custom-call(s32[1,3]{1,0:T(1,128)} %lengths.3, ...), custom_call_target="tpu_custom_call" | custom-call | tf_op jit(solution)/shard_map/gather_and_attend/pallas_call | solution.py:1282
  85.6 164.6 %back_and_sum.1 = (bf16[768,768]{1,0:T(8,128)(2,1)}, bf16[768,768]{1,0:T(8,128)(2,1)}, bf16[768,768]{1,0:T(8,128)(2,1)}, bf16[768,768]{1,0:T(8,128)(2,1)}, bf16[...) custom-call(s32[1,3]{1,0:T(1,128)} %lengths.3, ...), custom_call_target="tpu_custom_call" | custom-call | tf_op jit(solution)/shard_map/back_and_sum/pallas_call | solution.py:859
  250.2 12.6 %widen.1 = (f32[768,768]{1,0:T(8,128)}, f32[768,768]{1,0:T(8,128)}, f32[768,768]{1,0:T(8,128)}, f32[768,768]{1,0:T(8,128)}, f32[768,1536]{1,0:T(8,128)}, /*index...) custom-call(bf16[768,768]{1,0:T(8,128)(2,1)} %get-tuple-element.73.r, ...), custom_call_target="tpu_custom_call" | custom-call | tf_op jit(solution)/shard_map/widen/pallas_call | solution.py:1354
  262.8 1.3 pad_maximum_fusion
